TPU v7x, 32 devices: a whole 2x2x4 slice. The times are simulated.
32 devices in a mesh: seq: 4 (over y, core), batch: 8 (over z, x).
Axes of the slice: x: 2, y: 2, z: 4, core: 2. Of those that a mesh axis runs over, the one named last changes fastest.
Arguments:
- hidden: bfloat16 [8, 1536, 1024], P('batch', 'seq'), may hold values from -6 to 6
- grad_out: bfloat16 [8, 1536, 1024], P('batch', 'seq'), may hold values from -6 to 6
- block_offsets: int32 [8, 16, 12, 4], P('batch', 'seq'), may hold values from 0 to 11, as said below
- w_query: bfloat16 [1024, 1024], replicated, may hold values from -0.1875 to 0.1875
- w_key: bfloat16 [1024, 1024], replicated, may hold values from -0.1875 to 0.1875
- w_value: bfloat16 [1024, 1024], replicated, may hold values from -0.1875 to 0.1875
- w_out: bfloat16 [1024, 1024], replicated, may hold values from -0.1875 to 0.1875
Outputs:
- grad_hidden: bfloat16 [8, 1536, 1024], P('batch', 'seq')
- grad_weights: float32 [4, 1024, 1024], P(None, 'batch', 'seq')
Inputs may be any that keep to these rules, and one draw needn't show every extreme that they name: `block_offsets`: slot 0 of every list is 0 (the query's own block); the other slots of a list hold distinct values from 1 to 11, and a value greater than the query block's index leaves its slot empty.
All inputs are finite; a program needn't handle non-finite values.
Results may differ from a plain program's by a relative error of at most 0.012.
Values may be sent and summed in bfloat16 or wider, within the bound.
No kernel may reach another device: no remote copies, remote signals or barrier semaphores. Data moves between devices by JAX's collectives and lax.ppermute only.
A program may use at most 128 MiB of HBM per device.

v0:
```python
import math

import jax
import jax.numpy as jnp
from jax import lax
from jax.sharding import PartitionSpec as P

BLK = 128


def pick_blocks(source, chosen):
    return source[chosen]


def add_blocks(running, chosen, portion):
    return running.at[chosen].add(portion)


def scatter_blocks(running, block_ids, portion):
    heads_n = portion.shape[0]
    flat_ids = block_ids.reshape(heads_n, -1)
    flat_part = portion.reshape((heads_n, -1) + portion.shape[3:])
    return jax.vmap(add_blocks)(running, flat_ids, flat_part)


def times_transposed(matrix, weight):
    return lax.dot_general(
        matrix, weight, (((1,), (1,)), ((), ())), preferred_element_type=jnp.float32
    )


def inner_rows(left_side, right_side):
    return lax.dot_general(
        left_side, right_side, (((0,), (0,)), ((), ())), preferred_element_type=jnp.float32
    )


def attend_group(queries, key_all, value_all, out_grads, offsets, first_block):
    group_len = queries.shape[1]
    block_len = queries.shape[2]
    score_scale = 1.0 / math.sqrt(queries.shape[3])
    query_block = first_block + jnp.arange(group_len, dtype=jnp.int32)
    usable = offsets <= query_block[None, :, None]
    block_ids = jnp.where(usable, query_block[None, :, None] - offsets, 0)
    picked_keys = jax.vmap(pick_blocks)(key_all, block_ids)
    picked_values = jax.vmap(pick_blocks)(value_all, block_ids)
    scores = (
        jnp.einsum("hgqd,hgnkd->hgqnk", queries, picked_keys, preferred_element_type=jnp.float32)
        * score_scale
    )
    within = jnp.arange(block_len, dtype=jnp.int32)
    query_pos = query_block[:, None] * block_len + within[None, :]
    key_pos = block_ids[..., None] * block_len + within
    allowed = usable[:, :, None, :, None] & (
        key_pos[:, :, None, :, :] <= query_pos[None, :, :, None, None]
    )
    row_top = jnp.max(jnp.where(allowed, scores, -jnp.inf), axis=(3, 4), keepdims=True)
    raised = jnp.where(allowed, jnp.exp(scores - row_top), 0.0)
    denom_sum = jnp.sum(raised, axis=(3, 4), keepdims=True)
    probabilities = raised / denom_sum
    probs_half = probabilities.astype(jnp.bfloat16)
    attended = jnp.einsum(
        "hgqnk,hgnkd->hgqd", probs_half, picked_values, preferred_element_type=jnp.float32
    ).astype(jnp.bfloat16)
    delta_rows = jnp.sum(out_grads.astype(jnp.float32) * attended.astype(jnp.float32), axis=-1)
    prob_grad = jnp.einsum(
        "hgqd,hgnkd->hgqnk", out_grads, picked_values, preferred_element_type=jnp.float32
    )
    score_grad = (probabilities * (prob_grad - delta_rows[:, :, :, None, None])).astype(
        jnp.bfloat16
    )
    query_grad = (
        jnp.einsum("hgqnk,hgnkd->hgqd", score_grad, picked_keys, preferred_element_type=jnp.float32)
        * score_scale
    ).astype(jnp.bfloat16)
    key_part = (
        jnp.einsum("hgqnk,hgqd->hgnkd", score_grad, queries, preferred_element_type=jnp.float32)
        * score_scale
    )
    value_part = jnp.einsum(
        "hgqnk,hgqd->hgnkd", probs_half, out_grads, preferred_element_type=jnp.float32
    )
    return (attended, query_grad, key_part, value_part, block_ids)


def sharded_terms(factor_pairs, row_block, width):
    pair_count = len(factor_pairs)
    pieces = [inner_rows(left_side, right_side) for left_side, right_side in factor_pairs]
    summed_rows = lax.psum_scatter(pieces[0], "batch", scatter_dimension=0, tiled=True)
    summed_rows = summed_rows.reshape(row_block, pair_count, width)
    col_block = lax.psum_scatter(summed_rows, "seq", scatter_dimension=2, tiled=True)
    return col_block.transpose(1, 0, 2)


def per_device(hidden, grad_out, block_offsets, w_query, w_key, w_value, w_out):
    tokens = hidden[0]
    grad_rows = grad_out[0]
    row_count = tokens.shape[0]
    width = tokens.shape[1]
    seq_count = lax.axis_size("seq")
    batch_count = lax.axis_size("batch")
    queries = jnp.dot(tokens, w_query, preferred_element_type=jnp.float32).astype(jnp.bfloat16)
    key_rows = jnp.dot(tokens, w_key, preferred_element_type=jnp.float32).astype(jnp.bfloat16)
    value_rows = jnp.dot(tokens, w_value, preferred_element_type=jnp.float32).astype(jnp.bfloat16)
    attn_grad = times_transposed(grad_rows, w_out).astype(jnp.bfloat16)
    stacked = jnp.stack([queries, key_rows, value_rows, attn_grad])
    by_heads = lax.all_to_all(stacked, "seq", split_axis=2, concat_axis=1, tiled=True)
    seq_len = by_heads.shape[1]
    head_width = by_heads.shape[2]
    offsets = block_offsets[0]
    head_count = offsets.shape[0]
    head_size = head_width // head_count
    block_total = seq_len // BLK
    arranged = by_heads.reshape(4, block_total, BLK, head_count, head_size).transpose(0, 3, 1, 2, 4)
    group_len = min(block_total, max(1, 512 // BLK))
    group_count = block_total // group_len

    def grouped(source):
        shaped = source.reshape((source.shape[0], group_count, group_len) + source.shape[2:])
        return jnp.moveaxis(shaped, 1, 0)

    def ungrouped(source):
        moved = jnp.moveaxis(source, 0, 1)
        return moved.reshape((moved.shape[0], block_total) + moved.shape[3:])

    key_all = arranged[1]
    value_all = arranged[2]

    def group_step(running, inputs):
        key_acc, value_acc = running
        query_group, grad_group, offset_group, first_block = inputs
        attended, query_grad, key_part, value_part, block_ids = attend_group(
            query_group, key_all, value_all, grad_group, offset_group, first_block
        )
        key_acc = scatter_blocks(key_acc, block_ids, key_part)
        value_acc = scatter_blocks(value_acc, block_ids, value_part)
        return ((key_acc, value_acc), (attended, query_grad))

    empty = jnp.zeros((head_count, block_total, BLK, head_size), jnp.float32)
    starts = jnp.arange(group_count, dtype=jnp.int32) * group_len
    (key_acc, value_acc), (attended_g, query_g) = lax.scan(
        group_step,
        (empty, empty),
        (grouped(arranged[0]), grouped(arranged[3]), grouped(offsets), starts),
    )
    head_grads = jnp.stack(
        [
            ungrouped(query_g),
            key_acc.astype(jnp.bfloat16),
            value_acc.astype(jnp.bfloat16),
            ungrouped(attended_g),
        ]
    )
    head_grads = head_grads.transpose(0, 2, 3, 1, 4).reshape(4, seq_len, head_width)
    by_tokens = lax.all_to_all(head_grads, "seq", split_axis=1, concat_axis=2, tiled=True)
    query_tok = by_tokens[0]
    key_tok = by_tokens[1]
    value_tok = by_tokens[2]
    attended_tok = by_tokens[3]
    grad_hidden = (
        times_transposed(query_tok, w_query)
        + times_transposed(key_tok, w_key)
        + times_transposed(value_tok, w_value)
    ).astype(jnp.bfloat16)
    row_block = width // batch_count
    head_factors = head_grads[:3].transpose(1, 0, 2).reshape(seq_len, 3 * head_width)
    col_sums = inner_rows(lax.all_gather(tokens, "seq", axis=0, tiled=True), head_factors)
    head_part = lax.psum_scatter(
        col_sums.astype(jnp.bfloat16), "batch", scatter_dimension=0, tiled=True
    ).astype(jnp.float32)
    head_part = head_part.reshape(row_block, 3, head_width).transpose(1, 0, 2)
    out_part = sharded_terms([(attended_tok, grad_rows)], row_block, width)
    grad_weights = jnp.concatenate([head_part, out_part], axis=0)
    norm_factor = 1.0 / math.sqrt(row_count * seq_count * batch_count)
    return (grad_hidden[None], grad_weights * norm_factor)


def solution(mesh):
    placed = (
        P("batch", "seq", None),
        P("batch", "seq", None),
        P("batch", "seq", None, None),
        P(),
        P(),
        P(),
        P(),
    )
    return jax.shard_map(
        per_device,
        mesh=mesh,
        in_specs=placed,
        out_specs=(P("batch", "seq", None), P(None, "batch", "seq")),
        check_vma=False,
    )
```

profile of v0, /device:TPU:4, one launch (start us, length us, event | category | flops | bytes accessed | tf_op | source)
XLA Modules:
  0.0 553.6 jit_solution(12146060330108894232)
XLA Ops:
  18.1 6.0 %copy.98 = bf16[4,384,1024]{1,0,2:T(4,128)(2,1)} copy(bf16[4,384,1024]{2,1,0:T(8,128)(2,1)} %pad_maximum_fusion) | data formatting | bytes 6291456 | tf_op jit(solution)/shard_map/stack | solution.py:106
  24.1 4.8 all-to-all-start
  29.8 50.3 %all-to-all-done = bf16[4,384,1024]{1,0,2:T(4,128)(2,1)} async-done(((bf16[4,384,1024]{1,0,2:T(4,128)(2,1)}), bf16[4,384,1024]{1,0,2:T(4,128)(2,1)}, u32[]{:S(2)}, u32[]{:S(2)}) %all-to-all-start) | async-done | bytes 3145760 | tf_op jit(solution)/shard_map/all_to_all | solution.py:107
  80.1 6.0 %copy.143 = bf16[4,384,4,256]{1,2,3,0:T(4,128)(2,1)} copy(bf16[4,384,4,256]{1,0,3,2:T(4,128)(2,1)} %bitcast.27) | data formatting | bytes 6291456 | tf_op jit(solution)/shard_map/all_to_all | solution.py:107
  86.1 7.0 %reshape.209 = bf16[4,12,128,4,64]{2,1,4,3,0:T(8,128)(2,1)} reshape(bf16[4,4,384,256]{2,1,3,0:T(4,128)(2,1)} %bitcast.229) | data formatting | bytes 6291456 | tf_op jit(solution)/shard_map/reshape | solution.py:114
  108.3 179.9 %while.16 = (s32[]{:T(128)}, f32[4,12,128,64]{2,3,1,0:T(8,128)}, f32[4,12,128,64]{2,3,1,0:T(8,128)}, bf16[3,4,4,128,64]{3,4,2,0,1:T(8,128)(2,1)}, bf16[3,4,4,128...) while((s32[]{:T(128)}, f32[4,12,128,64]{2,3,1,0:T(8,128)}, ...), condition=%wide.region_6.7_spmd, body=%wide.region_0.6_spmd.sunk | while | flops 843452864 | bytes 102284720 | solution.py:141
  113.8 5.3 select_reduce_fusion.2
  125.7 12.3 %scatter_fusion.1 = f32[4,12,128,64]{2,3,1,0:T(8,128)} fusion(f32[4,12,128,64]{2,3,1,0:T(8,128)} %get-tuple-element.241, s32[64]{0:T(128)S(1)} %reshape.267, f32[64,128,64]{1,2,0:T(8,128)} %bitcast.223), kind=kCustom, calls=%fused_computation.3.clone.1 | custom fusion | flops 524288 | bytes 6291968 | tf_op jit(solution)/shard_map/while/body/eval_jaxpr/vmap()/scatter-add | solution.py:16
  153.3 12.1 %scatter_fusion = f32[4,12,128,64]{2,3,1,0:T(8,128)} fusion(f32[4,12,128,64]{2,3,1,0:T(8,128)} %get-tuple-element.240, s32[64]{0:T(128)S(1)} %reshape.267, f32[64,128,64]{1,2,0:T(8,128)} %bitcast.222), kind=kCustom, calls=%fused_computation.2.clone.1 | custom fusion | flops 524288 | bytes 6291968 | tf_op jit(solution)/shard_map/while/body/eval_jaxpr/vmap()/scatter-add | solution.py:16
  175.4 5.3 select_reduce_fusion.2
  182.4 4.6 fusion.105
  187.3 11.1 %scatter_fusion.1 = f32[4,12,128,64]{2,3,1,0:T(8,128)} fusion(f32[4,12,128,64]{2,3,1,0:T(8,128)} %get-tuple-element.241, s32[64]{0:T(128)S(1)} %reshape.267, f32[64,128,64]{1,2,0:T(8,128)} %bitcast.223), kind=kCustom, calls=%fused_computation.3.clone.1 | custom fusion | flops 524288 | bytes 6291968 | tf_op jit(solution)/shard_map/while/body/eval_jaxpr/vmap()/scatter-add | solution.py:16
  213.6 11.0 %scatter_fusion = f32[4,12,128,64]{2,3,1,0:T(8,128)} fusion(f32[4,12,128,64]{2,3,1,0:T(8,128)} %get-tuple-element.240, s32[64]{0:T(128)S(1)} %reshape.267, f32[64,128,64]{1,2,0:T(8,128)} %bitcast.222), kind=kCustom, calls=%fused_computation.2.clone.1 | custom fusion | flops 524288 | bytes 6291968 | tf_op jit(solution)/shard_map/while/body/eval_jaxpr/vmap()/scatter-add | solution.py:16
  234.6 5.3 select_reduce_fusion.2
  246.5 10.9 %scatter_fusion.1 = f32[4,12,128,64]{2,3,1,0:T(8,128)} fusion(f32[4,12,128,64]{2,3,1,0:T(8,128)} %get-tuple-element.241, s32[64]{0:T(128)S(1)} %reshape.267, f32[64,128,64]{1,2,0:T(8,128)} %bitcast.223), kind=kCustom, calls=%fused_computation.3.clone.1 | custom fusion | flops 524288 | bytes 6291968 | tf_op jit(solution)/shard_map/while/body/eval_jaxpr/vmap()/scatter-add | solution.py:16
  272.7 11.0 %scatter_fusion = f32[4,12,128,64]{2,3,1,0:T(8,128)} fusion(f32[4,12,128,64]{2,3,1,0:T(8,128)} %get-tuple-element.240, s32[64]{0:T(128)S(1)} %reshape.267, f32[64,128,64]{1,2,0:T(8,128)} %bitcast.222), kind=kCustom, calls=%fused_computation.2.clone.1 | custom fusion | flops 524288 | bytes 6291968 | tf_op jit(solution)/shard_map/while/body/eval_jaxpr/vmap()/scatter-add | solution.py:16
  293.4 10.6 %copy.131 = bf16[4,12,128,4,64]{4,3,0,2,1:T(4,128)(2,1)} copy(bf16[4,12,128,4,64]{2,4,1,3,0:T(8,128)(2,1)} %maximum_bitcast_fusion) | data formatting | bytes 6291456 | tf_op jit(solution)/shard_map/reshape | solution.py:154
  303.9 10.7 %reshape.246 = bf16[4,1536,256]{2,0,1:T(4,128)(2,1)} reshape(bf16[4,12,128,4,64]{4,3,0,2,1:T(4,128)(2,1)} %copy.131) | data formatting | bytes 6291456 | tf_op jit(solution)/shard_map/reshape | solution.py:154
  314.6 41.0 %all_to_all.30 = bf16[4,1536,256]{2,0,1:T(4,128)(2,1)S(1)} all-to-all(bf16[4,1536,256]{2,0,1:T(4,128)(2,1)} %reshape.246), channel_id=1, replica_groups=mesh['seq'=4,'batch'=8] {'seq'}, dimensions={1} | all-to-all | bytes 6291456 | tf_op jit(solution)/shard_map/all_to_all | solution.py:155
  368.8 5.5 slice.42
  374.3 6.3 %fusion.40 = bf16[1024,768]{0,1:T(8,128)(2,1)} fusion(bf16[1536,768]{0,1:T(8,128)(2,1)} %bitcast.234, bf16[1,1536,1024]{2,1,0:T(8,128)(2,1)} %all-gather.3.cloned.1.call-done), kind=kOutput, calls=%fused_computation.68 | convolution fusion | flops 2416705536 | bytes 7077888 | tf_op jit(solution)/shard_map/dot_general | solution.py:33
  389.3 64.8 %reduce-scatter.6.cloned.1.call-done = f32[128,1024]{1,0:T(8,128)} async-done(((f32[1024,1024]{1,0:T(8,128)}), f32[128,1024]{1,0:T(8,128)}) %reduce-scatter.6.cloned.1.call-update) | async-done | bytes 524304 | tf_op jit(solution)/shard_map/reduce_scatter | solution.py:89
  460.3 62.3 %reduce-scatter.10.cloned.1.call-done = bf16[128,768]{1,0:T(8,128)(2,1)} async-done(((bf16[1024,768]{1,0:T(8,128)(2,1)}), bf16[128,768]{1,0:T(8,128)(2,1)}) %reduce-scatter.10.cloned.1.call-update) | async-done | bytes 196624
  523.9 20.4 %reduce-scatter.8.cloned.1.call-done = f32[128,1,256]{2,0,1:T(8,128)} async-done(((f32[128,1,1024]{2,0,1:T(8,128)}), f32[128,1,256]{2,0,1:T(8,128)}) %reduce-scatter.8.cloned.1.call-update) | async-done | bytes 131088 | tf_op jit(solution)/shard_map/reduce_scatter | solution.py:91
  (165 shorter events, 152.8 us)
Async XLA Ops:
  8.0 3.7 copy-start.10
  8.0 3.7 copy-start.15
  13.3 1.8 copy-start.14
  24.1 5.6 %copy-start.13 = (s32[1,4,12,4]{2,3,1,0:T(4,128)S(1)}, s32[1,4,12,4]{2,3,1,0:T(4,128)}, u32[]{:S(2)}) copy-start(s32[1,4,12,4]{2,3,1,0:T(4,128)} %param.11) | copy-start | bytes 2308
  24.1 56.0 %all-to-all-start = ((bf16[4,384,1024]{1,0,2:T(4,128)(2,1)}), bf16[4,384,1024]{1,0,2:T(4,128)(2,1)}, u32[]{:S(2)}, u32[]{:S(2)}) async-start(bf16[4,384,1024]{1,0,2:T(4,128)(2,1)} %copy.98), calls=%async_computation | async-start | bytes 6291456 | tf_op jit(solution)/shard_map/all_to_all | solution.py:107
  28.9 345.4 %all-gather.3.cloned.1.call-start = ((), (), s32[]{:S(2)}) async-start(), calls=%async_computation.7 | async-start | bytes 3932160 | tf_op jit(solution)/shard_map/all_gather | solution.py:167
  29.6 424.6 %reduce-scatter.6.cloned.1.call-start = ((), (), s32[]{:S(2)}) async-start(), calls=%async_computation.5 | async-start | bytes 4718592 | tf_op jit(solution)/shard_map/reduce_scatter | solution.py:89
  119.1 6.3 %copy-start.2 = (f32[4,4,128,4,128]{2,4,3,1,0:T(8,128)}, f32[4,4,128,4,128]{2,4,3,1,0:T(8,128)S(1)}, u32[]{:S(2)}) copy-start(f32[4,4,128,4,128]{2,4,3,1,0:T(8,128)S(1)} %get-tuple-element.223) | copy-start | bytes 12582916 | tf_op jit(solution)/shard_map/while
  141.6 4.5 copy-start.3
  141.6 4.8 copy-start.4
  180.7 6.3 %copy-start.2 = (f32[4,4,128,4,128]{2,4,3,1,0:T(8,128)}, f32[4,4,128,4,128]{2,4,3,1,0:T(8,128)S(1)}, u32[]{:S(2)}) copy-start(f32[4,4,128,4,128]{2,4,3,1,0:T(8,128)S(1)} %get-tuple-element.223) | copy-start | bytes 12582916 | tf_op jit(solution)/shard_map/while
  201.9 4.5 copy-start.3
  201.9 4.8 copy-start.4
  239.9 6.3 %copy-start.2 = (f32[4,4,128,4,128]{2,4,3,1,0:T(8,128)}, f32[4,4,128,4,128]{2,4,3,1,0:T(8,128)S(1)}, u32[]{:S(2)}) copy-start(f32[4,4,128,4,128]{2,4,3,1,0:T(8,128)S(1)} %get-tuple-element.223) | copy-start | bytes 12582916 | tf_op jit(solution)/shard_map/while
  261.0 4.5 copy-start.3
  261.0 4.8 copy-start.4
  288.2 2.3 copy-start.9
  363.6 159.1 %reduce-scatter.10.cloned.1.call-start = ((), (), s32[]{:S(2)}) async-start(), calls=%async_computation.8 | async-start | bytes 1769472
  363.6 1.7 slice-start
  383.2 5.0 copy-start.5
  383.3 161.0 %reduce-scatter.8.cloned.1.call-start = ((), (), s32[]{:S(2)}) async-start(), calls=%async_computation.6 | async-start | bytes 655360 | tf_op jit(solution)/shard_map/reduce_scatter | solution.py:91
  454.2 2.3 copy-start.11
  454.2 2.3 copy-start.16
  456.6 1.8 copy-start.8
  (7 other events, 9.5 us)
Sparse Core Ops, SparseCore 0:
  31.3 46.0 all-gather.2
Sparse Core Ops, SparseCore 1:
  363.7 90.5 reduce-scatter.5
  457.8 64.8 reduce-scatter.9
  525.0 19.2 reduce-scatter.7
where the time goes:
time: 559 us; the launch traced here: 554 us
  waiting for transfers between devices  199 us (36%)
  local copies, waits for them, and re-layouts  115 us (21%)
  matrix products  92 us (16%)
  other arithmetic  85.2 us (15%)
  blocking collectives  41 us (7%)
  between operations  15.9 us (3%)
    scatter-add x9, other arithmetic, add_blocks(): return running.at[chosen].add(portion)  68.5 us
    reduce_scatter x1, waiting for transfers between devices, sharded_terms(): lax.psum_scatter(pieces[0], 'batch', scatter_dimension=0, tiled=True)  64.8 us
    unnamed x5, waiting for transfers between devices  63.1 us
    all_to_all x1, waiting for transfers between devices, per_device(): lax.all_to_all(stacked, 'seq', split_axis=2, concat_axis=1, tiled=True)  50.3 us
    all_to_all x1, blocking collectives, per_device(): lax.all_to_all(head_grads, 'seq', split_axis=1, concat_axis=2, tiled=True)  41 us
    gather x9, local copies, waits for them, and re-layouts, pick_blocks(): return source[chosen]  21.7 us
    reshape x2, local copies, waits for them, and re-layouts, per_device(): head_grads.transpose(0, 2, 3, 1, 4).reshape(4, seq_len, head_width)  21.2 us
    reduce_scatter x1, waiting for transfers between devices, sharded_terms(): lax.psum_scatter(summed_rows, 'seq', scatter_dimension=2, tiled=True)  20.4 us
  transfers between devices with their start and end apart: 5, of which 4 were waited for; matrix products, arithmetic and copies ran while one was open for 48% of the time, Pallas kernels for 0%

commit v1 on v0

v1 whole, which is shorter than its diff:
```python
import functools
import math

import jax
import jax.numpy as jnp
from jax import lax
from jax.experimental import pallas as pl
from jax.experimental.pallas import tpu as pltpu
from jax.sharding import PartitionSpec as P

BLK = 128
BF = jnp.bfloat16
F32 = jnp.float32
LAST_LAST = (((1,), (1,)), ((), ()))
FIRST_LAST = (((0,), (1,)), ((), ()))
FIRST_FIRST = (((0,), (0,)), ((), ()))


def dot(left_side, right_side, dims):
    return lax.dot_general(left_side, right_side, dims, preferred_element_type=F32)


def swap(value, axis, distance):
    count = lax.axis_size(axis)
    return lax.ppermute(value, axis, [(at, at ^ distance) for at in range(count)])


def gather_pieces(shard, axis):
    pieces = {0: shard}
    bit = lax.axis_size(axis) // 2
    while bit:
        for place in sorted(pieces):
            pieces[place | bit] = swap(pieces[place], axis, bit)
        bit //= 2
    return [pieces[place] for place in sorted(pieces)]


def attention_kernel(
    place_of,
    offsets,
    queries_t,
    out_grads_t,
    keys_t,
    values_t,
    keys,
    values,
    attended_t,
    query_grad_t,
    key_grad_t,
    value_grad_t,
    key_acc,
    value_acc,
    *,
    blocks,
    slots,
    head_size,
):
    pair = pl.program_id(0)
    key_acc[...] = jnp.zeros_like(key_acc)
    value_acc[...] = jnp.zeros_like(value_acc)
    key_at = lax.broadcasted_iota(jnp.int32, (BLK, BLK), 0)
    query_at = lax.broadcasted_iota(jnp.int32, (BLK, BLK), 1)
    causal = key_at <= query_at
    first_head = lax.broadcasted_iota(jnp.int32, (2 * head_size, BLK), 0) < head_size
    plus = functools.partial(functools.reduce, jnp.add)

    def one_block(place, carry):
        block = place_of[place]
        cols = pl.ds(pl.multiple_of(place * BLK, BLK), BLK)
        pair_queries = queries_t[:, cols]
        pair_grads = out_grads_t[:, cols]
        scored = []
        for half in range(2):
            head = 2 * pair + half
            rows = slice(half * head_size, (half + 1) * head_size)
            keep = first_head if half == 0 else ~first_head
            head_queries = jnp.where(keep, pair_queries, jnp.zeros_like(pair_queries))
            head_grads = jnp.where(keep, pair_grads, jnp.zeros_like(pair_grads))
            named, usable = [], []
            for slot in range(slots):
                offset = offsets[(head * blocks + block) * slots + slot]
                usable.append(offset <= block)
                named.append(place_of[jnp.where(offset <= block, block - offset, 0)])
            spans = [pl.ds(pl.multiple_of(at * BLK, BLK), BLK) for at in named]
            scores = [
                jnp.dot(keys[span, :], head_queries, preferred_element_type=F32) for span in spans
            ]
            prob_grad = [
                jnp.dot(values[span, :], head_grads, preferred_element_type=F32) for span in spans
            ]
            scores = [
                jnp.where(causal if slot == 0 else usable[slot], scores[slot], -jnp.inf)
                for slot in range(slots)
            ]
            scored.append((rows, named, spans, scores, prob_grad))
        parts = []
        for rows, named, spans, scores, prob_grad in scored:
            top = jnp.max(functools.reduce(jnp.maximum, scores), axis=0, keepdims=True)
            raised = [jnp.exp(part - top) for part in scores]
            total = jnp.sum(plus(raised), axis=0, keepdims=True)
            inverse = 1.0 / total
            probs = [part * inverse for part in raised]
            probs_half = [part.astype(BF) for part in probs]
            attended = plus(
                [
                    jnp.dot(values_t[rows, span], part, preferred_element_type=F32)
                    for span, part in zip(spans, probs_half)
                ]
            ).astype(BF)
            attended_t[rows, cols] = attended
            grads = out_grads_t[rows, cols]
            delta = jnp.sum(grads.astype(F32) * attended.astype(F32), axis=0, keepdims=True)
            score_grad = [
                (part * (grad - delta)).astype(BF) for part, grad in zip(probs, prob_grad)
            ]
            query_grad = plus(
                [
                    jnp.dot(keys_t[rows, span], part, preferred_element_type=F32)
                    for span, part in zip(spans, score_grad)
                ]
            )
            query_grad_t[rows, cols] = (query_grad * (1.0 / math.sqrt(head_size))).astype(BF)
            queries = queries_t[rows, cols]
            value_parts = [dot(grads, part, LAST_LAST) for part in probs_half]
            key_parts = [dot(queries, part, LAST_LAST) for part in score_grad]
            parts.append((rows, named, key_parts, value_parts))
        for rows, named, key_parts, value_parts in parts:
            for at, key_part, value_part in zip(named, key_parts, value_parts):
                key_acc[at, rows, :] += key_part
                value_acc[at, rows, :] += value_part
        return carry

    lax.fori_loop(0, blocks, one_block, 0)
    for at in range(blocks):
        span = slice(at * BLK, (at + 1) * BLK)
        key_grad_t[:, span] = key_acc[at].astype(BF)
        value_grad_t[:, span] = value_acc[at].astype(BF)


def attention(place_of, offsets, queries_t, out_grads_t, keys_t, values_t, keys, values):
    width, tokens = queries_t.shape
    heads, blocks, slots = offsets.shape
    head_size = width // heads
    pair_rows = pl.BlockSpec((2 * head_size, tokens), lambda pair, *_: (pair, 0))
    pair_cols = pl.BlockSpec((tokens, 2 * head_size), lambda pair, *_: (0, pair))
    result = jax.ShapeDtypeStruct((width, tokens), BF)
    pair_flops = 2 * 6 * BLK * BLK * head_size
    return pl.pallas_call(
        functools.partial(attention_kernel, blocks=blocks, slots=slots, head_size=head_size),
        grid_spec=pltpu.PrefetchScalarGridSpec(
            num_scalar_prefetch=2,
            grid=(heads // 2,),
            in_specs=[pair_rows] * 4 + [pair_cols] * 2,
            out_specs=[pair_rows] * 4,
            scratch_shapes=[pltpu.VMEM((blocks, 2 * head_size, BLK), F32)] * 2,
        ),
        out_shape=[result] * 4,
        compiler_params=pltpu.CompilerParams(vmem_limit_bytes=40 * 1024 * 1024),
        cost_estimate=pl.CostEstimate(
            flops=heads * blocks * slots * pair_flops,
            bytes_accessed=10 * width * tokens * 2,
            transcendentals=heads * blocks * slots * BLK * BLK,
        ),
        name="attention",
    )(place_of, offsets.reshape(-1), queries_t, out_grads_t, keys_t, values_t, keys, values)


def sum_over_batch(terms):
    count = lax.axis_size("batch")
    me = lax.axis_index("batch")
    rows, width = terms.shape
    block = width // count
    pieces = {
        place: lax.dynamic_slice(terms, (0, (me ^ place) * block), (rows, block))
        for place in range(count)
    }
    low = 1
    while low < count:
        span = 2 if low == 1 or low * 4 > count else 4
        kept = [place for place in pieces if (place // low) % span == 0]
        summed = {place: pieces[place] for place in kept}
        for step in range(1, span):
            sent = jnp.concatenate([pieces[place + step * low] for place in kept], axis=1)
            came = swap(sent.astype(BF), "batch", step * low)
            for at, place in enumerate(kept):
                summed[place] = summed[place] + came[:, at * block : (at + 1) * block].astype(F32)
        pieces = summed
        low *= span
    return pieces[0]


def rows_to_owner(block_sum):
    seq_count, batch_count = lax.axis_size("seq"), lax.axis_size("batch")
    batch_at = lax.axis_index("batch")
    ratio = batch_count // seq_count
    height, width = block_sum.shape[0] // ratio, block_sum.shape[1]
    placed = jnp.zeros((height, ratio * width), F32)
    for turn in range(ratio):
        moves = []
        for b in range(batch_count):
            for s in range(seq_count):
                target = (b // ratio) * batch_count + ratio * s + (b + turn) % ratio
                moves.append((s * batch_count + b, target))
        piece = lax.dynamic_slice(
            block_sum, (((batch_at + turn) % ratio) * height, 0), (height, width)
        )
        came = lax.ppermute(piece, ("seq", "batch"), moves)
        placed = lax.dynamic_update_slice(
            placed, came, (0, ((batch_at - turn) % ratio) * width)
        )
    return placed


def per_device(hidden, grad_out, block_offsets, w_query, w_key, w_value, w_out):
    tokens = hidden[0]
    grad_rows = grad_out[0]
    offsets = block_offsets[0]
    row_count, width = tokens.shape
    seq_count = lax.axis_size("seq")
    batch_count = lax.axis_size("batch")
    seq_at = lax.axis_index("seq")
    head_width = width // seq_count
    head_size = head_width // offsets.shape[0]

    def head_rows(weight, seq_index):
        return lax.dynamic_slice(weight, (0, seq_index * head_width), (width, head_width)).T

    def three_rows(seq_index):
        return jnp.concatenate(
            [head_rows(weight, seq_index) for weight in (w_query, w_key, w_value)], axis=0
        )

    own_rows = three_rows(seq_at)
    chip_rows = jnp.concatenate([own_rows, three_rows(seq_at ^ 1)], axis=0)
    out_rows = lax.dynamic_slice(w_out, (seq_at * head_width, 0), (head_width, width))

    hidden_all = jnp.concatenate(gather_pieces(tokens, "seq"), axis=0)
    grad_all = jnp.concatenate(gather_pieces(grad_rows, "seq"), axis=0)
    heads_t = dot(own_rows, hidden_all, LAST_LAST).astype(BF)
    out_grads_t = dot(out_rows, grad_all, LAST_LAST).astype(BF)
    queries_t = heads_t[:head_width] * jnp.asarray(1.0 / math.sqrt(head_size), BF)
    keys_t = heads_t[head_width : 2 * head_width]
    values_t = heads_t[2 * head_width :]
    keys, values = keys_t.T, values_t.T

    shard_blocks = row_count // BLK
    block_at = jnp.arange(shard_blocks * seq_count, dtype=jnp.int32)
    place_of = ((block_at // shard_blocks) ^ seq_at) * shard_blocks + block_at % shard_blocks
    attended_t, query_grad_t, key_grad_t, value_grad_t = attention(
        place_of, offsets, queries_t, out_grads_t, keys_t, values_t, keys, values
    )
    grads_t = jnp.concatenate([query_grad_t, key_grad_t, value_grad_t], axis=0)

    by_place = grads_t.reshape(3 * head_width, seq_count // 2, 2, row_count)
    came = swap(by_place[:, :, 1], "seq", 1)
    chip_grads = jnp.concatenate([by_place[:, :, 0], came], axis=0)
    partial = [
        dot(chip_grads[:, at], chip_rows, FIRST_FIRST) for at in range(seq_count // 2)
    ]
    token_grads = partial[0]
    for at in range(1, seq_count // 2):
        token_grads = token_grads + swap(partial[at].astype(BF), "seq", 2 * at).astype(F32)
    grad_hidden = token_grads.astype(BF)

    head_sums = sum_over_batch(jnp.dot(grads_t, hidden_all, preferred_element_type=F32))
    out_sums = sum_over_batch(jnp.dot(attended_t, grad_all, preferred_element_type=F32))
    row_block = width // batch_count
    head_part = head_sums.reshape(3, head_width, row_block).transpose(0, 2, 1)
    out_part = rows_to_owner(out_sums)[None]
    grad_weights = jnp.concatenate([head_part, out_part], axis=0)
    norm_factor = 1.0 / math.sqrt(row_count * seq_count * batch_count)
    return (grad_hidden[None], grad_weights * norm_factor)


def solution(mesh):
    placed = (
        P("batch", "seq", None),
        P("batch", "seq", None),
        P("batch", "seq", None, None),
        P(),
        P(),
        P(),
        P(),
    )
    return jax.shard_map(
        per_device,
        mesh=mesh,
        in_specs=placed,
        out_specs=(P("batch", "seq", None), P(None, "batch", "seq")),
        check_vma=False,
    )
```

time: 559 us -> 159 us (0.28)
  waiting for transfers between devices: 199 us -> 46.8 us
  local copies, waits for them, and re-layouts: 115 us -> 31.6 us
  other arithmetic: 85.2 us -> 3.85 us
  matrix products: 92 us -> 21.2 us
  blocking collectives: 41 us -> 0 us
  Pallas kernels: 0 us -> 29.1 us
  starting transfers between devices: 5.21 us -> 22.4 us
  between operations: 15.9 us -> 1.1 us
    reduce_scatter x2 -> x0, waiting for transfers between devices: 85.2 us -> none  [the longest x1 64.8 us: sharded_terms(): lax.psum_scatter(pieces[0], 'batch', scatter_dimension=0, tiled=True)]
    dot_general x27 -> x6, matrix products: 92 us -> 21.2 us  [the longest x4 14.1 us: dot(): lax.dot_general(left_side, right_side, dims, preferred_element_type=F32)]
    scatter-add x9 -> x0, other arithmetic: 68.5 us -> none  [add_blocks(): return running.at[chosen].add(portion)]
    unnamed x5 -> x0, waiting for transfers between devices: 63.1 us -> none
    all_to_all x1 -> x0, waiting for transfers between devices: 50.3 us -> none  [per_device(): lax.all_to_all(stacked, 'seq', split_axis=2, concat_axis=1, tiled=True)]
    ppermute x0 -> x18, waiting for transfers between devices: none -> 46.8 us  [the longest x16 44.7 us: swap(): lax.ppermute(value, axis, [(at, at ^ distance) for at in range(count)])]
    all_to_all x1 -> x0, blocking collectives: 41 us -> none  [per_device(): lax.all_to_all(head_grads, 'seq', split_axis=1, concat_axis=2, tiled=True)]
    pallas_call x0 -> x1, Pallas kernels: none -> 29.1 us  [attention(): pl.pallas_call(functools.partial(attention_kernel, blocks=blocks, slots=s...]
  transfers between devices with their start and end apart: 5 -> 18, of which waited for: 4 -> 7; matrix products, arithmetic and copies ran while one was open for 48% -> 28% of each run, Pallas kernels for 0% -> 0%
where the time goes in v1:
time: 159 us; the launch traced here: 156 us
  waiting for transfers between devices  46.8 us (29%)
  local copies, waits for them, and re-layouts  31.6 us (20%)
  Pallas kernels  29.1 us (18%)
  starting transfers between devices  22.4 us (14%)
  matrix products  21.2 us (13%)
  other arithmetic  3.85 us (2%)
    ppermute x16, waiting for transfers between devices, swap(): lax.ppermute(value, axis, [(at, at ^ distance) for at in range(count)])  44.7 us
    pallas_call x1, Pallas kernels, attention(): pl.pallas_call(functools.partial(attention_kernel, blocks=blocks, slots=s...  29.1 us
    ppermute x16, starting transfers between devices, swap(): lax.ppermute(value, axis, [(at, at ^ distance) for at in range(count)])  16.4 us
    dot_general x4, matrix products, dot(): lax.dot_general(left_side, right_side, dims, preferred_element_type=F32)  14.1 us
    unnamed x40, local copies, waits for them, and re-layouts  9.59 us
    slice x1, local copies, waits for them, and re-layouts, per_device(): chip_grads = jnp.concatenate([by_place[:, :, 0], came], axis=0)  6.52 us
    ppermute x2, starting transfers between devices, rows_to_owner(): came = lax.ppermute(piece, ('seq', 'batch'), moves)  6 us
    reshape x1, local copies, waits for them, and re-layouts, per_device(): by_place = grads_t.reshape(3 * head_width, seq_count // 2, 2, row_count)  5.94 us
  transfers between devices with their start and end apart: 18, of which 7 were waited for; matrix products, arithmetic and copies ran while one was open for 28% of the time, Pallas kernels for 0%

profile of v1, /device:TPU:4, one launch (start us, length us, event | category | flops | bytes accessed | tf_op | source)
XLA Modules:
  0.0 156.1 jit_solution(8572673369996638448)
XLA Ops:
  0.7 2.0 %collective-permute-start.4 = (bf16[384,1024]{1,0:T(8,128)(2,1)}, bf16[384,1024]{1,0:T(8,128)(2,1)}, u32[]{:S(2)}, u32[]{:S(2)}) collective-permute-start(bf16[384,1024]{1,0:T(8,128)(2,1)} %bitcast.50), channel_id=1, source_target_pairs={{0,16},{8,24},{16,0},{24,8},{1,17},{9,25},{17,1},{25,9},{2,18},{10... | collective-permute-start | bytes 2359304 | tf_op jit(solution)/shard_map/ppermute | solution.py:25
  2.7 18.6 %collective-permute-done.1 = bf16[384,1024]{1,0:T(8,128)(2,1)S(1)} collective-permute-done((bf16[384,1024]{1,0:T(8,128)(2,1)}, bf16[384,1024]{1,0:T(8,128)(2,1)S(1)}, u32[]{:S(2)}, u32[]{:S(2)}) %collective-permute-start.1) | collective-permute-done | bytes 786464 | tf_op jit(solution)/shard_map/ppermute | solution.py:25
  28.5 8.7 %collective-permute-done.4 = bf16[384,1024]{1,0:T(8,128)(2,1)} collective-permute-done((bf16[384,1024]{1,0:T(8,128)(2,1)}, bf16[384,1024]{1,0:T(8,128)(2,1)}, u32[]{:S(2)}, u32[]{:S(2)}) %collective-permute-start.4) | collective-permute-done | bytes 786464 | tf_op jit(solution)/shard_map/ppermute | solution.py:25
  37.2 4.0 %convolution_convert_fusion = bf16[768,1536]{0,1:T(8,128)(2,1)S(1)} fusion(bf16[256,1024]{0,1:T(8,128)(2,1)S(1)} %get-tuple-element.11, bf16[256,1024]{0,1:T(8,128)(2,1)S(1)} %get-tuple-element.13, bf16[256,1024]{0,1:T(8,128)(2,1)S(1)} %get-tuple-element.15, bf16[384,1024]{1,0:T(8,128)(2,1)} %collective-permute-done.2, ...), kind=kOutput, calls=%fused_computation | convolution fusion | flops 2434400256 | bytes 7077888 | tf_op jit(solution)/shard_map/dot_general | solution.py:20
  41.2 1.8 %slice_bitcast_fusion = (bf16[1536,256]{1,0:T(8,128)(2,1)S(1)}, bf16[1536,256]{1,0:T(8,128)(2,1)}, bf16[256,1536]{0,1:T(8,128)(2,1)}, bf16[256,1536]{0,1:T(8,128)(2,1)}, bf16[256,1536]{0,1:T(8,128)(2,1)}) fusion(bf16[768,1536]{0,1:T(8,128)(2,1)S(1)} %convolution_convert_fusion), kind=kLoop, calls=%fused_computation.75 | loop fusion | flops 393216 | bytes 6291456 | tf_op jit(solution)/shard_map/transpose | solution.py:244
  43.0 2.3 %copy.17.queries_t = bf16[256,1536]{1,0:T(8,128)(2,1)} copy(bf16[256,1536]{0,1:T(8,128)(2,1)} %get-tuple-element.29) | data formatting | bytes 1572864 | tf_op jit(solution)/shard_map/mul | solution.py:241
  45.3 2.3 %copy.18.keys_t = bf16[256,1536]{1,0:T(8,128)(2,1)} copy(bf16[256,1536]{0,1:T(8,128)(2,1)} %get-tuple-element.28) | data formatting | bytes 1572864 | tf_op jit(solution)/shard_map/slice | solution.py:242
  47.6 2.3 %copy.19.values_t = bf16[256,1536]{1,0:T(8,128)(2,1)} copy(bf16[256,1536]{0,1:T(8,128)(2,1)} %get-tuple-element.27) | data formatting | bytes 1572864 | tf_op jit(solution)/shard_map/slice | solution.py:243
  49.9 3.0 %convolution_convert_fusion.1.out_grads_t = bf16[256,1536]{1,0:T(8,128)(2,1)S(1)} fusion(bf16[384,1024]{1,0:T(8,128)(2,1)} %collective-permute-done.5, bf16[384,1024]{1,0:T(8,128)(2,1)} %collective-permute-done.4, bf16[384,1024]{1,0:T(8,128)(2,1)} %collective-permute-done.3, bf16[384,1024]{1,0:T(8,128)(2,1)} %bitcast.52, bf16[1024,1024]{1,0:T(8,128)(2,1)S(1)} %copy-done, ...), kind=kOutput, calls=%fused_computation.3 | convolution fusion | flops 818282496 | bytes 4456452 | tf_op jit(solution)/shard_map/dot_general | solution.py:20
  53.0 29.1 %attention.1 = (bf16[256,1536]{1,0:T(8,128)(2,1)S(1)}, bf16[256,1536]{1,0:T(8,128)(2,1)S(1)}, bf16[256,1536]{1,0:T(8,128)(2,1)S(1)}, bf16[256,1536]{1,0:T(8,128)(2,1)S(1)}) custom-call(s32[12]{0:T(128)S(1)} %fusion.16.place_of, s32[192]{0:T(256)S(1)} %reshape_squeeze.3.offsets, bf16[256,1536]{1,0:T(8,128)(2,1)S(1)} %copy-done.2, ...), custom_call_target="tpu_custom_call" | custom-call | flops 2415919104 | bytes 7864320 | tf_op jit(solution)/shard_map/attention/pallas_call | solution.py:148
  83.1 2.4 %fusion.13 = f32[256,1024]{1,0:T(8,128)S(1)} fusion(bf16[256,1536]{1,0:T(8,128)(2,1)S(1)} %get-tuple-element.9, bf16[384,1024]{1,0:T(8,128)(2,1)} %collective-permute-done.5, bf16[384,1024]{1,0:T(8,128)(2,1)} %collective-permute-done.4, bf16[384,1024]{1,0:T(8,128)(2,1)} %collective-permute-done.3, bf16[384,1024]{1,0:T(8,128)(2,1)S(1)} %bitcast.53), kind=kOutput, calls=%fused_computation.24 | convolution fusion | flops 817889280 | bytes 4980736 | tf_op jit(solution)/shard_map/dot_general | solution.py:266
  89.8 5.9 %reshape.14 = bf16[768,2,2,384]{3,2,1,0:T(2,128)(2,1)} reshape(bf16[768,1536]{1,0:T(8,128)(2,1)} %constant_dynamic-update-slice_fusion) | data formatting | bytes 4718592 | tf_op jit(solution)/shard_map/reshape | solution.py:254
  95.7 6.5 %fusion.25 = (bf16[768,2,1,384]{3,2,1,0:T(2,128)(2,1)S(1)}, bf16[768,2,1,384]{3,2,1,0:T(2,128)(2,1)S(1)}) fusion(bf16[768,2,2,384]{3,2,1,0:T(2,128)(2,1)} %reshape.14), kind=kLoop, calls=%fused_computation.77 | loop fusion | bytes 4718592 | tf_op jit(solution)/shard_map/slice | solution.py:256
  103.6 4.7 %fusion.12 = f32[768,1024]{1,0:T(8,128)S(1)} fusion(bf16[768,1536]{1,0:T(8,128)(2,1)} %constant_dynamic-update-slice_fusion, bf16[384,1024]{1,0:T(8,128)(2,1)} %collective-permute-done.2, bf16[384,1024]{1,0:T(8,128)(2,1)S(1)} %copy-done.14, bf16[384,1024]{1,0:T(8,128)(2,1)} %collective-permute-done, bf16[384,1024]{1,0:T(8,128)(2,1)S(1)} %bitcast.57), kind=kOutput, calls=%fused_computation.23 | convolution fusion | flops 2428502016 | bytes 8650752 | tf_op jit(solution)/shard_map/dot_general | solution.py:265
  110.3 2.6 %collective-permute-start.14 = (bf16[256,128]{1,0:T(8,128)(2,1)S(1)}, bf16[256,128]{1,0:T(8,128)(2,1)S(1)}, u32[]{:S(2)}, u32[]{:S(2)}) collective-permute-start(bf16[256,128]{1,0:T(8,128)(2,1)S(1)} %get-tuple-element.32), channel_id=1, source_target_pairs={{0,4},{1,5},{2,6},{3,7},{4,0},{5,1},{6,2},{7,3},{8,12},{9,13},{10,... | collective-permute-start | bytes 196616 | tf_op jit(solution)/shard_map/ppermute | solution.py:25
  113.8 4.1 %collective-permute-done.14 = bf16[256,128]{1,0:T(8,128)(2,1)S(1)} collective-permute-done((bf16[256,128]{1,0:T(8,128)(2,1)S(1)}, bf16[256,128]{1,0:T(8,128)(2,1)S(1)}, u32[]{:S(2)}, u32[]{:S(2)}) %collective-permute-start.14) | collective-permute-done | bytes 65568 | tf_op jit(solution)/shard_map/ppermute | solution.py:25
  119.1 3.9 %collective-permute-start.16 = (f32[128,128]{1,0:T(8,128)S(1)}, f32[128,128]{1,0:T(8,128)S(1)}, u32[]{:S(2)}, u32[]{:S(2)}) collective-permute-start(f32[128,128]{1,0:T(8,128)S(1)} %get-tuple-element.38), channel_id=1, source_target_pairs={{0,0},{8,2},{16,4},{24,6},{1,1},{9,3},{17,5},{25,7},{2,8},{10,10},... | collective-permute-start | bytes 196616 | tf_op jit(solution)/shard_map/ppermute | solution.py:207
  124.4 2.1 %collective-permute-start.17 = (f32[128,128]{1,0:T(8,128)S(1)}, f32[128,128]{1,0:T(8,128)S(1)}, u32[]{:S(2)}, u32[]{:S(2)}) collective-permute-start(f32[128,128]{1,0:T(8,128)S(1)} %get-tuple-element.37), channel_id=1, source_target_pairs={{0,1},{8,3},{16,5},{24,7},{1,0},{9,2},{17,4},{25,6},{2,9},{10,11},... | collective-permute-start | bytes 196616 | tf_op jit(solution)/shard_map/ppermute | solution.py:207
  126.4 2.0 %collective-permute-done.16 = f32[128,128]{1,0:T(8,128)S(1)} collective-permute-done((f32[128,128]{1,0:T(8,128)S(1)}, f32[128,128]{1,0:T(8,128)S(1)}, u32[]{:S(2)}, u32[]{:S(2)}) %collective-permute-start.16) | collective-permute-done | bytes 65568 | tf_op jit(solution)/shard_map/ppermute | solution.py:207
  128.5 2.3 %convolution_convert_fusion.2 = bf16[384,1024]{1,0:T(8,128)(2,1)} fusion(bf16[1536,1024]{0,1:T(8,128)(2,1)S(1)} %bitcast_dynamic-update-slice_fusion, bf16[768,2,384]{2,0,1:T(8,128)(2,1)S(1)} %collective-permute-done.6, bf16[768,2,384]{2,0,1:T(8,128)(2,1)S(1)} %bitcast.48), kind=kOutput, calls=%fused_computation.12 | convolution fusion | flops 1210712064 | bytes 6291456 | tf_op jit(solution)/shard_map/dot_general | solution.py:20
  132.3 3.8 %collective-permute-start.10 = (bf16[768,128]{1,0:T(8,128)(2,1)S(1)}, bf16[768,128]{1,0:T(8,128)(2,1)S(1)}, u32[]{:S(2)}, u32[]{:S(2)}) collective-permute-start(bf16[768,128]{1,0:T(8,128)(2,1)S(1)} %get-tuple-element.18), channel_id=1, source_target_pairs={{0,4},{1,5},{2,6},{3,7},{4,0},{5,1},{6,2},{7,3},{8,12},{9,13},{10,... | collective-permute-start | bytes 589832 | tf_op jit(solution)/shard_map/ppermute | solution.py:25
  136.1 2.7 %collective-permute-start.11 = (bf16[768,128]{1,0:T(8,128)(2,1)S(1)}, bf16[768,128]{1,0:T(8,128)(2,1)S(1)}, u32[]{:S(2)}, u32[]{:S(2)}) collective-permute-start(bf16[768,128]{1,0:T(8,128)(2,1)S(1)} %get-tuple-element.17), channel_id=1, source_target_pairs={{0,6},{1,7},{2,4},{3,5},{4,2},{5,3},{6,0},{7,1},{8,14},{9,15},{10,... | collective-permute-start | bytes 589832 | tf_op jit(solution)/shard_map/ppermute | solution.py:25
  139.3 10.9 %collective-permute-done.10 = bf16[768,128]{1,0:T(8,128)(2,1)S(1)} collective-permute-done((bf16[768,128]{1,0:T(8,128)(2,1)S(1)}, bf16[768,128]{1,0:T(8,128)(2,1)S(1)}, u32[]{:S(2)}, u32[]{:S(2)}) %collective-permute-start.10) | collective-permute-done | bytes 196640 | tf_op jit(solution)/shard_map/ppermute | solution.py:25
  151.4 4.8 %fusion.5 = bf16[1,384,1024]{2,1,0:T(8,128)(2,1)} fusion(bf16[384,1024]{1,0:T(8,128)(2,1)} %collective-permute-done.7, bf16[1536,1024]{0,1:T(8,128)(2,1)} %copy-done.8, bf16[768,2,384]{2,0,1:T(8,128)(2,1)} %bitcast.49, bf16[768,2,384]{2,0,1:T(8,128)(2,1)} %copy-done.9), kind=kOutput, calls=%fused_computation.13 | convolution fusion | flops 1211498496 | bytes 7077888 | tf_op jit(solution)/shard_map/dot_general | solution.py:20
  (83 shorter events, 22.1 us)
Async XLA Ops:
  0.6 49.3 %copy-start = (bf16[1024,1024]{1,0:T(8,128)(2,1)S(1)}, bf16[1024,1024]{1,0:T(8,128)(2,1)}, u32[]{:S(2)}) copy-start(bf16[1024,1024]{1,0:T(8,128)(2,1)} %param.13) | copy-start | bytes 6291460
  0.6 20.7 %collective-permute-start.1 = (bf16[384,1024]{1,0:T(8,128)(2,1)}, bf16[384,1024]{1,0:T(8,128)(2,1)S(1)}, u32[]{:S(2)}, u32[]{:S(2)}) collective-permute-start(bf16[384,1024]{1,0:T(8,128)(2,1)} %bitcast.54), channel_id=1, source_target_pairs={{0,16},{8,24},{16,0},{24,8},{1,17},{9,25},{17,1},{25,9},{2,18},{10... | collective-permute-start | bytes 2359304 | tf_op jit(solution)/shard_map/ppermute | solution.py:25
  0.7 36.4 %collective-permute-start.4 = (bf16[384,1024]{1,0:T(8,128)(2,1)}, bf16[384,1024]{1,0:T(8,128)(2,1)}, u32[]{:S(2)}, u32[]{:S(2)}) collective-permute-start(bf16[384,1024]{1,0:T(8,128)(2,1)} %bitcast.50), channel_id=1, source_target_pairs={{0,16},{8,24},{16,0},{24,8},{1,17},{9,25},{17,1},{25,9},{2,18},{10... | collective-permute-start | bytes 2359304 | tf_op jit(solution)/shard_map/ppermute | solution.py:25
  2.7 34.4 %collective-permute-start = (bf16[384,1024]{1,0:T(8,128)(2,1)}, bf16[384,1024]{1,0:T(8,128)(2,1)}, u32[]{:S(2)}, u32[]{:S(2)}) collective-permute-start(bf16[384,1024]{1,0:T(8,128)(2,1)} %bitcast.55), channel_id=1, source_target_pairs={{0,8},{8,0},{16,24},{24,16},{1,9},{9,1},{17,25},{25,17},{2,10},{10... | collective-permute-start | bytes 2359304 | tf_op jit(solution)/shard_map/ppermute | solution.py:25
  21.3 15.8 %copy-start.13 = (bf16[384,1024]{1,0:T(8,128)(2,1)}, bf16[384,1024]{1,0:T(8,128)(2,1)S(1)}, u32[]{:S(2)}) copy-start(bf16[384,1024]{1,0:T(8,128)(2,1)S(1)} %collective-permute-done.1) | copy-start | bytes 2359300
  21.4 15.8 %collective-permute-start.2 = (bf16[384,1024]{1,0:T(8,128)(2,1)S(1)}, bf16[384,1024]{1,0:T(8,128)(2,1)}, u32[]{:S(2)}, u32[]{:S(2)}) collective-permute-start(bf16[384,1024]{1,0:T(8,128)(2,1)S(1)} %collective-permute-done.1), channel_id=1, source_target_pairs={{0,8},{8,0},{16,24},{24,16},{1,9},{9,1},{17,25},{25,17},{2,10},{10... | collective-permute-start | bytes 2359304 | tf_op jit(solution)/shard_map/ppermute | solution.py:25
  21.4 28.6 %collective-permute-start.3 = (bf16[384,1024]{1,0:T(8,128)(2,1)}, bf16[384,1024]{1,0:T(8,128)(2,1)}, u32[]{:S(2)}, u32[]{:S(2)}) collective-permute-start(bf16[384,1024]{1,0:T(8,128)(2,1)} %bitcast.51), channel_id=1, source_target_pairs={{0,8},{8,0},{16,24},{24,16},{1,9},{9,1},{17,25},{25,17},{2,10},{10... | collective-permute-start | bytes 2359304 | tf_op jit(solution)/shard_map/ppermute | solution.py:25
  22.8 14.3 %copy-start.11 = (bf16[1,384,1024]{2,1,0:T(8,128)(2,1)S(1)}, bf16[1,384,1024]{2,1,0:T(8,128)(2,1)}, u32[]{:S(2)}) copy-start(bf16[1,384,1024]{2,1,0:T(8,128)(2,1)} %param.7) | copy-start | bytes 2359300
  37.2 12.8 %collective-permute-start.5 = (bf16[384,1024]{1,0:T(8,128)(2,1)}, bf16[384,1024]{1,0:T(8,128)(2,1)}, u32[]{:S(2)}, u32[]{:S(2)}) collective-permute-start(bf16[384,1024]{1,0:T(8,128)(2,1)} %collective-permute-done.4), channel_id=1, source_target_pairs={{0,8},{8,0},{16,24},{24,16},{1,9},{9,1},{17,25},{25,17},{2,10},{10... | collective-permute-start | bytes 2359304 | tf_op jit(solution)/shard_map/ppermute | solution.py:25
  53.0 30.1 %copy-start.10 = (bf16[1,384,1024]{2,1,0:T(8,128)(2,1)S(1)}, bf16[1,384,1024]{2,1,0:T(8,128)(2,1)}, u32[]{:S(2)}) copy-start(bf16[1,384,1024]{2,1,0:T(8,128)(2,1)} %param.8) | copy-start | bytes 2359300
  86.3 22.2 %collective-permute-start.12 = (bf16[256,512]{1,0:T(8,128)(2,1)}, bf16[256,512]{1,0:T(8,128)(2,1)S(1)}, u32[]{:S(2)}, u32[]{:S(2)}) collective-permute-start(bf16[256,512]{1,0:T(8,128)(2,1)} %pad_maximum_fusion.8), channel_id=1, source_target_pairs={{0,1},{1,0},{2,3},{3,2},{4,5},{5,4},{6,7},{7,6},{8,9},{9,8},{10,11... | collective-permute-start | bytes 786440 | tf_op jit(solution)/shard_map/ppermute | solution.py:25
  102.4 26.1 %collective-permute-start.6 = (bf16[768,2,384]{2,0,1:T(8,128)(2,1)S(1)}, bf16[768,2,384]{2,0,1:T(8,128)(2,1)S(1)}, u32[]{:S(2)}, u32[]{:S(2)}) collective-permute-start(bf16[768,2,384]{2,0,1:T(8,128)(2,1)S(1)} %bitcast.47), channel_id=1, source_target_pairs={{0,8},{8,0},{16,24},{24,16},{1,9},{9,1},{17,25},{25,17},{2,10},{10... | collective-permute-start | bytes 3538952 | tf_op jit(solution)/shard_map/ppermute | solution.py:25
  108.3 14.7 %copy-start.7 = (bf16[1536,1024]{0,1:T(8,128)(2,1)S(1)}, bf16[1536,1024]{0,1:T(8,128)(2,1)}, u32[]{:S(2)}) copy-start(bf16[1536,1024]{0,1:T(8,128)(2,1)} %copy-done.6) | copy-start | bytes 9437188
  108.6 5.1 %collective-permute-start.13 = (bf16[256,128]{1,0:T(8,128)(2,1)S(1)}, bf16[256,128]{1,0:T(8,128)(2,1)S(1)}, u32[]{:S(2)}, u32[]{:S(2)}) collective-permute-start(bf16[256,128]{1,0:T(8,128)(2,1)S(1)} %get-tuple-element.30), channel_id=1, source_target_pairs={{0,2},{1,3},{2,0},{3,1},{4,6},{5,7},{6,4},{7,5},{8,10},{9,11},{10,... | collective-permute-start | bytes 196616 | tf_op jit(solution)/shard_map/ppermute | solution.py:25
  110.3 7.6 %collective-permute-start.14 = (bf16[256,128]{1,0:T(8,128)(2,1)S(1)}, bf16[256,128]{1,0:T(8,128)(2,1)S(1)}, u32[]{:S(2)}, u32[]{:S(2)}) collective-permute-start(bf16[256,128]{1,0:T(8,128)(2,1)S(1)} %get-tuple-element.32), channel_id=1, source_target_pairs={{0,4},{1,5},{2,6},{3,7},{4,0},{5,1},{6,2},{7,3},{8,12},{9,13},{10,... | collective-permute-start | bytes 196616 | tf_op jit(solution)/shard_map/ppermute | solution.py:25
  112.9 6.2 %collective-permute-start.15 = (bf16[256,128]{1,0:T(8,128)(2,1)S(1)}, bf16[256,128]{1,0:T(8,128)(2,1)S(1)}, u32[]{:S(2)}, u32[]{:S(2)}) collective-permute-start(bf16[256,128]{1,0:T(8,128)(2,1)S(1)} %get-tuple-element.31), channel_id=1, source_target_pairs={{0,6},{1,7},{2,4},{3,5},{4,2},{5,3},{6,0},{7,1},{8,14},{9,15},{10,... | collective-permute-start | bytes 196616 | tf_op jit(solution)/shard_map/ppermute | solution.py:25
  113.2 18.9 %collective-permute-start.8 = (bf16[768,512]{1,0:T(8,128)(2,1)S(1)}, bf16[768,512]{1,0:T(8,128)(2,1)S(1)}, u32[]{:S(2)}, u32[]{:S(2)}) collective-permute-start(bf16[768,512]{1,0:T(8,128)(2,1)S(1)} %pad_maximum_fusion.3), channel_id=1, source_target_pairs={{0,1},{1,0},{2,3},{3,2},{4,5},{5,4},{6,7},{7,6},{8,9},{9,8},{10,11... | collective-permute-start | bytes 2359304 | tf_op jit(solution)/shard_map/ppermute | solution.py:25
  119.1 9.4 %collective-permute-start.16 = (f32[128,128]{1,0:T(8,128)S(1)}, f32[128,128]{1,0:T(8,128)S(1)}, u32[]{:S(2)}, u32[]{:S(2)}) collective-permute-start(f32[128,128]{1,0:T(8,128)S(1)} %get-tuple-element.38), channel_id=1, source_target_pairs={{0,0},{8,2},{16,4},{24,6},{1,1},{9,3},{17,5},{25,7},{2,8},{10,10},... | collective-permute-start | bytes 196616 | tf_op jit(solution)/shard_map/ppermute | solution.py:207
  124.2 26.2 %copy-start.8 = (bf16[1536,1024]{0,1:T(8,128)(2,1)}, bf16[1536,1024]{0,1:T(8,128)(2,1)S(1)}, u32[]{:S(2)}) copy-start(bf16[1536,1024]{0,1:T(8,128)(2,1)S(1)} %bitcast_dynamic-update-slice_fusion) | copy-start | bytes 9437188
  124.4 14.9 %collective-permute-start.17 = (f32[128,128]{1,0:T(8,128)S(1)}, f32[128,128]{1,0:T(8,128)S(1)}, u32[]{:S(2)}, u32[]{:S(2)}) collective-permute-start(f32[128,128]{1,0:T(8,128)S(1)} %get-tuple-element.37), channel_id=1, source_target_pairs={{0,1},{8,3},{16,5},{24,7},{1,0},{9,2},{17,4},{25,6},{2,9},{10,11},... | collective-permute-start | bytes 196616 | tf_op jit(solution)/shard_map/ppermute | solution.py:207
  130.9 20.5 %collective-permute-start.7 = (bf16[384,1024]{1,0:T(8,128)(2,1)}, bf16[384,1024]{1,0:T(8,128)(2,1)}, u32[]{:S(2)}, u32[]{:S(2)}) collective-permute-start(bf16[384,1024]{1,0:T(8,128)(2,1)} %convolution_convert_fusion.2), channel_id=1, source_target_pairs={{0,16},{8,24},{16,0},{24,8},{1,17},{9,25},{17,1},{25,9},{2,18},{10... | collective-permute-start | bytes 2359304 | tf_op jit(solution)/shard_map/ppermute | solution.py:25
  132.3 17.9 %collective-permute-start.10 = (bf16[768,128]{1,0:T(8,128)(2,1)S(1)}, bf16[768,128]{1,0:T(8,128)(2,1)S(1)}, u32[]{:S(2)}, u32[]{:S(2)}) collective-permute-start(bf16[768,128]{1,0:T(8,128)(2,1)S(1)} %get-tuple-element.18), channel_id=1, source_target_pairs={{0,4},{1,5},{2,6},{3,7},{4,0},{5,1},{6,2},{7,3},{8,12},{9,13},{10,... | collective-permute-start | bytes 589832 | tf_op jit(solution)/shard_map/ppermute | solution.py:25
  136.1 14.1 %collective-permute-start.11 = (bf16[768,128]{1,0:T(8,128)(2,1)S(1)}, bf16[768,128]{1,0:T(8,128)(2,1)S(1)}, u32[]{:S(2)}, u32[]{:S(2)}) collective-permute-start(bf16[768,128]{1,0:T(8,128)(2,1)S(1)} %get-tuple-element.17), channel_id=1, source_target_pairs={{0,6},{1,7},{2,4},{3,5},{4,2},{5,3},{6,0},{7,1},{8,14},{9,15},{10,... | collective-permute-start | bytes 589832 | tf_op jit(solution)/shard_map/ppermute | solution.py:25
  138.8 11.4 %collective-permute-start.9 = (bf16[768,128]{1,0:T(8,128)(2,1)S(1)}, bf16[768,128]{1,0:T(8,128)(2,1)S(1)}, u32[]{:S(2)}, u32[]{:S(2)}) collective-permute-start(bf16[768,128]{1,0:T(8,128)(2,1)S(1)} %get-tuple-element.16), channel_id=1, source_target_pairs={{0,2},{1,3},{2,0},{3,1},{4,6},{5,7},{6,4},{7,5},{8,10},{9,11},{10,... | collective-permute-start | bytes 589832 | tf_op jit(solution)/shard_map/ppermute | solution.py:25
  (9 other events, 32.4 us)

commit v2 on v1

v2 whole, which is shorter than its diff:
```python
import functools
import math

import jax
import jax.numpy as jnp
from jax import lax
from jax.experimental import pallas as pl
from jax.experimental.pallas import tpu as pltpu
from jax.sharding import PartitionSpec as P

BLK = 128
BF = jnp.bfloat16
F32 = jnp.float32
LAST_LAST = (((1,), (1,)), ((), ()))
FIRST_FIRST = (((0,), (0,)), ((), ()))
VMEM_BYTES = 62 * 1024 * 1024
HEAVY = pl.CostEstimate(flops=1, bytes_accessed=70_000_000, transcendentals=0)
LIGHT = pl.CostEstimate(flops=1, bytes_accessed=1, transcendentals=0)


def dot(left_side, right_side, dims):
    return lax.dot_general(left_side, right_side, dims, preferred_element_type=F32)


def swap(value, axis, distance):
    count = lax.axis_size(axis)
    return lax.ppermute(value, axis, [(at, at ^ distance) for at in range(count)])


def spread(shard, axis, count):
    pieces = {0: shard}
    bit = count // 2
    while bit:
        for place in sorted(pieces):
            pieces[place | bit] = swap(pieces[place], axis, bit)
        bit //= 2
    return [pieces[place] for place in sorted(pieces)]


def side_by_side(parts):
    return parts[0] if len(parts) == 1 else jnp.concatenate(parts, axis=1)


def weight_rows_kernel(_, query_cols, key_cols, value_cols, rows):
    for at, cols in enumerate((query_cols, key_cols, value_cols)):
        rows[at * BLK : (at + 1) * BLK, :] = cols[...].T


def weight_rows(seq_index, head_width, weights):
    width = weights[0].shape[0]
    pairs = head_width // BLK
    first = jnp.reshape(seq_index * pairs, (1,)).astype(jnp.int32)
    return pl.pallas_call(
        weight_rows_kernel,
        grid_spec=pltpu.PrefetchScalarGridSpec(
            num_scalar_prefetch=1,
            grid=(pairs,),
            in_specs=[pl.BlockSpec((width, BLK), lambda pair, first: (0, first[0] + pair))] * 3,
            out_specs=pl.BlockSpec((3 * BLK, width), lambda pair, _: (pair, 0)),
        ),
        out_shape=jax.ShapeDtypeStruct((3 * head_width, width), BF),
        compiler_params=pltpu.CompilerParams(vmem_limit_bytes=VMEM_BYTES),
        cost_estimate=LIGHT,
        name="weight_rows",
    )(first, *weights)


def project_kernel(*refs, count, pairs, scale):
    tokens, grads = refs[:count], refs[count : 2 * count]
    rows, out_rows = refs[2 * count : 2 * count + 2]
    queries_t, out_grads_t, keys_t, values_t, keys, values = refs[2 * count + 2 :]
    step = tokens[0].shape[0]
    for at in range(count):
        span = slice(at * step, (at + 1) * step)
        heads_t = dot(rows[...], tokens[at][...], LAST_LAST)
        out_grads_t[:, span] = dot(out_rows[...], grads[at][...], LAST_LAST).astype(BF)
        for pair in range(pairs):
            own = slice(pair * BLK, (pair + 1) * BLK)
            base = pair * 3 * BLK
            queries_t[own, span] = heads_t[base : base + BLK].astype(BF) * scale
            key_part = heads_t[base + BLK : base + 2 * BLK]
            value_part = heads_t[base + 2 * BLK : base + 3 * BLK]
            keys_t[own, span] = key_part.astype(BF)
            values_t[own, span] = value_part.astype(BF)
            keys[span, own] = key_part.T.astype(BF)
            values[span, own] = value_part.T.astype(BF)


def project(tokens, grads, rows, out_rows, scale):
    count, step = len(tokens), tokens[0].shape[0]
    width = out_rows.shape[0]
    across = jax.ShapeDtypeStruct((width, count * step), BF)
    down = jax.ShapeDtypeStruct((count * step, width), BF)
    return pl.pallas_call(
        functools.partial(project_kernel, count=count, pairs=width // BLK, scale=scale),
        out_shape=[across] * 4 + [down] * 2,
        compiler_params=pltpu.CompilerParams(vmem_limit_bytes=VMEM_BYTES),
        cost_estimate=LIGHT,
        name="project",
    )(*tokens, *grads, rows, out_rows)


def attend(
    place_of, offsets, head_base, places, queries_t, out_grads_t, key_refs, sums, put, slots, blocks, head_size
):
    keys_t, values_t, keys, values = key_refs
    key_acc, value_acc = sums
    key_at = lax.broadcasted_iota(jnp.int32, (BLK, BLK), 0)
    query_at = lax.broadcasted_iota(jnp.int32, (BLK, BLK), 1)
    causal = key_at <= query_at
    first_head = lax.broadcasted_iota(jnp.int32, (2 * head_size, BLK), 0) < head_size
    plus = functools.partial(functools.reduce, jnp.add)
    cut = [slice(slot * BLK, (slot + 1) * BLK) for slot in range(slots)]

    for step in range(queries_t.shape[1] // BLK):
        place = places + step
        block = place_of[place]
        cols = slice(step * BLK, (step + 1) * BLK)
        pair_queries = queries_t[:, cols]
        pair_grads = out_grads_t[:, cols]
        scored = []
        for half in range(2):
            head = head_base + half
            rows = slice(half * head_size, (half + 1) * head_size)
            keep = first_head if half == 0 else ~first_head
            head_queries = jnp.where(keep, pair_queries, jnp.zeros_like(pair_queries))
            head_grads = jnp.where(keep, pair_grads, jnp.zeros_like(pair_grads))
            named, usable = [], []
            for slot in range(slots):
                offset = offsets[(head * blocks + block) * slots + slot]
                usable.append(offset <= block)
                named.append(place_of[jnp.where(offset <= block, block - offset, 0)])
            spans = [pl.ds(pl.multiple_of(at * BLK, BLK), BLK) for at in named]
            seen_keys = jnp.concatenate([keys[span, :] for span in spans], axis=0)
            seen_values = jnp.concatenate([values[span, :] for span in spans], axis=0)
            scores = jnp.dot(seen_keys, head_queries, preferred_element_type=F32)
            prob_grad = jnp.dot(seen_values, head_grads, preferred_element_type=F32)
            scores = [
                jnp.where(causal if slot == 0 else usable[slot], scores[cut[slot]], -jnp.inf)
                for slot in range(slots)
            ]
            scored.append((rows, named, spans, scores, [prob_grad[part] for part in cut]))
        parts = []
        for rows, named, spans, scores, prob_grad in scored:
            top = jnp.max(functools.reduce(jnp.maximum, scores), axis=0, keepdims=True)
            raised = [jnp.exp(part - top) for part in scores]
            total = jnp.sum(plus(raised), axis=0, keepdims=True)
            inverse = 1.0 / total
            probs = [part * inverse for part in raised]
            probs_half = jnp.concatenate([part.astype(BF) for part in probs], axis=0)
            delta = jnp.sum(
                plus([part * grad for part, grad in zip(probs, prob_grad)]), axis=0, keepdims=True
            )
            score_grad = jnp.concatenate(
                [(part * (grad - delta)).astype(BF) for part, grad in zip(probs, prob_grad)], axis=0
            )
            seen_values_t = side_by_side([values_t[rows, span] for span in spans])
            seen_keys_t = side_by_side([keys_t[rows, span] for span in spans])
            attended = jnp.dot(seen_values_t, probs_half, preferred_element_type=F32)
            query_grad = jnp.dot(seen_keys_t, score_grad, preferred_element_type=F32)
            put(rows, cols, attended, query_grad * (1.0 / math.sqrt(head_size)))
            value_part = dot(out_grads_t[rows, cols], probs_half, LAST_LAST)
            key_part = dot(queries_t[rows, cols], score_grad, LAST_LAST)
            parts.append((rows, named, key_part, value_part))
        for rows, named, key_part, value_part in parts:
            for at, part in zip(named, cut):
                key_acc[at, rows, :] += key_part[:, part]
                value_acc[at, rows, :] += value_part[:, part]


def own_half_kernel(place_of, offsets, *refs, count, slots, blocks, head_size, scale):
    tokens = refs[:count]
    (rows, queries_t, out_grads_t, keys_in, values_in, keys_down, values_down) = refs[count : count + 7]
    (
        later_queries_t,
        keys_t,
        values_t,
        keys,
        values,
        attended_t,
        query_grad_t,
        key_acc_out,
        value_acc_out,
    ) = refs[count + 7 :]
    pair = pl.program_id(0)
    key_acc, value_acc = key_acc_out.at[0], value_acc_out.at[0]
    half = queries_t.shape[1]
    step = tokens[0].shape[0]
    keys_t[:, :half] = keys_in[...]
    values_t[:, :half] = values_in[...]
    keys[:half, :] = keys_down[...]
    values[:half, :] = values_down[...]
    for at in range(count):
        span = slice(at * step, (at + 1) * step)
        whole = slice(half + at * step, half + (at + 1) * step)
        heads_t = dot(rows[...], tokens[at][...], LAST_LAST)
        later_queries_t[:, span] = heads_t[:BLK].astype(BF) * scale
        keys_t[:, whole] = heads_t[BLK : 2 * BLK].astype(BF)
        values_t[:, whole] = heads_t[2 * BLK :].astype(BF)
        keys[whole, :] = heads_t[BLK : 2 * BLK].T.astype(BF)
        values[whole, :] = heads_t[2 * BLK :].T.astype(BF)
    key_acc[...] = jnp.zeros(key_acc.shape, F32)
    value_acc[...] = jnp.zeros(value_acc.shape, F32)

    def put(at_rows, cols, attended, query_grad):
        attended_t[at_rows, cols] = attended.astype(BF)
        query_grad_t[at_rows, cols] = query_grad.astype(BF)

    attend(
        place_of,
        offsets,
        2 * pair,
        0,
        queries_t,
        out_grads_t,
        (keys_t, values_t, keys, values),
        (key_acc, value_acc),
        put,
        slots,
        blocks,
        head_size,
    )


def own_half(place_of, offsets, tokens, rows, projected):
    queries_t = projected[0]
    width, half = queries_t.shape
    heads, blocks, slots = offsets.shape
    head_size = width // heads
    pairs = width // BLK
    total = blocks * BLK
    model = rows.shape[1]
    whole_piece = pl.BlockSpec(tokens[0].shape, lambda pair, *_: (0, 0))
    half_across = pl.BlockSpec((BLK, half), lambda pair, *_: (pair, 0))
    across = pl.BlockSpec((BLK, total), lambda pair, *_: (pair, 0))
    half_down = pl.BlockSpec((half, BLK), lambda pair, *_: (0, pair))
    down = pl.BlockSpec((total, BLK), lambda pair, *_: (0, pair))
    sums = pl.BlockSpec((1, blocks, BLK, BLK), lambda pair, *_: (pair, 0, 0, 0))
    shape = jax.ShapeDtypeStruct
    return pl.pallas_call(
        functools.partial(
            own_half_kernel,
            count=len(tokens),
            slots=slots,
            blocks=blocks,
            head_size=head_size,
            scale=1.0 / math.sqrt(head_size),
        ),
        grid_spec=pltpu.PrefetchScalarGridSpec(
            num_scalar_prefetch=2,
            grid=(pairs,),
            in_specs=[whole_piece] * len(tokens)
            + [pl.BlockSpec((3 * BLK, model), lambda pair, *_: (pair, 0))]
            + [half_across] * 4
            + [half_down] * 2,
            out_specs=[half_across, across, across, down, down, half_across, half_across, sums, sums],
        ),
        out_shape=[
            shape((width, half), BF),
            shape((width, total), BF),
            shape((width, total), BF),
            shape((total, width), BF),
            shape((total, width), BF),
            shape((width, half), BF),
            shape((width, half), BF),
            shape((pairs, blocks, BLK, BLK), F32),
            shape((pairs, blocks, BLK, BLK), F32),
        ],
        compiler_params=pltpu.CompilerParams(vmem_limit_bytes=VMEM_BYTES),
        cost_estimate=LIGHT,
        name="own_half",
    )(place_of, offsets.reshape(-1), *tokens, rows, *projected)


def later_half_kernel(place_of, offsets, col_order, *refs, count, pair, slots, blocks, head_size):
    tokens_at, grads_at = refs[:count], refs[count : 2 * count]
    (
        out_rows,
        queries_t,
        keys_t,
        values_t,
        keys,
        values,
        attended_first,
        query_grad_first,
        key_first,
        value_first,
        stay,
        leave,
        *terms,
        attended_t,
        out_grads_t,
        key_acc,
        value_acc,
        tokens_here,
        grads_here,
        arrived,
    ) = refs[2 * count :]
    half = queries_t.shape[1]
    near = count // 2
    tokens = [tokens_here.at[at] for at in range(count)]
    grads = [grads_here.at[at] for at in range(count)]
    step = grads[0].shape[0]

    def fetch(sources, targets, first_sem):
        copies = [
            pltpu.make_async_copy(source, target, arrived.at[first_sem + at])
            for at, (source, target) in enumerate(zip(sources, targets))
        ]
        for copy in copies:
            copy.start()
        return copies

    first_copies = fetch(grads_at[near:], grads[near:], 0)
    later_copies = fetch((*tokens_at, *grads_at[:near]), (*tokens, *grads[:near]), near)
    for copy in first_copies:
        copy.wait()
    for at in range(near):
        span = slice(at * step, (at + 1) * step)
        out_grads_t[:, span] = dot(out_rows[...], grads[near + at][...], LAST_LAST).astype(BF)
    key_acc[...] = key_first[0]
    value_acc[...] = value_first[0]
    attended_t[:, :half] = attended_first[...]

    def columns(place, at):
        left = place // 2 * step + at
        return (leave if place % 2 else stay), slice(left, left + BLK)

    for at in range(0, half, BLK):
        target, cols = columns(at // step, at % step)
        target[:BLK, cols] = query_grad_first[:, at : at + BLK]

    def put(at_rows, cols, attended, query_grad):
        attended_t[at_rows, half + cols.start : half + cols.stop] = attended.astype(BF)
        target, placed = columns(near + cols.start // step, cols.start % step)
        target[at_rows, placed] = query_grad.astype(BF)

    attend(
        place_of,
        offsets,
        2 * pair,
        blocks // 2,
        queries_t,
        out_grads_t,
        (keys_t, values_t, keys, values),
        (key_acc, value_acc),
        put,
        slots,
        blocks,
        head_size,
    )
    for at in range(blocks):
        target, cols = columns(at * BLK // step, at * BLK % step)
        target[BLK : 2 * BLK, cols] = key_acc[at].astype(BF)
        target[2 * BLK :, cols] = value_acc[at].astype(BF)

    for copy in later_copies:
        copy.wait()
    stay_rows, leave_rows, attended_rows = stay[...], leave[...], attended_t[...]
    width = tokens[0].shape[1]
    for col in range(0, width, 2 * BLK):
        spans = [
            pl.ds(pl.multiple_of(col_order[col // BLK + side] * BLK, BLK), BLK) for side in range(2)
        ]

        def taken(pieces):
            return jnp.concatenate(
                [side_by_side([piece[:, span] for span in spans]) for piece in pieces], axis=0
            )

        head_terms = jnp.dot(stay_rows, taken(tokens[0::2]), preferred_element_type=F32)
        head_terms += jnp.dot(leave_rows, taken(tokens[1::2]), preferred_element_type=F32)
        out_terms = jnp.dot(attended_rows, taken(grads), preferred_element_type=F32)
        first_rows, last_rows = terms[:2] if col < width // 2 else terms[2:]
        cols = slice(col % (width // 2), col % (width // 2) + 2 * BLK)
        first_rows[:BLK, cols] = out_terms.astype(first_rows.dtype)
        first_rows[BLK:, cols] = head_terms[:BLK].astype(first_rows.dtype)
        last_rows[:, cols] = head_terms[BLK:].astype(last_rows.dtype)


def later_half(place_of, offsets, col_order, tokens, grads, out_rows, pair, first):
    (queries_t, keys_t, values_t, keys, values, attended_t, query_grad_t, key_acc, value_acc) = first
    width, half = queries_t.shape
    heads, blocks, slots = offsets.shape
    head_size = width // heads
    total = blocks * BLK
    model = out_rows.shape[1]
    whole_piece = pl.BlockSpec(memory_space=pl.ANY)
    half_across = pl.BlockSpec((BLK, half), lambda *_: (pair, 0))
    across = pl.BlockSpec((BLK, total), lambda *_: (pair, 0))
    down = pl.BlockSpec((total, BLK), lambda *_: (0, pair))
    sums = pl.BlockSpec((1, blocks, BLK, BLK), lambda *_: (pair, 0, 0, 0))
    shape = jax.ShapeDtypeStruct
    results = [
        shape((3 * BLK, half), BF),
        shape((3 * BLK, half), BF),
        shape((2 * BLK, model // 2), BF),
        shape((2 * BLK, model // 2), BF),
        shape((2 * BLK, model // 2), F32),
        shape((2 * BLK, model // 2), F32),
    ]
    return pl.pallas_call(
        functools.partial(
            later_half_kernel,
            count=len(grads),
            pair=pair,
            slots=slots,
            blocks=blocks,
            head_size=head_size,
        ),
        grid_spec=pltpu.PrefetchScalarGridSpec(
            num_scalar_prefetch=3,
            grid=(1,),
            in_specs=[whole_piece] * (2 * len(grads))
            + [pl.BlockSpec((BLK, model), lambda *_: (pair, 0))]
            + [half_across, across, across, down, down, half_across, half_across, sums, sums],
            out_specs=[pl.BlockSpec(result.shape, lambda *_: (0, 0)) for result in results],
            scratch_shapes=[pltpu.VMEM((BLK, total), BF), pltpu.VMEM((BLK, half), BF)]
            + [pltpu.VMEM((blocks, BLK, BLK), F32)] * 2
            + [pltpu.VMEM((len(grads), *grads[0].shape), BF)] * 2
            + [pltpu.SemaphoreType.DMA((2 * len(grads),))],
        ),
        out_shape=results,
        compiler_params=pltpu.CompilerParams(vmem_limit_bytes=VMEM_BYTES),
        cost_estimate=LIGHT,
        name="later_half",
    )(place_of, offsets.reshape(-1), col_order, *tokens, *grads, out_rows, *first)


def finish_kernel(*refs):
    total = refs[0][...]
    for part in refs[1:-1]:
        total = total + part[...].astype(F32)
    refs[-1][...] = total.astype(BF)


def finish(own, came):
    return pl.pallas_call(
        finish_kernel,
        out_shape=jax.ShapeDtypeStruct(own.shape, BF),
        compiler_params=pltpu.CompilerParams(vmem_limit_bytes=VMEM_BYTES),
        cost_estimate=HEAVY,
        name="finish",
    )(own, *came)


def halves(pieces, low):
    kept = {place: part for place, part in pieces.items() if (place // low) % 2 == 0}
    return side_by_side([pieces[place + low].astype(BF) for place in kept]), kept


def joined(kept, came):
    block = came.shape[1] // len(kept)
    return {
        place: part + came[:, at * block : (at + 1) * block].astype(F32)
        for at, (place, part) in enumerate(kept.items())
    }


def tied(values, others):
    return list(lax.optimization_barrier((*values, *others))[: len(values)])


def rows_to_owner(block_sum):
    seq_count, batch_count = lax.axis_size("seq"), lax.axis_size("batch")
    batch_at = lax.axis_index("batch")
    ratio = batch_count // seq_count
    height, width = block_sum.shape[0] // ratio, block_sum.shape[1]
    placed = jnp.zeros((height, ratio * width), F32)
    for turn in range(ratio):
        moves = []
        for b in range(batch_count):
            for s in range(seq_count):
                target = (b // ratio) * batch_count + ratio * s + (b + turn) % ratio
                moves.append((s * batch_count + b, target))
        piece = lax.dynamic_slice(
            block_sum, (((batch_at + turn) % ratio) * height, 0), (height, width)
        )
        came = lax.ppermute(piece, ("seq", "batch"), moves)
        placed = lax.dynamic_update_slice(
            placed, came, (0, ((batch_at - turn) % ratio) * width)
        )
    return placed


def per_device(hidden, grad_out, block_offsets, w_query, w_key, w_value, w_out):
    tokens = hidden[0]
    grad_rows = grad_out[0]
    offsets = block_offsets[0]
    row_count, width = tokens.shape
    seq_count = lax.axis_size("seq")
    batch_count = lax.axis_size("batch")
    seq_at = lax.axis_index("seq")
    head_width = width // seq_count
    head_size = head_width // offsets.shape[0]
    pairs = head_width // BLK
    half_count = seq_count // 2

    weights = (w_query, w_key, w_value)
    rows = weight_rows(seq_at, head_width, weights)
    out_rows = lax.dynamic_slice(w_out, (seq_at * head_width, 0), (head_width, width))

    shard_blocks = row_count // BLK
    block_at = jnp.arange(shard_blocks * seq_count, dtype=jnp.int32)
    place_of = ((block_at // shard_blocks) ^ seq_at) * shard_blocks + block_at % shard_blocks

    near_tokens = spread(tokens, "seq", half_count)
    near_grads = spread(grad_rows, "seq", half_count)
    projected = project(near_tokens, near_grads, rows, out_rows, 1.0 / math.sqrt(head_size))
    far_tokens = swap(tokens, "seq", half_count)
    mate_rows = weight_rows(seq_at ^ 1, head_width, weights)
    far_grads, far_tokens, mate_rows, *projected = lax.optimization_barrier(
        (grad_rows, far_tokens, mate_rows, *projected)
    )
    far_grads = swap(far_grads, "seq", half_count)
    far_tokens = spread(far_tokens, "seq", half_count)
    first = own_half(place_of, offsets, far_tokens, rows, projected)
    far_grads, *first = lax.optimization_barrier((far_grads, *first))
    far_grads = spread(far_grads, "seq", half_count)
    all_tokens, all_grads = near_tokens + far_tokens, near_grads + far_grads

    col_block = width // batch_count
    direct = col_block == BLK
    relative = [*range(1, batch_count, 2), *range(0, batch_count, 2)]
    col_order = jnp.arange(width // BLK, dtype=jnp.int32)
    if direct:
        col_order = jnp.stack([lax.axis_index("batch") ^ place for place in relative]).astype(jnp.int32)
    batch_at = lax.axis_index("batch")

    even = range(0, batch_count, 2)

    def begin(sent_terms, kept_terms):
        if direct:
            return sent_terms, {p: kept_terms[:, p // 2 * BLK : (p // 2 + 1) * BLK] for p in even}
        terms = jnp.concatenate([sent_terms.astype(F32), kept_terms], axis=1)
        pieces = [
            lax.dynamic_slice(
                terms, (0, (batch_at ^ p) * col_block), (terms.shape[0], col_block)
            )
            for p in range(batch_count)
        ]
        return side_by_side([pieces[p + 1].astype(BF) for p in even]), {p: pieces[p] for p in even}

    stayed, left, groups = [], [], []
    for pair in range(pairs):
        stay, leave, *terms = later_half(
            place_of, offsets, col_order, all_tokens, all_grads, out_rows, pair, first
        )
        stayed.append(stay)
        left.append(leave)
        if pair < pairs - 1:
            terms = [jnp.concatenate(terms[:2], axis=0), jnp.concatenate(terms[2:], axis=0)]
        count = len(terms) // 2
        for at in range(count):
            goes, kept = begin(terms[at], terms[count + at])
            if at:
                goes, *came = tied([goes, *came], [])
            groups.append((swap(goes, "batch", 1), kept))
            if pair == pairs - 1 and not at:
                came = [swap(leave, "seq", 1) for leave in left]

    stayed, came = jnp.concatenate(stayed, axis=0), jnp.concatenate(came, axis=0)
    partial = []
    for at in range(half_count):
        cols = slice(at * row_count, (at + 1) * row_count)
        partial.append(
            dot(stayed[:, cols], rows, FIRST_FIRST) + dot(came[:, cols], mate_rows, FIRST_FIRST)
        )
    sent = [partial[at].astype(BF) for at in range(1, half_count)]
    token_parts = [swap(part, "seq", 2 * at) for at, part in enumerate(sent, 1)]
    came_terms = [part for part, _ in groups]
    came_terms[pairs - 1] = tied([came_terms[pairs - 1]], sent)[0]

    pieces = [joined(kept, came) for (_, kept), came in zip(groups, came_terms)]
    low = 2
    while low < batch_count:
        for at, parts in enumerate(pieces):
            goes, kept = halves(parts, low)
            if at == pairs - 1 and low * 2 == batch_count:
                goes = tied([goes], [came_terms[pairs]])[0]
            pieces[at] = joined(kept, swap(goes, "batch", low))
        low *= 2
    sums = [parts[0] for parts in pieces]
    out_sums = jnp.concatenate([part[:BLK] for part in sums[:pairs]], axis=0)
    out_sums = tied([out_sums], token_parts)[0]
    out_part = rows_to_owner(out_sums)[None]
    grad_hidden = finish(partial[0], token_parts)
    sums = [*sums[: pairs - 1], jnp.concatenate(sums[pairs - 1 :], axis=0)]
    sums[0], out_part = tied([sums[0], out_part], [grad_hidden])
    row_block = width // batch_count
    head_part = jnp.stack([part[BLK:].reshape(3, BLK, row_block) for part in sums], axis=1)
    head_part = head_part.reshape(3, head_width, row_block).transpose(0, 2, 1)
    grad_weights = jnp.concatenate([head_part, out_part], axis=0)
    norm_factor = 1.0 / math.sqrt(row_count * seq_count * batch_count)
    return (grad_hidden[None], grad_weights * norm_factor)


def solution(mesh):
    placed = (
        P("batch", "seq", None),
        P("batch", "seq", None),
        P("batch", "seq", None, None),
        P(),
        P(),
        P(),
        P(),
    )
    return jax.shard_map(
        per_device,
        mesh=mesh,
        in_specs=placed,
        out_specs=(P("batch", "seq", None), P(None, "batch", "seq")),
        check_vma=False,
    )
```

time: 159 us -> 120 us (0.75)
  Pallas kernels: 29.1 us -> 54.8 us
  local copies, waits for them, and re-layouts: 31.6 us -> 8.55 us
  waiting for transfers between devices: 46.8 us -> 25.9 us
  matrix products: 21.2 us -> 4.37 us
  starting transfers between devices: 22.4 us -> 19.4 us
    pallas_call x1 -> x7, Pallas kernels: 29.1 us -> 54.8 us  [the longest x2 25.3 us: later_half(): pl.pallas_call(functools.partial(later_half_kernel, count=len(grads), pai...]
    ppermute x16 -> x18, waiting for transfers between devices: 44.7 us -> 24.9 us  [swap(): lax.ppermute(value, axis, [(at, at ^ distance) for at in range(count)])]
    slice x3, local copies, waits for them, and re-layouts: 11.1 us -> 0.03 us  [the longest x1 0.01 us: per_device(): part[BLK:].reshape(3, BLK, row_block)]
    dot_general x4, matrix products: 14.1 us -> 4.37 us  [dot(): lax.dot_general(left_side, right_side, dims, preferred_element_type=F32)]
    dot_general x2 -> x0, matrix products: 7.14 us -> none  [the longest x1 4.72 us: per_device(): jnp.dot(grads_t, hidden_all, preferred_element_type=F32)]
    reshape x2 -> x1, local copies, waits for them, and re-layouts: 6.1 us -> 0.32 us  [per_device(): head_part = head_part.reshape(3, head_width, row_block).transpose(0, 2, 1)]
    unnamed x40 -> x32, local copies, waits for them, and re-layouts: 9.59 us -> 4.68 us
    ppermute x16 -> x18, starting transfers between devices: 16.4 us -> 13.7 us  [swap(): lax.ppermute(value, axis, [(at, at ^ distance) for at in range(count)])]
  transfers between devices with their start and end apart: 18 -> 20, of which waited for: 7 -> 11; matrix products, arithmetic and copies ran while one was open for 28% -> 9% of each run, Pallas kernels for 0% -> 36%
where the time goes in v2:
time: 120 us; the launch traced here: 118 us
  Pallas kernels  54.8 us (46%)
  waiting for transfers between devices  25.9 us (22%)
  starting transfers between devices  19.4 us (16%)
  local copies, waits for them, and re-layouts  8.55 us (7%)
  matrix products  4.37 us (4%)
  other arithmetic  3.8 us (3%)
    pallas_call x2, Pallas kernels, later_half(): pl.pallas_call(functools.partial(later_half_kernel, count=len(grads), pai...  25.3 us
    ppermute x18, waiting for transfers between devices, swap(): lax.ppermute(value, axis, [(at, at ^ distance) for at in range(count)])  24.9 us
    pallas_call x1, Pallas kernels, own_half(): pl.pallas_call(functools.partial(own_half_kernel, count=len(tokens), slot...  15.8 us
    ppermute x18, starting transfers between devices, swap(): lax.ppermute(value, axis, [(at, at ^ distance) for at in range(count)])  13.7 us
    pallas_call x1, Pallas kernels, project(): pl.pallas_call(functools.partial(project_kernel, count=count, pairs=width...  5.9 us
    ppermute x2, starting transfers between devices, rows_to_owner(): came = lax.ppermute(piece, ('seq', 'batch'), moves)  5.73 us
    pallas_call x2, Pallas kernels, weight_rows(): pl.pallas_call(weight_rows_kernel, grid_spec=pltpu.PrefetchScalarGridSpec...  5.14 us
    unnamed x32, local copies, waits for them, and re-layouts  4.68 us
  transfers between devices with their start and end apart: 20, of which 11 were waited for; matrix products, arithmetic and copies ran while one was open for 9% of the time, Pallas kernels for 36%

profile of v2, /device:TPU:4, one launch (start us, length us, event | category | flops | bytes accessed | tf_op | source)
XLA Modules:
  0.0 117.8 jit_solution(17626720311780211326)
XLA Ops:
  1.2 2.6 %weight_rows.2 = bf16[768,1024]{1,0:T(8,128)(2,1)} custom-call(s32[1]{0:T(128)} %bitcast.10._, bf16[1024,1024]{1,0:T(8,128)(2,1)} %query_cols.3, bf16[1024,1024]{1,0:T(8,128)(2,1)} %key_cols.3, bf16[1024,1024]{1,0:T(8,128)(2,1)} %value_cols.3), custom_call_target="tpu_custom_call" | custom-call | flops 1 | bytes 1 | tf_op jit(solution)/shard_map/weight_rows/pallas_call | solution.py:53
  3.8 2.6 %weight_rows.3.refs_4_.refs_2_ = bf16[768,1024]{1,0:T(8,128)(2,1)} custom-call(s32[1]{0:T(128)} %bitcast.11._, bf16[1024,1024]{1,0:T(8,128)(2,1)} %query_cols.3, bf16[1024,1024]{1,0:T(8,128)(2,1)} %key_cols.3, bf16[1024,1024]{1,0:T(8,128)(2,1)} %value_cols.3), custom_call_target="tpu_custom_call" | custom-call | flops 1 | bytes 1 | tf_op jit(solution)/shard_map/weight_rows/pallas_call | solution.py:53
  6.4 1.9 %constant_dynamic-slice_fusion.2.refs_5_.refs_8_ = bf16[256,1024]{1,0:T(8,128)(2,1)} fusion(bf16[1024,1024]{1,0:T(8,128)(2,1)} %param.13, s32[]{:T(128)S(6)} %select_n.43), kind=kLoop, calls=%fused_computation.46 | loop fusion | bytes 1048580 | tf_op jit(solution)/shard_map/dynamic_slice | solution.py:501
  9.1 5.9 %project.1 = (bf16[256,768]{1,0:T(8,128)(2,1)}, bf16[256,768]{1,0:T(8,128)(2,1)}, bf16[256,768]{1,0:T(8,128)(2,1)}, bf16[256,768]{1,0:T(8,128)(2,1)}, bf16[768,2...) custom-call(bf16[384,1024]{1,0:T(8,128)(2,1)} %bitcast.28, bf16[384,1024]{1,0:T(8,128)(2,1)} %copy-done.2, ...), custom_call_target="tpu_custom_call" | custom-call | flops 1 | bytes 1 | tf_op jit(solution)/shard_map/project/pallas_call | solution.py:94
  15.0 6.0 %collective-permute-done.1.refs_0_.refs_2_ = bf16[384,1024]{1,0:T(8,128)(2,1)} collective-permute-done((bf16[384,1024]{1,0:T(8,128)(2,1)}, bf16[384,1024]{1,0:T(8,128)(2,1)}, u32[]{:S(2)}, u32[]{:S(2)}) %collective-permute-start.1) | collective-permute-done | bytes 786464 | tf_op jit(solution)/shard_map/ppermute | solution.py:27
  24.5 15.8 %own_half.1 = (bf16[256,768]{1,0:T(8,128)(2,1)}, bf16[256,1536]{1,0:T(8,128)(2,1)}, bf16[256,1536]{1,0:T(8,128)(2,1)}, bf16[1536,256]{1,0:T(8,128)(2,1)}, bf16[1...) custom-call(s32[12]{0:T(128)} %fusion.12.place_of, ...), custom_call_target="tpu_custom_call" | custom-call | flops 1 | bytes 1 | tf_op jit(solution)/shard_map/own_half/pallas_call | solution.py:240
  41.8 1.9 %collective-permute-done.5.refs_7_ = bf16[384,1024]{1,0:T(8,128)(2,1)S(1)} collective-permute-done((bf16[384,1024]{1,0:T(8,128)(2,1)}, bf16[384,1024]{1,0:T(8,128)(2,1)S(1)}, u32[]{:S(2)}, u32[]{:S(2)}) %collective-permute-start.5) | collective-permute-done | bytes 786464 | tf_op jit(solution)/shard_map/ppermute | solution.py:27
  44.5 12.5 %later_half.2 = (bf16[384,768]{1,0:T(8,128)(2,1)}, bf16[384,768]{1,0:T(8,128)(2,1)}, bf16[256,512]{1,0:T(8,128)(2,1)}, bf16[256,512]{1,0:T(8,128)(2,1)}, f32[256,512]{1,0:T(8,128)}, /*index=5*/f32[256,512]{1,0:T(8,128)}) custom-call(s32[12]{0:T(128)} %fusion.12.place_of, s32[192]{0:T(256)} %reshape_squeeze.2.offsets, s32[8]{0:T(128)} %stack.38.col_order, ...), custom_call_target="tpu_custom_call" | custom-call | flops 1 | bytes 1 | tf_op jit(solution)/shard_map/later_half/pallas_call | solution.py:402
  57.0 1.9 %pad_maximum_fusion = bf16[512,512]{1,0:T(8,128)(2,1)} fusion(bf16[256,512]{1,0:T(8,128)(2,1)} %get-tuple-element.100, bf16[256,512]{1,0:T(8,128)(2,1)} %get-tuple-element.99), kind=kLoop, calls=%fused_computation.8 | loop fusion | flops 1048576 | bytes 1048576 | tf_op jit(solution)/shard_map/concatenate | solution.py:552
  58.9 1.5 %collective-permute-start.9 = (bf16[512,512]{1,0:T(8,128)(2,1)}, bf16[512,512]{1,0:T(8,128)(2,1)S(1)}, u32[]{:S(2)}, u32[]{:S(2)}) collective-permute-start(bf16[512,512]{1,0:T(8,128)(2,1)} %pad_maximum_fusion), channel_id=1, source_target_pairs={{0,1},{1,0},{2,3},{3,2},{4,5},{5,4},{6,7},{7,6},{8,9},{9,8},{10,11... | collective-permute-start | bytes 1572872 | tf_op jit(solution)/shard_map/ppermute | solution.py:27
  60.4 12.8 %later_half.3 = (bf16[384,768]{1,0:T(8,128)(2,1)}, bf16[384,768]{1,0:T(8,128)(2,1)}, bf16[256,512]{1,0:T(8,128)(2,1)}, bf16[256,512]{1,0:T(8,128)(2,1)}, f32[256,512]{1,0:T(8,128)}, /*index=5*/f32[256,512]{1,0:T(8,128)}) custom-call(s32[12]{0:T(128)} %fusion.12.place_of, s32[192]{0:T(256)} %reshape_squeeze.2.offsets, s32[8]{0:T(128)} %stack.38.col_order, ...), custom_call_target="tpu_custom_call" | custom-call | flops 1 | bytes 1 | tf_op jit(solution)/shard_map/later_half/pallas_call | solution.py:402
  75.7 1.6 %collective-permute-start.10 = (bf16[512,256]{1,0:T(8,128)(2,1)S(1)}, bf16[512,256]{1,0:T(8,128)(2,1)S(1)}, u32[]{:S(2)}, u32[]{:S(2)}) collective-permute-start(bf16[512,256]{1,0:T(8,128)(2,1)S(1)} %pad_maximum_fusion.2), channel_id=1, source_target_pairs={{0,2},{1,3},{2,0},{3,1},{4,6},{5,7},{6,4},{7,5},{8,10},{9,11},{10,... | collective-permute-start | bytes 786440 | tf_op jit(solution)/shard_map/ppermute | solution.py:27
  80.9 1.3 %collective-permute-done.12 = bf16[256,512]{1,0:T(8,128)(2,1)S(1)} collective-permute-done((bf16[256,512]{1,0:T(8,128)(2,1)}, bf16[256,512]{1,0:T(8,128)(2,1)S(1)}, u32[]{:S(2)}, u32[]{:S(2)}) %collective-permute-start.12) | collective-permute-done | bytes 262176 | tf_op jit(solution)/shard_map/ppermute | solution.py:27
  82.4 1.6 %collective-permute-start.13 = (bf16[256,256]{1,0:T(8,128)(2,1)S(1)}, bf16[256,256]{1,0:T(8,128)(2,1)S(1)}, u32[]{:S(2)}, u32[]{:S(2)}) collective-permute-start(bf16[256,256]{1,0:T(8,128)(2,1)S(1)} %pad_maximum_fusion.4), channel_id=1, source_target_pairs={{0,2},{1,3},{2,0},{3,1},{4,6},{5,7},{6,4},{7,5},{8,10},{9,11},{10,... | collective-permute-start | bytes 393224 | tf_op jit(solution)/shard_map/ppermute | solution.py:27
  84.0 2.0 %convolution_add_fusion.refs_0_ = f32[384,1024]{1,0:T(8,128)} fusion(f32[384,1024]{1,0:T(8,128)S(1)} %fusion.3, bf16[768,1024]{1,0:T(8,128)(2,1)S(1)} %copy-done, bf16[768,768]{1,0:T(8,128)(2,1)S(1)} %constant_dynamic-update-slice_fusion), kind=kOutput, calls=%fused_computation.1 | convolution fusion | flops 604372992 | bytes 5308416 | tf_op jit(solution)/shard_map/dot_general | solution.py:22
  87.5 2.6 %collective-permute-start.11 = (bf16[512,128]{1,0:T(8,128)(2,1)S(1)}, bf16[512,128]{1,0:T(8,128)(2,1)S(1)}, u32[]{:S(2)}, u32[]{:S(2)}) collective-permute-start(bf16[512,128]{1,0:T(8,128)(2,1)S(1)} %fusion.7), channel_id=1, source_target_pairs={{0,4},{1,5},{2,6},{3,7},{4,0},{5,1},{6,2},{7,3},{8,12},{9,13},{10,... | collective-permute-start | bytes 393224 | tf_op jit(solution)/shard_map/ppermute | solution.py:27
  90.1 3.1 %collective-permute-done.14 = bf16[256,512]{1,0:T(8,128)(2,1)S(1)} collective-permute-done((bf16[256,512]{1,0:T(8,128)(2,1)S(1)}, bf16[256,512]{1,0:T(8,128)(2,1)S(1)}, u32[]{:S(2)}, u32[]{:S(2)}) %collective-permute-start.14) | collective-permute-done | bytes 262176 | tf_op jit(solution)/shard_map/ppermute | solution.py:27
  93.3 2.6 %collective-permute-start.15 = (bf16[256,128]{1,0:T(8,128)(2,1)S(1)}, bf16[256,128]{1,0:T(8,128)(2,1)S(1)}, u32[]{:S(2)}, u32[]{:S(2)}) collective-permute-start(bf16[256,128]{1,0:T(8,128)(2,1)S(1)} %add_convert_fusion.4), channel_id=1, source_target_pairs={{0,4},{1,5},{2,6},{3,7},{4,0},{5,1},{6,2},{7,3},{8,12},{9,13},{10,... | collective-permute-start | bytes 196616 | tf_op jit(solution)/shard_map/ppermute | solution.py:27
  96.4 2.7 %collective-permute-done.15 = bf16[256,128]{1,0:T(8,128)(2,1)S(1)} collective-permute-done((bf16[256,128]{1,0:T(8,128)(2,1)S(1)}, bf16[256,128]{1,0:T(8,128)(2,1)S(1)}, u32[]{:S(2)}, u32[]{:S(2)}) %collective-permute-start.15) | collective-permute-done | bytes 65568 | tf_op jit(solution)/shard_map/ppermute | solution.py:27
  99.2 1.8 %collective-permute-done.18 = bf16[256,256]{1,0:T(8,128)(2,1)S(1)} collective-permute-done((bf16[256,256]{1,0:T(8,128)(2,1)S(1)}, bf16[256,256]{1,0:T(8,128)(2,1)S(1)}, u32[]{:S(2)}, u32[]{:S(2)}) %collective-permute-start.18) | collective-permute-done | bytes 131104 | tf_op jit(solution)/shard_map/ppermute | solution.py:27
  101.4 5.5 %collective-permute-done.19 = bf16[256,128]{1,0:T(8,128)(2,1)S(1)} collective-permute-done((bf16[256,128]{1,0:T(8,128)(2,1)S(1)}, bf16[256,128]{1,0:T(8,128)(2,1)S(1)}, u32[]{:S(2)}, u32[]{:S(2)}) %collective-permute-start.19) | collective-permute-done | bytes 65568 | tf_op jit(solution)/shard_map/ppermute | solution.py:27
  107.0 1.9 %collective-permute-start.16 = (f32[128,128]{1,0:T(8,128)S(1)}, f32[128,128]{1,0:T(8,128)S(1)}, u32[]{:S(2)}, u32[]{:S(2)}) collective-permute-start(f32[128,128]{1,0:T(8,128)S(1)} %get-tuple-element.117), channel_id=1, source_target_pairs={{0,0},{8,2},{16,4},{24,6},{1,1},{9,3},{17,5},{25,7},{2,8},{10,10},... | collective-permute-start | bytes 196616 | tf_op jit(solution)/shard_map/ppermute | solution.py:479
  108.9 3.8 %collective-permute-start.17 = (f32[128,128]{1,0:T(8,128)S(1)}, f32[128,128]{1,0:T(8,128)S(1)}, u32[]{:S(2)}, u32[]{:S(2)}) collective-permute-start(f32[128,128]{1,0:T(8,128)S(1)} %get-tuple-element.116), channel_id=1, source_target_pairs={{0,1},{8,3},{16,5},{24,7},{1,0},{9,2},{17,4},{25,6},{2,9},{10,11},... | collective-permute-start | bytes 196616 | tf_op jit(solution)/shard_map/ppermute | solution.py:479
  112.8 2.6 %finish.1 = bf16[384,1024]{1,0:T(8,128)(2,1)} custom-call(f32[384,1024]{1,0:T(8,128)} %convolution_add_fusion.refs_0_, bf16[384,1024]{1,0:T(8,128)(2,1)} %copy-done.6), custom_call_target="tpu_custom_call" | custom-call | flops 1 | bytes 70000000 | tf_op jit(solution)/shard_map/finish/pallas_call | solution.py:438
  (92 shorter events, 18.3 us)
Async XLA Ops:
  0.6 7.6 %collective-permute-start = (bf16[384,1024]{1,0:T(8,128)(2,1)}, bf16[384,1024]{1,0:T(8,128)(2,1)S(1)}, u32[]{:S(2)}, u32[]{:S(2)}) collective-permute-start(bf16[384,1024]{1,0:T(8,128)(2,1)} %bitcast.26), channel_id=1, source_target_pairs={{0,8},{8,0},{16,24},{24,16},{1,9},{9,1},{17,25},{25,17},{2,10},{10... | collective-permute-start | bytes 2359304 | tf_op jit(solution)/shard_map/ppermute | solution.py:27
  0.7 7.5 %collective-permute-start.2 = (bf16[384,1024]{1,0:T(8,128)(2,1)}, bf16[384,1024]{1,0:T(8,128)(2,1)}, u32[]{:S(2)}, u32[]{:S(2)}) collective-permute-start(bf16[384,1024]{1,0:T(8,128)(2,1)} %bitcast.31), channel_id=1, source_target_pairs={{0,8},{8,0},{16,24},{24,16},{1,9},{9,1},{17,25},{25,17},{2,10},{10... | collective-permute-start | bytes 2359304 | tf_op jit(solution)/shard_map/ppermute | solution.py:27
  1.2 19.8 %collective-permute-start.1 = (bf16[384,1024]{1,0:T(8,128)(2,1)}, bf16[384,1024]{1,0:T(8,128)(2,1)}, u32[]{:S(2)}, u32[]{:S(2)}) collective-permute-start(bf16[384,1024]{1,0:T(8,128)(2,1)} %bitcast.27), channel_id=1, source_target_pairs={{0,16},{8,24},{16,0},{24,8},{1,17},{9,25},{17,1},{25,9},{2,18},{10... | collective-permute-start | bytes 2359304 | tf_op jit(solution)/shard_map/ppermute | solution.py:27
  8.2 12.8 %copy-start.1 = (bf16[1,384,1024]{2,1,0:T(8,128)(2,1)S(1)}, bf16[1,384,1024]{2,1,0:T(8,128)(2,1)}, u32[]{:S(2)}) copy-start(bf16[1,384,1024]{2,1,0:T(8,128)(2,1)} %param.8) | copy-start | bytes 2359300
  8.2 13.1 %copy-start.12 = (s32[1,4,12,4]{2,3,1,0:T(4,128)S(1)}, s32[1,4,12,4]{2,3,1,0:T(4,128)}, u32[]{:S(2)}) copy-start(s32[1,4,12,4]{2,3,1,0:T(4,128)} %param.9) | copy-start | bytes 2308
  21.0 2.5 %collective-permute-start.3 = (bf16[384,1024]{1,0:T(8,128)(2,1)}, bf16[384,1024]{1,0:T(8,128)(2,1)S(1)}, u32[]{:S(2)}, u32[]{:S(2)}) collective-permute-start(bf16[384,1024]{1,0:T(8,128)(2,1)} %collective-permute-done.1.refs_0_.refs_2_), channel_id=1, source_target_pairs={{0,8},{8,0},{16,24},{24,16},{1,9},{9,1},{17,25},{25,17},{2,10},{10... | collective-permute-start | bytes 2359304 | tf_op jit(solution)/shard_map/ppermute | solution.py:27
  21.1 20.1 %collective-permute-start.4 = (bf16[384,1024]{1,0:T(8,128)(2,1)S(1)}, bf16[384,1024]{1,0:T(8,128)(2,1)}, u32[]{:S(2)}, u32[]{:S(2)}) collective-permute-start(bf16[384,1024]{1,0:T(8,128)(2,1)S(1)} %bitcast.35), channel_id=1, source_target_pairs={{0,16},{8,24},{16,0},{24,8},{1,17},{9,25},{17,1},{25,9},{2,18},{10... | collective-permute-start | bytes 2359304 | tf_op jit(solution)/shard_map/ppermute | solution.py:27
  41.1 2.5 %collective-permute-start.5 = (bf16[384,1024]{1,0:T(8,128)(2,1)}, bf16[384,1024]{1,0:T(8,128)(2,1)S(1)}, u32[]{:S(2)}, u32[]{:S(2)}) collective-permute-start(bf16[384,1024]{1,0:T(8,128)(2,1)} %collective-permute-done.4.refs_6_), channel_id=1, source_target_pairs={{0,8},{8,0},{16,24},{24,16},{1,9},{9,1},{17,25},{25,17},{2,10},{10... | collective-permute-start | bytes 2359304 | tf_op jit(solution)/shard_map/ppermute | solution.py:27
  58.9 16.6 %collective-permute-start.9 = (bf16[512,512]{1,0:T(8,128)(2,1)}, bf16[512,512]{1,0:T(8,128)(2,1)S(1)}, u32[]{:S(2)}, u32[]{:S(2)}) collective-permute-start(bf16[512,512]{1,0:T(8,128)(2,1)} %pad_maximum_fusion), channel_id=1, source_target_pairs={{0,1},{1,0},{2,3},{3,2},{4,5},{5,4},{6,7},{7,6},{8,9},{9,8},{10,11... | collective-permute-start | bytes 1572872 | tf_op jit(solution)/shard_map/ppermute | solution.py:27
  60.4 15.0 %copy-start.7 = (bf16[384,768]{1,0:T(8,128)(2,1)S(1)}, bf16[384,768]{1,0:T(8,128)(2,1)}, u32[]{:S(2)}) copy-start(bf16[384,768]{1,0:T(8,128)(2,1)} %get-tuple-element.89) | copy-start | bytes 1769476
  60.4 16.9 %collective-permute-start.6 = (bf16[384,768]{1,0:T(8,128)(2,1)}, bf16[384,768]{1,0:T(8,128)(2,1)S(1)}, u32[]{:S(2)}, u32[]{:S(2)}) collective-permute-start(bf16[384,768]{1,0:T(8,128)(2,1)} %get-tuple-element.92), channel_id=1, source_target_pairs={{0,8},{8,0},{16,24},{24,16},{1,9},{9,1},{17,25},{25,17},{2,10},{10... | collective-permute-start | bytes 1769480 | tf_op jit(solution)/shard_map/ppermute | solution.py:27
  73.3 4.0 %collective-permute-start.7 = (bf16[384,768]{1,0:T(8,128)(2,1)}, bf16[384,768]{1,0:T(8,128)(2,1)S(1)}, u32[]{:S(2)}, u32[]{:S(2)}) collective-permute-start(bf16[384,768]{1,0:T(8,128)(2,1)} %get-tuple-element.93), channel_id=1, source_target_pairs={{0,8},{8,0},{16,24},{24,16},{1,9},{9,1},{17,25},{25,17},{2,10},{10... | collective-permute-start | bytes 1769480 | tf_op jit(solution)/shard_map/ppermute | solution.py:27
  73.7 8.6 %collective-permute-start.12 = (bf16[256,512]{1,0:T(8,128)(2,1)}, bf16[256,512]{1,0:T(8,128)(2,1)S(1)}, u32[]{:S(2)}, u32[]{:S(2)}) collective-permute-start(bf16[256,512]{1,0:T(8,128)(2,1)} %get-tuple-element.102), channel_id=1, source_target_pairs={{0,1},{1,0},{2,3},{3,2},{4,5},{5,4},{6,7},{7,6},{8,9},{9,8},{10,11... | collective-permute-start | bytes 786440 | tf_op jit(solution)/shard_map/ppermute | solution.py:27
  75.7 11.8 %collective-permute-start.10 = (bf16[512,256]{1,0:T(8,128)(2,1)S(1)}, bf16[512,256]{1,0:T(8,128)(2,1)S(1)}, u32[]{:S(2)}, u32[]{:S(2)}) collective-permute-start(bf16[512,256]{1,0:T(8,128)(2,1)S(1)} %pad_maximum_fusion.2), channel_id=1, source_target_pairs={{0,2},{1,3},{2,0},{3,1},{4,6},{5,7},{6,4},{7,5},{8,10},{9,11},{10,... | collective-permute-start | bytes 786440 | tf_op jit(solution)/shard_map/ppermute | solution.py:27
  79.6 27.3 %collective-permute-start.8 = (bf16[384,1024]{1,0:T(8,128)(2,1)S(1)}, bf16[384,1024]{1,0:T(8,128)(2,1)S(1)}, u32[]{:S(2)}, u32[]{:S(2)}) collective-permute-start(bf16[384,1024]{1,0:T(8,128)(2,1)S(1)} %add_convert_fusion), channel_id=1, source_target_pairs={{0,16},{8,24},{16,0},{24,8},{1,17},{9,25},{17,1},{25,9},{2,18},{10... | collective-permute-start | bytes 2359304 | tf_op jit(solution)/shard_map/ppermute | solution.py:27
  82.3 13.5 %copy-start.9 = (f32[256,512]{1,0:T(8,128)S(1)}, f32[256,512]{1,0:T(8,128)}, u32[]{:S(2)}) copy-start(f32[256,512]{1,0:T(8,128)} %get-tuple-element.108) | copy-start | bytes 1572868
  82.4 5.0 %collective-permute-start.13 = (bf16[256,256]{1,0:T(8,128)(2,1)S(1)}, bf16[256,256]{1,0:T(8,128)(2,1)S(1)}, u32[]{:S(2)}, u32[]{:S(2)}) collective-permute-start(bf16[256,256]{1,0:T(8,128)(2,1)S(1)} %pad_maximum_fusion.4), channel_id=1, source_target_pairs={{0,2},{1,3},{2,0},{3,1},{4,6},{5,7},{6,4},{7,5},{8,10},{9,11},{10,... | collective-permute-start | bytes 393224 | tf_op jit(solution)/shard_map/ppermute | solution.py:27
  86.0 7.3 %collective-permute-start.14 = (bf16[256,512]{1,0:T(8,128)(2,1)S(1)}, bf16[256,512]{1,0:T(8,128)(2,1)S(1)}, u32[]{:S(2)}, u32[]{:S(2)}) collective-permute-start(bf16[256,512]{1,0:T(8,128)(2,1)S(1)} %copy-done.13), channel_id=1, source_target_pairs={{0,1},{1,0},{2,3},{3,2},{4,5},{5,4},{6,7},{7,6},{8,9},{9,8},{10,11... | collective-permute-start | bytes 786440 | tf_op jit(solution)/shard_map/ppermute | solution.py:27
  87.5 11.6 %collective-permute-start.11 = (bf16[512,128]{1,0:T(8,128)(2,1)S(1)}, bf16[512,128]{1,0:T(8,128)(2,1)S(1)}, u32[]{:S(2)}, u32[]{:S(2)}) collective-permute-start(bf16[512,128]{1,0:T(8,128)(2,1)S(1)} %fusion.7), channel_id=1, source_target_pairs={{0,4},{1,5},{2,6},{3,7},{4,0},{5,1},{6,2},{7,3},{8,12},{9,13},{10,... | collective-permute-start | bytes 393224 | tf_op jit(solution)/shard_map/ppermute | solution.py:27
  93.3 5.8 %collective-permute-start.15 = (bf16[256,128]{1,0:T(8,128)(2,1)S(1)}, bf16[256,128]{1,0:T(8,128)(2,1)S(1)}, u32[]{:S(2)}, u32[]{:S(2)}) collective-permute-start(bf16[256,128]{1,0:T(8,128)(2,1)S(1)} %add_convert_fusion.4), channel_id=1, source_target_pairs={{0,4},{1,5},{2,6},{3,7},{4,0},{5,1},{6,2},{7,3},{8,12},{9,13},{10,... | collective-permute-start | bytes 196616 | tf_op jit(solution)/shard_map/ppermute | solution.py:27
  95.9 5.0 %collective-permute-start.18 = (bf16[256,256]{1,0:T(8,128)(2,1)S(1)}, bf16[256,256]{1,0:T(8,128)(2,1)S(1)}, u32[]{:S(2)}, u32[]{:S(2)}) collective-permute-start(bf16[256,256]{1,0:T(8,128)(2,1)S(1)} %pad_maximum_fusion.6), channel_id=1, source_target_pairs={{0,2},{1,3},{2,0},{3,1},{4,6},{5,7},{6,4},{7,5},{8,10},{9,11},{10,... | collective-permute-start | bytes 393224 | tf_op jit(solution)/shard_map/ppermute | solution.py:27
  101.0 5.9 %collective-permute-start.19 = (bf16[256,128]{1,0:T(8,128)(2,1)S(1)}, bf16[256,128]{1,0:T(8,128)(2,1)S(1)}, u32[]{:S(2)}, u32[]{:S(2)}) collective-permute-start(bf16[256,128]{1,0:T(8,128)(2,1)S(1)} %add_convert_fusion.1), channel_id=1, source_target_pairs={{0,4},{1,5},{2,6},{3,7},{4,0},{5,1},{6,2},{7,3},{8,12},{9,13},{10,... | collective-permute-start | bytes 196616 | tf_op jit(solution)/shard_map/ppermute | solution.py:27
  107.0 8.4 %collective-permute-start.16 = (f32[128,128]{1,0:T(8,128)S(1)}, f32[128,128]{1,0:T(8,128)S(1)}, u32[]{:S(2)}, u32[]{:S(2)}) collective-permute-start(f32[128,128]{1,0:T(8,128)S(1)} %get-tuple-element.117), channel_id=1, source_target_pairs={{0,0},{8,2},{16,4},{24,6},{1,1},{9,3},{17,5},{25,7},{2,8},{10,10},... | collective-permute-start | bytes 196616 | tf_op jit(solution)/shard_map/ppermute | solution.py:479
  108.9 7.4 %collective-permute-start.17 = (f32[128,128]{1,0:T(8,128)S(1)}, f32[128,128]{1,0:T(8,128)S(1)}, u32[]{:S(2)}, u32[]{:S(2)}) collective-permute-start(f32[128,128]{1,0:T(8,128)S(1)} %get-tuple-element.116), channel_id=1, source_target_pairs={{0,1},{8,3},{16,5},{24,7},{1,0},{9,2},{17,4},{25,6},{2,9},{10,11},... | collective-permute-start | bytes 196616 | tf_op jit(solution)/shard_map/ppermute | solution.py:479
  (10 other events, 21.5 us)

commit v3 on v1

v3 whole, which is shorter than its diff:
```python
import functools
import math

import jax
import jax.numpy as jnp
from jax import lax
from jax.experimental import pallas as pl
from jax.experimental.pallas import tpu as pltpu
from jax.sharding import PartitionSpec as P

BLK = 128
BF = jnp.bfloat16
F32 = jnp.float32
LAST_LAST = (((1,), (1,)), ((), ()))
VMEM_BYTES = 66584576
LIGHT = pl.CostEstimate(flops=1, bytes_accessed=1, transcendentals=0)


def dot(left_side, right_side, dims):
    return lax.dot_general(left_side, right_side, dims, preferred_element_type=F32)


def swap(value, axis, distance):
    count = lax.axis_size(axis)
    return lax.ppermute(value, axis, [(at, at ^ distance) for at in range(count)])


def spread(shard, axis, count):
    pieces = {0: shard}
    bit = count // 2
    while bit:
        for place in sorted(pieces):
            pieces[place | bit] = swap(pieces[place], axis, bit)
        bit //= 2
    return [pieces[place] for place in sorted(pieces)]


def side_by_side(parts):
    return parts[0] if len(parts) == 1 else jnp.concatenate(parts, axis=1)


class Held:
    def __init__(self, source, target, arrived):
        self.target, self.copy, self.there = target, None, False
        self.copy = pltpu.make_async_copy(source, target, arrived)
        self.copy.start()

    def __call__(self):
        if not self.there:
            self.copy.wait()
            self.there = True
        return self.target


class Sent:
    def __init__(self, outs, held, left):
        self.outs, self.held, self.left, self.copies = outs, held, left, []

    def __getitem__(self, at):
        return self.held[at]

    def start(self, at, part=None):
        source, target = self.held[at], self.outs[at]
        if part is not None:
            source, target = source.at[part], target.at[part]
        copy = pltpu.make_async_copy(source, target, self.left.at[len(self.copies)])
        copy.start()
        self.copies.append(copy)

    def finish(self):
        for copy in self.copies:
            copy.wait()


def part_shape(shape, part):
    if part is None:
        return shape
    kept = []
    for size, index in zip(shape, part):
        if isinstance(index, slice):
            kept.append(len(range(*index.indices(size))))
        elif not isinstance(index, int):
            kept.append(index.size)
    return tuple(kept)


def run(body, name, scalars, operands, results, scratch, most_copies):
    arrays = [array for array, _ in operands]
    taken = [
        part_shape(array.shape, part([None] * 99, 0) if callable(part) else part)
        for array, part in operands
    ]
    n, k, m = len(scalars), len(arrays), len(results)

    def kernel(*refs):
        given, sources, outs = refs[:n], refs[n : n + k], refs[n + k : n + k + m]
        refs = refs[n + k + m :]
        targets, held, own, (arrived, left) = refs[:k], refs[k : k + m], refs[k + m : -2], refs[-2:]
        ready = []
        for at, (source, (_, part)) in enumerate(zip(sources, operands)):
            if callable(part):
                part = part(given, None)
            source = source if part is None else source.at[part]
            ready.append(Held(source, targets[at], arrived.at[at]))
        sent = Sent(outs, held, left)
        body(given, ready, sent, *own)
        sent.finish()

    return pl.pallas_call(
        kernel,
        in_specs=[pl.BlockSpec(memory_space=pltpu.SMEM)] * n + [pl.BlockSpec(memory_space=pl.ANY)] * k,
        out_specs=[pl.BlockSpec(memory_space=pl.ANY)] * m,
        out_shape=[jax.ShapeDtypeStruct(*result) for result in results],
        scratch_shapes=[pltpu.VMEM(shape, array.dtype) for shape, array in zip(taken, arrays)]
        + [pltpu.VMEM(*result) for result in results]
        + scratch
        + [pltpu.SemaphoreType.DMA((k,)), pltpu.SemaphoreType.DMA((most_copies,))],
        compiler_params=pltpu.CompilerParams(vmem_limit_bytes=VMEM_BYTES),
        cost_estimate=LIGHT,
        name=name,
    )(*scalars, *arrays)


def whole(arrays):
    return [(array, None) for array in arrays]


def weight_rows(seq_index, head_width, weights):
    width, count = weights[0].shape[0], len(weights)
    pairs = head_width // BLK
    first = jnp.reshape(seq_index * head_width, (1,)).astype(jnp.int32)

    def cols(scalars, dry):
        start = 0 if dry is not None else pl.multiple_of(scalars[0][0], BLK)
        return (slice(0, width), pl.ds(start, head_width))

    def body(_, ready, sent):
        rows = sent[0]
        for at in range(count):
            taken = ready[at]()
            for pair in range(pairs):
                base = (pair * count + at) * BLK
                rows[base : base + BLK, :] = taken[:, pair * BLK : (pair + 1) * BLK].T
        sent.start(0)

    operands = [(weight, cols) for weight in weights]
    return run(body, "weight_rows", [first], operands, [((count * head_width, width), BF)], [], 1)[0]


def out_rows_part(blocks, more, height, model):
    def part(scalars, dry):
        start = 0 if dry is not None else pl.multiple_of(scalars[0][blocks] + more, BLK)
        return (pl.ds(start, height), slice(0, model))

    return part


def project(plan, blocks, tokens, grads, rows, out_weight, scale):
    count, (step, model) = len(tokens), tokens[0].shape
    width = rows.shape[0] // 3
    pairs = width // BLK
    across, down = ((width, count * step), BF), ((count * step, width), BF)

    def body(_, ready, sent):
        rows, out_rows, far_rows = ready[0], ready[1], ready[2 : 2 + count]
        tokens_here, grads_here = ready[2 + count : 2 + 2 * count], ready[2 + 2 * count :]
        queries_t, out_grads_t, keys_t, values_t, keys, values = (sent[at] for at in range(6))
        own_grads = grads_here[0]()[...]
        for at in range(count):
            sent[6 + at][...] = dot(far_rows[at]()[...], own_grads, LAST_LAST).astype(BF)
            sent.start(6 + at)
        for at in range(2):
            sent[6 + count + at][...] = own_grads[at * step // 2 : (at + 1) * step // 2]
            sent.start(6 + count + at)
        for at in range(count):
            span = slice(at * step, (at + 1) * step)
            heads_t = dot(rows()[...], tokens_here[at]()[...], LAST_LAST)
            for pair in range(pairs):
                own = slice(pair * BLK, (pair + 1) * BLK)
                base = pair * 3 * BLK
                queries_t[own, span] = heads_t[base : base + BLK].astype(BF) * scale
                key_part = heads_t[base + BLK : base + 2 * BLK]
                value_part = heads_t[base + 2 * BLK : base + 3 * BLK]
                keys_t[own, span] = key_part.astype(BF)
                values_t[own, span] = value_part.astype(BF)
                keys[span, own] = key_part.T.astype(BF)
                values[span, own] = value_part.T.astype(BF)
        for at in (0, 2, 3, 4, 5):
            sent.start(at)
        for at in range(count):
            span = slice(at * step, (at + 1) * step)
            out_grads_t[:, span] = dot(out_rows()[...], grads_here[at]()[...], LAST_LAST).astype(BF)
        sent.start(1)

    operands = [(rows, None), (out_weight, out_rows_part(blocks, 0, width, model))]
    operands += [
        (out_weight, out_rows_part(blocks + 1 + at, 0, width, model)) for at in range(count)
    ]
    operands += whole(tokens) + whole(grads)
    results = [across] * 4 + [down] * 2 + [((width, step), BF)] * count
    results += [((step // 2, model), BF)] * 2
    return run(body, "project", [plan], operands, results, [], 8 + count)


def attend(
    place_of, offsets, head_base, places, queries_t, out_grads_t, key_refs, sums, put, slots, blocks, head_size
):
    keys_t, values_t, keys, values = key_refs
    key_acc, value_acc = sums
    key_at = lax.broadcasted_iota(jnp.int32, (BLK, BLK), 0)
    query_at = lax.broadcasted_iota(jnp.int32, (BLK, BLK), 1)
    causal = key_at <= query_at
    first_head = lax.broadcasted_iota(jnp.int32, (2 * head_size, BLK), 0) < head_size
    plus = functools.partial(functools.reduce, jnp.add)
    cut = [slice(slot * BLK, (slot + 1) * BLK) for slot in range(slots)]

    for step in range(queries_t.shape[1] // BLK):
        place = places + step
        block = place_of[place]
        cols = slice(step * BLK, (step + 1) * BLK)
        pair_queries = queries_t[:, cols]
        pair_grads = out_grads_t[:, cols]
        scored = []
        for half in range(2):
            head = head_base + half
            rows = slice(half * head_size, (half + 1) * head_size)
            keep = first_head if half == 0 else ~first_head
            head_queries = jnp.where(keep, pair_queries, jnp.zeros_like(pair_queries))
            head_grads = jnp.where(keep, pair_grads, jnp.zeros_like(pair_grads))
            named, usable = [], []
            for slot in range(slots):
                offset = offsets[(head * blocks + block) * slots + slot]
                usable.append(offset <= block)
                named.append(place_of[jnp.where(offset <= block, block - offset, 0)])
            spans = [pl.ds(pl.multiple_of(at * BLK, BLK), BLK) for at in named]
            seen_keys = jnp.concatenate([keys[span, :] for span in spans], axis=0)
            seen_values = jnp.concatenate([values[span, :] for span in spans], axis=0)
            scores = jnp.dot(seen_keys, head_queries, preferred_element_type=F32)
            prob_grad = jnp.dot(seen_values, head_grads, preferred_element_type=F32)
            scores = [
                jnp.where(causal if slot == 0 else usable[slot], scores[cut[slot]], -jnp.inf)
                for slot in range(slots)
            ]
            scored.append((rows, named, spans, scores, [prob_grad[part] for part in cut]))
        parts = []
        for rows, named, spans, scores, prob_grad in scored:
            top = jnp.max(functools.reduce(jnp.maximum, scores), axis=0, keepdims=True)
            raised = [jnp.exp(part - top) for part in scores]
            total = jnp.sum(plus(raised), axis=0, keepdims=True)
            inverse = 1.0 / total
            probs = [part * inverse for part in raised]
            probs_half = jnp.concatenate([part.astype(BF) for part in probs], axis=0)
            delta = jnp.sum(
                plus([part * grad for part, grad in zip(probs, prob_grad)]), axis=0, keepdims=True
            )
            score_grad = jnp.concatenate(
                [(part * (grad - delta)).astype(BF) for part, grad in zip(probs, prob_grad)], axis=0
            )
            seen_values_t = side_by_side([values_t[rows, span] for span in spans])
            seen_keys_t = side_by_side([keys_t[rows, span] for span in spans])
            attended = jnp.dot(seen_values_t, probs_half, preferred_element_type=F32)
            query_grad = jnp.dot(seen_keys_t, score_grad, preferred_element_type=F32)
            put(rows, cols, attended, query_grad * (1.0 / math.sqrt(head_size)))
            value_part = dot(out_grads_t[rows, cols], probs_half, LAST_LAST)
            key_part = dot(queries_t[rows, cols], score_grad, LAST_LAST)
            parts.append((rows, named, key_part, value_part))
        for rows, named, key_part, value_part in parts:
            for at, part in zip(named, cut):
                key_acc[at, rows, :] += key_part[:, part]
                value_acc[at, rows, :] += value_part[:, part]


def own_half(plan, offsets, tokens, rows, projected):
    width, half = projected[0].shape
    heads, blocks, slots = offsets.shape
    head_size, pairs, total, count = width // heads, width // BLK, blocks * BLK, len(tokens)
    half_across, across, down = ((width, half), BF), ((width, total), BF), ((total, width), BF)
    sums = ((pairs, blocks, BLK, BLK), F32)
    scale = 1.0 / math.sqrt(head_size)

    def body(scalars, ready, sent):
        rows, tokens_here = ready[0], ready[1 : 1 + count]
        queries_t, out_grads_t, keys_in, values_in, keys_down, values_down = ready[1 + count :]
        later_queries_t, keys_t, values_t, keys, values = (sent[at] for at in range(5))
        attended_t, query_grad_t, key_acc, value_acc = (sent[at] for at in range(5, 9))
        key_acc[...] = jnp.zeros(key_acc.shape, F32)
        value_acc[...] = jnp.zeros(value_acc.shape, F32)
        step = tokens[0].shape[0]
        for at in range(count):
            span = slice(at * step, (at + 1) * step)
            placed = slice(half + at * step, half + (at + 1) * step)
            for pair in range(pairs):
                own = slice(pair * BLK, (pair + 1) * BLK)
                pair_rows = rows()[pair * 3 * BLK : (pair + 1) * 3 * BLK, :]
                heads_t = dot(pair_rows, tokens_here[at]()[...], LAST_LAST)
                later_queries_t[own, span] = heads_t[:BLK].astype(BF) * scale
                keys_t[own, placed] = heads_t[BLK : 2 * BLK].astype(BF)
                values_t[own, placed] = heads_t[2 * BLK :].astype(BF)
                keys[placed, own] = heads_t[BLK : 2 * BLK].T.astype(BF)
                values[placed, own] = heads_t[2 * BLK :].T.astype(BF)
        keys_t[:, :half] = keys_in()[...]
        values_t[:, :half] = values_in()[...]
        keys[:half, :] = keys_down()[...]
        values[:half, :] = values_down()[...]
        for at in range(5):
            sent.start(at)

        for pair in range(pairs):
            own = slice(pair * BLK, (pair + 1) * BLK)

            def put(at_rows, cols, attended, query_grad):
                placed = slice(own.start + at_rows.start, own.start + at_rows.stop)
                attended_t[placed, cols] = attended.astype(BF)
                query_grad_t[placed, cols] = query_grad.astype(BF)

            attend(
                scalars[0],
                scalars[1],
                2 * pair,
                0,
                queries_t().at[own, :],
                out_grads_t().at[own, :],
                (keys_t.at[own, :], values_t.at[own, :], keys.at[:, own], values.at[:, own]),
                (key_acc.at[pair], value_acc.at[pair]),
                put,
                slots,
                blocks,
                head_size,
            )
            for at in (5, 6):
                sent.start(at, (own, slice(0, half)))
            for at in (7, 8):
                sent.start(at, (pair,))

    results = [half_across, across, across, down, down, half_across, half_across, sums, sums]
    operands = whole([rows, *tokens, *projected])
    return run(
        body, "own_half", [plan, offsets.reshape(-1)], operands, results, [], 5 + 4 * pairs
    )


def later_half(
    plan, offsets, order_at, far_grads_t, pair, first, tokens, grads, attended, before, rows, mate_rows
):
    width, half = first[0].shape
    heads, blocks, slots = offsets.shape
    head_size, total = width // heads, blocks * BLK
    near, step = len(far_grads_t), far_grads_t[0].shape[1]
    model, count = tokens[0].shape[1], len(tokens)
    own = slice(pair * BLK, (pair + 1) * BLK)
    across, half_across, down = (own, slice(0, total)), (own, slice(0, half)), (slice(0, total), own)
    last, final = bool(grads), rows is not None

    def body(scalars, ready, sent, out_grads_t, stay, leave):
        plan = scalars[0]
        queries_t, keys_t, values_t, keys, values, key_acc, value_acc = (
            part() for part in ready[near : near + 7]
        )
        query_grad_first = ready[near + 7]
        tokens_here = ready[near + 8 : near + 8 + count]
        grads_here = ready[near + 8 + count : near + 8 + count + len(grads)]
        attended_here = ready[near + 8 + count + len(grads) :]
        attended_here, shares_here = attended_here[: len(attended)], attended_here[len(attended) :]
        attended_t = sent[0]
        for at in range(near):
            out_grads_t[:, at * step : (at + 1) * step] = ready[at]()[...]

        def columns(place, at):
            left = place // 2 * step + at
            return (leave if place % 2 else stay), slice(left, left + BLK)

        def put(at_rows, cols, attended, query_grad):
            attended_t[at_rows, cols] = attended.astype(BF)
            target, placed = columns(near + cols.start // step, cols.start % step)
            target[at_rows, placed] = query_grad.astype(BF)

        attend(
            plan,
            scalars[1],
            2 * pair,
            blocks // 2,
            queries_t,
            out_grads_t,
            (keys_t, values_t, keys, values),
            (key_acc, value_acc),
            put,
            slots,
            blocks,
            head_size,
        )
        if not last:
            sent.start(0)
        for at in range(0, half, BLK):
            target, cols = columns(at // step, at % step)
            target[:BLK, cols] = query_grad_first()[:, at : at + BLK]
        for at in range(blocks):
            target, cols = columns(at * BLK // step, at * BLK % step)
            target[BLK : 2 * BLK, cols] = key_acc[at].astype(BF)
            target[2 * BLK :, cols] = value_acc[at].astype(BF)
        for at, held in ((1, stay), (2, leave)):
            for cols in range(0, half, BLK):
                sent[at][cols : cols + BLK, :] = held[:, cols : cols + BLK].T
            sent.start(at)
        if final:
            parts = [(sent[1], shares_here[-1], pair)]
            parts += [
                (shares_here[2 * at + side], shares_here[-1 - side], at)
                for at in range(len(before))
                for side in (1, 0)
            ]
            lefts = [(left() if isinstance(left, Held) else left)[step:, :] for left, _, _ in parts]
            left = jnp.concatenate(lefts, axis=1)
            model_n = rows.shape[1]
            for col in range(0, model_n, 2 * BLK):
                cols = slice(col, col + 2 * BLK)
                held = [
                    right()[at * 3 * BLK : (at + 1) * 3 * BLK, cols] for _, right, at in parts
                ]
                sent[5][:, cols] = jnp.dot(
                    left, jnp.concatenate(held, axis=0), preferred_element_type=F32
                )
            sent.start(5)

        def put_terms(at, lefts, rights):
            pieces = [[part() for part in right] for right in rights]
            for col in range(0, model, 2 * BLK):
                spans = [
                    pl.ds(pl.multiple_of(plan[order_at + col // BLK + side] * BLK, BLK), BLK)
                    for side in range(2)
                ]
                terms = 0.0
                for left, right in zip(lefts, pieces):
                    cut = [side_by_side([part[:, span] for span in spans]) for part in right]
                    terms += jnp.dot(
                        left, jnp.concatenate(cut, axis=0), preferred_element_type=F32
                    )
                target, cols = sent[at + col // (model // 2)], col % (model // 2)
                target[:, cols : cols + 2 * BLK] = terms.astype(target.dtype)
                if cols + 2 * BLK == model // 2:
                    sent.start(at + col // (model // 2))

        if last:
            lefts = [attended_here[0]()[...]]
            lefts.append(
                jnp.concatenate([part()[...] for part in attended_here[1:]] + [attended_t[...]], axis=0)
            )
            pieces = [[part() for part in grads_here[:near]], [part() for part in grads_here[near:]]]
            own_rows = plan[order_at + model // BLK + model // width]
            for at in range(model // width):
                span = pl.ds(
                    pl.multiple_of(plan[order_at + model // BLK + at] * width, width), width
                )
                terms = 0.0
                for left, right in zip(lefts, pieces):
                    taken = jnp.concatenate([part[:, span] for part in right], axis=0)
                    terms += jnp.dot(left, taken, preferred_element_type=F32)
                cols = slice(at * width, (at + 1) * width)
                sent[6][:, cols] = jnp.where(own_rows == 0, terms[BLK:], terms[:BLK]).astype(BF)
                sent[7][:, cols] = jnp.where(own_rows == 0, terms[:BLK], terms[BLK:])
            sent.start(6)
            sent.start(7)
        put_terms(3, [stay[...], leave[...]], [tokens_here[0::2], tokens_here[1::2]])

    (queries_t, keys_t, values_t, keys, values, _, query_grad_t, key_acc, value_acc) = first
    sums = (pair, slice(0, blocks), slice(0, BLK), slice(0, BLK))
    operands = [(part, (own, slice(0, step))) for part in far_grads_t]
    operands += [(queries_t, half_across), (keys_t, across), (values_t, across)]
    operands += [(keys, down), (values, down), (key_acc, sums), (value_acc, sums)]
    operands += [(query_grad_t, half_across)]
    operands += whole([*tokens, *grads, *attended])
    results = [((BLK, half), BF)] + [((half, 3 * BLK), BF)] * 2
    results += [((3 * BLK, model // 2), BF), ((3 * BLK, model // 2), F32)]
    if final:
        results += [((half - step, model), F32)]
        operands += whole([part for both in before for part in both])
        operands += whole([mate_rows, rows])
    if last:
        results += [((BLK, model), BF), ((BLK, model), F32)]
    scratch = [pltpu.VMEM((BLK, half), BF)] + [pltpu.VMEM((3 * BLK, half), BF)] * 2
    return run(body, "later_half", [plan, offsets.reshape(-1)], operands, results, scratch, 8)


def halves(pieces, low):
    kept = {place: part for place, part in pieces.items() if (place // low) % 2 == 0}
    return side_by_side([pieces[place + low].astype(BF) for place in kept]), kept


def joined(kept, came):
    block = came.shape[1] // len(kept)
    return {
        place: part + came[:, at * block : (at + 1) * block].astype(F32)
        for at, (place, part) in enumerate(kept.items())
    }


def tied(values, others):
    return list(lax.optimization_barrier((*values, *others))[: len(values)])


def phase(*values):
    flat, tree = jax.tree.flatten(values)
    return jax.tree.unflatten(tree, lax.optimization_barrier(tuple(flat)))


def to_owner(block_sum):
    seq_count, batch_count = lax.axis_size("seq"), lax.axis_size("batch")
    ratio = batch_count // seq_count
    moves = [
        (s * batch_count + b, (b // ratio) * batch_count + s * ratio + b % ratio)
        for s in range(seq_count)
        for b in range(batch_count)
    ]
    return lax.ppermute(block_sum, ("seq", "batch"), moves)


def per_device(hidden, grad_out, block_offsets, w_query, w_key, w_value, w_out):
    tokens = hidden[0]
    grad_rows = grad_out[0]
    offsets = block_offsets[0]
    row_count, width = tokens.shape
    seq_count = lax.axis_size("seq")
    batch_count = lax.axis_size("batch")
    seq_at = lax.axis_index("seq")
    head_width = width // seq_count
    head_size = head_width // offsets.shape[0]
    pairs = head_width // BLK
    half_count = seq_count // 2

    weights = (w_query, w_key, w_value)
    rows = weight_rows(seq_at, head_width, weights)
    shard_blocks = row_count // BLK
    blocks = shard_blocks * seq_count
    block_at = jnp.arange(blocks, dtype=jnp.int32)
    place_of = ((block_at // shard_blocks) ^ seq_at) * shard_blocks + block_at % shard_blocks
    col_block = width // batch_count
    direct = col_block == BLK
    col_order = jnp.arange(width // BLK, dtype=jnp.int32)
    if direct:
        half_at = jnp.arange(batch_count // 2, dtype=jnp.int32) * 2
        col_order = lax.axis_index("batch") ^ jnp.concatenate([half_at + 1, half_at])
    seq_rows = (seq_at ^ jnp.asarray([0, *range(half_count, seq_count)])) * head_width
    batch_at = lax.axis_index("batch")
    ratio = batch_count // seq_count
    out_order = jnp.concatenate(
        [(batch_at // ratio) ^ jnp.arange(seq_count), jnp.reshape(batch_at % ratio, (1,))]
    )
    plan = jnp.concatenate([place_of, seq_rows, col_order, out_order])
    order_at = blocks + 1 + half_count
    plan = plan.astype(jnp.int32)

    mate_rows = weight_rows(seq_at ^ 1, head_width, weights)
    near_tokens = spread(tokens, "seq", half_count)
    near_grads = spread(grad_rows, "seq", half_count)
    projected = project(
        plan, blocks, near_tokens, near_grads, rows, w_out, 1.0 / math.sqrt(head_size)
    )
    projected, far_grads_t, (early, late) = projected[:6], projected[6:-2], projected[-2:]
    far_tokens = swap(tokens, "seq", half_count)
    plan, flat_offsets = plan, offsets.reshape(-1)
    far_tokens, mate_rows, projected, far_grads_t, early, late, plan, flat_offsets = phase(
        far_tokens, mate_rows, projected, far_grads_t, early, late, plan, flat_offsets
    )
    offsets = flat_offsets.reshape(offsets.shape)
    far_grads_t = [swap(part, "seq", half_count + at) for at, part in enumerate(far_grads_t)]
    early = swap(early, "seq", half_count)
    far_tokens = spread(far_tokens, "seq", half_count)
    first = own_half(plan, offsets, far_tokens, rows, projected)
    first, far_grads_t, early, late = phase(first, far_grads_t, early, late)
    late = swap(late, "seq", half_count)
    early = spread(early, "seq", half_count)
    all_tokens = near_tokens + far_tokens

    even = range(0, batch_count, 2)

    def begin(sent_terms, kept_terms):
        if direct:
            return sent_terms, {p: kept_terms[:, p // 2 * BLK : (p // 2 + 1) * BLK] for p in even}
        terms = jnp.concatenate([sent_terms.astype(F32), kept_terms], axis=1)
        pieces = [
            lax.dynamic_slice(
                terms, (0, (batch_at ^ p) * col_block), (terms.shape[0], col_block)
            )
            for p in range(batch_count)
        ]
        return side_by_side([pieces[p + 1].astype(BF) for p in even]), {p: pieces[p] for p in even}

    def begin_out(attended, terms):
        if direct and ratio == pairs:
            return terms[0], {p: terms[1][:, p // 2 * head_width : (p // 2 + 1) * head_width] for p in even}
        attended_t = jnp.concatenate([first[5], jnp.concatenate(attended, axis=0)], axis=1)
        grads = jnp.concatenate(all_grads, axis=0)
        terms = jnp.dot(attended_t, grads, preferred_element_type=F32)
        height = head_width // ratio
        pieces = []
        for p in range(batch_count):
            target = batch_at ^ p
            corner = ((target % ratio) * height, (target // ratio) * head_width)
            pieces.append(lax.dynamic_slice(terms, corner, (height, head_width)))
        return side_by_side([pieces[p + 1].astype(BF) for p in even]), {p: pieces[p] for p in even}

    kept, came_terms, stayed, came, attended = [], [], [], [], []
    for pair in range(pairs):
        last = pair == pairs - 1
        all_grads = []
        if last:
            late = spread(late, "seq", half_count)
            late, came = phase(late, came)
            all_grads = near_grads + [part for both in zip(early, late) for part in both]
        far_attended, stay, leave, *terms = later_half(
            plan,
            offsets,
            order_at,
            far_grads_t,
            pair,
            first,
            all_tokens,
            all_grads if direct and ratio == pairs else [],
            [first[5], *attended] if last and direct and ratio == pairs else [],
            list(zip(stayed, came)),
            rows if last else None,
            mate_rows,
        )
        if last:
            stay, leave, terms, came_terms = phase(stay, leave, terms, came_terms)
        else:
            stay, leave, terms, far_attended, early, late, first = phase(
                stay, leave, terms, far_attended, early, late, first
            )
        attended.append(far_attended)
        stayed.append(stay)
        came.append(swap(leave, "seq", 1))
        if not last:
            goes, kept_head = begin(*terms)
            kept.append(kept_head)
            came_terms.append(swap(goes, "batch", 1))

    levels = [1 << bit for bit in range(1, batch_count.bit_length() - 1)]
    goes, kept_out = begin_out(attended, terms[3:])
    came_out = swap(goes, "batch", 1)
    goes_head, kept_head = begin(*terms[:2])
    pieces = [None] * len(kept)
    lags = [1] * len(pieces)

    def start(at, turn):
        goes, kept = halves(pieces[at], levels[turn - lags[at]])
        return at, kept, swap(goes, "batch", levels[turn - lags[at]])

    def due(turn):
        return [at for at in range(len(pieces)) if 0 <= turn - lags[at] < len(levels)]

    moving = []

    held = [rows, mate_rows]
    sent = []
    for at in range(1, half_count):
        mate = came[-1][at * row_count : (at + 1) * row_count]
        total = jnp.dot(mate, mate_rows[(pairs - 1) * 3 * BLK :], preferred_element_type=F32)
        total += terms[2][(at - 1) * row_count : at * row_count]
        sent.append(total.astype(BF))
    cut = row_count // 2
    sent = [(part[:cut], part[cut:]) for part in sent]
    stayed, came, sent_after = phase(stayed, came, sent)
    partial = 0.0
    for pair in range(pairs):
        for side, parts in enumerate((stayed, came)):
            weight = held[side][pair * 3 * BLK : (pair + 1) * 3 * BLK]
            partial += jnp.dot(parts[pair][:row_count], weight, preferred_element_type=F32)
    token_parts = [swap(part[0], "seq", 2 * at) for at, part in enumerate(sent, 1)]
    came_head = swap(goes_head, "batch", 1)

    turn, out_part = 0, None
    while turn < 2 + len(levels):
        transfers = [came for _, _, came in moving]
        if turn == 0:
            came_terms, came_out, sent_after = phase(came_terms, came_out, sent_after)
            pieces = [joined(*both) for both in zip(kept, came_terms)]
            later_parts = [swap(part[1], "seq", 2 * at) for at, part in enumerate(sent_after, 1)]
            pieces.append(joined(kept_out, came_out))
            lags.append(1)
        elif turn == 1:
            transfers, came_head, token_parts = phase(transfers, came_head, token_parts)
            pieces.append(joined(kept_head, came_head))
            lags.append(2)
        elif turn == 2:
            transfers, later_parts = phase(transfers, later_parts)
        else:
            transfers = phase(transfers)[0]
        for (at, kept_now, _), came_now in zip(moving, transfers):
            pieces[at] = joined(kept_now, came_now)
        turn += 1
        moving = [start(at, turn) for at in due(turn)]
        if turn == 1 + len(levels):
            out_part = to_owner(pieces[pairs - 1][0])[None]

    grad_hidden = partial
    for both in zip(token_parts, later_parts):
        grad_hidden = grad_hidden + jnp.concatenate(both, axis=0).astype(F32)
    grad_hidden = grad_hidden.astype(BF)
    head_sums = [pieces[at][0] for at in range(len(pieces)) if at != pairs - 1]
    row_block = width // batch_count
    head_part = jnp.stack([part.reshape(3, BLK, row_block) for part in head_sums], axis=1)
    head_part = head_part.reshape(3, head_width, row_block).transpose(0, 2, 1)
    grad_weights = jnp.concatenate([head_part, out_part], axis=0)
    norm_factor = 1.0 / math.sqrt(row_count * seq_count * batch_count)
    return (grad_hidden[None], grad_weights * norm_factor)


def solution(mesh):
    placed = (
        P("batch", "seq", None),
        P("batch", "seq", None),
        P("batch", "seq", None, None),
        P(),
        P(),
        P(),
        P(),
    )
    return jax.shard_map(
        per_device,
        mesh=mesh,
        in_specs=placed,
        out_specs=(P("batch", "seq", None), P(None, "batch", "seq")),
        check_vma=False,
    )
```

time: 159 us -> 113 us (0.71); the launches traced: 156 us -> 113 us
  local copies, waits for them, and re-layouts: 31.6 us -> 2.43 us
  Pallas kernels: 29.1 us -> 51.2 us
  waiting for transfers between devices: 46.8 us -> 29.5 us
  matrix products: 21.2 us -> 6.65 us
  other arithmetic: 3.85 us -> 1.41 us
  starting transfers between devices: 22.4 us -> 20.4 us
    pallas_call x1 -> x6, Pallas kernels: 29.1 us -> 51.2 us  [run(): pl.pallas_call(kernel, in_specs=[pl.BlockSpec(memory_space=pltpu.SMEM)] *...]
    ppermute x16 -> x23, waiting for transfers between devices: 44.7 us -> 23 us  [swap(): lax.ppermute(value, axis, [(at, at ^ distance) for at in range(count)])]
    dot_general x6 -> x5, matrix products: 21.2 us -> 6.65 us  [the longest x4 4.32 us: per_device(): jnp.dot(parts[pair][:row_count], weight, preferred_element_type=F32)]
    slice x3 -> x1, local copies, waits for them, and re-layouts: 11.1 us -> 0.05 us  [per_device(): sent = [(part[:cut], part[cut:]) for part in sent]]
    unnamed x40 -> x23, local copies, waits for them, and re-layouts: 9.59 us -> 0.54 us
    reshape x2 -> x1, local copies, waits for them, and re-layouts: 6.1 us -> 0.32 us  [per_device(): head_part = head_part.reshape(3, head_width, row_block).transpose(0, 2, 1)]
    ppermute x2 -> x1, waiting for transfers between devices: 2.05 us -> 6.48 us  [to_owner(): return lax.ppermute(block_sum, ('seq', 'batch'), moves)]
    ppermute x2 -> x1, starting transfers between devices: 6 us -> 2.37 us  [to_owner(): return lax.ppermute(block_sum, ('seq', 'batch'), moves)]
  transfers between devices with their start and end apart: 18 -> 24, of which waited for: 7 -> 13; matrix products, arithmetic and copies ran while one was open for 28% -> 8% of each run, Pallas kernels for 0% -> 45%
where the time goes in v3:
time: 113 us
  Pallas kernels  51.2 us (45%)
  waiting for transfers between devices  29.5 us (26%)
  starting transfers between devices  20.4 us (18%)
  matrix products  6.65 us (6%)
  local copies, waits for them, and re-layouts  2.43 us (2%)
  other arithmetic  1.41 us (1%)
    pallas_call x6, Pallas kernels, run(): pl.pallas_call(kernel, in_specs=[pl.BlockSpec(memory_space=pltpu.SMEM)] *...  51.2 us
    ppermute x23, waiting for transfers between devices, swap(): lax.ppermute(value, axis, [(at, at ^ distance) for at in range(count)])  23 us
    ppermute x23, starting transfers between devices, swap(): lax.ppermute(value, axis, [(at, at ^ distance) for at in range(count)])  18.1 us
    ppermute x1, waiting for transfers between devices, to_owner(): return lax.ppermute(block_sum, ('seq', 'batch'), moves)  6.48 us
    dot_general x4, matrix products, per_device(): jnp.dot(parts[pair][:row_count], weight, preferred_element_type=F32)  4.32 us
    ppermute x1, starting transfers between devices, to_owner(): return lax.ppermute(block_sum, ('seq', 'batch'), moves)  2.37 us
    dot_general x1, matrix products, per_device(): jnp.dot(mate, mate_rows[(pairs - 1) * 3 * BLK:], preferred_element_type=F32)  2.33 us
  transfers between devices with their start and end apart: 24, of which 13 were waited for; matrix products, arithmetic and copies ran while one was open for 8% of the time, Pallas kernels for 45%

profile of v3, /device:TPU:4, one launch (start us, length us, event | category | flops | bytes accessed | tf_op | source)
XLA Modules:
  0.0 112.5 jit_solution(3317268866315742484)
XLA Ops:
  1.2 2.8 %weight_rows.3.refs_1_.refs_2_.refs_27_ = bf16[768,1024]{1,0:T(8,128)(2,1)} custom-call(s32[1]{0:T(128)} %bitcast.3.refs_0_, bf16[1024,1024]{1,0:T(8,128)(2,1)} %refs_1_.3, bf16[1024,1024]{1,0:T(8,128)(2,1)} %refs_2_.4, bf16[1024,1024]{1,0:T(8,128)(2,1)} %refs_3_.4), custom_call_target="tpu_custom_call" | custom-call | flops 1 | bytes 1 | tf_op jit(solution)/shard_map/weight_rows/pallas_call | solution.py:109
  4.1 2.8 %weight_rows.2.refs_26_ = bf16[768,1024]{1,0:T(8,128)(2,1)} custom-call(s32[1]{0:T(128)} %bitcast.1.refs_0_, bf16[1024,1024]{1,0:T(8,128)(2,1)} %refs_1_.3, bf16[1024,1024]{1,0:T(8,128)(2,1)} %refs_2_.4, bf16[1024,1024]{1,0:T(8,128)(2,1)} %refs_3_.4), custom_call_target="tpu_custom_call" | custom-call | flops 1 | bytes 1 | tf_op jit(solution)/shard_map/weight_rows/pallas_call | solution.py:109
  8.5 8.5 %project.1 = (bf16[256,768]{1,0:T(8,128)(2,1)}, bf16[256,768]{1,0:T(8,128)(2,1)}, bf16[256,768]{1,0:T(8,128)(2,1)}, bf16[256,768]{1,0:T(8,128)(2,1)}, bf16[768,2...) custom-call(s32[28]{0:T(128)} %concatenate.22.refs_0_, ...), custom_call_target="tpu_custom_call" | custom-call | flops 1 | bytes 1 | tf_op jit(solution)/shard_map/project/pallas_call | solution.py:109
  16.9 4.1 %collective-permute-done.refs_3_.refs_14_ = bf16[384,1024]{1,0:T(8,128)(2,1)} collective-permute-done((bf16[384,1024]{1,0:T(8,128)(2,1)}, bf16[384,1024]{1,0:T(8,128)(2,1)}, u32[]{:S(2)}, u32[]{:S(2)}) %collective-permute-start) | collective-permute-done | bytes 786464 | tf_op jit(solution)/shard_map/ppermute | solution.py:25
  21.3 1.7 %collective-permute-start.4 = (bf16[256,384]{1,0:T(8,128)(2,1)}, bf16[256,384]{1,0:T(8,128)(2,1)S(1)}, u32[]{:S(2)}, u32[]{:S(2)}) collective-permute-start(bf16[256,384]{1,0:T(8,128)(2,1)} %get-tuple-element.132), channel_id=1, source_target_pairs={{0,16},{8,24},{16,0},{24,8},{1,17},{9,25},{17,1},{25,9},{2,18},{10... | collective-permute-start | bytes 589832 | tf_op jit(solution)/shard_map/ppermute | solution.py:25
  23.7 14.3 %own_half.1 = (bf16[256,768]{1,0:T(8,128)(2,1)}, bf16[256,1536]{1,0:T(8,128)(2,1)}, bf16[256,1536]{1,0:T(8,128)(2,1)}, bf16[1536,256]{1,0:T(8,128)(2,1)}, bf16[1...) custom-call(s32[28]{0:T(128)} %concatenate.22.refs_0_, ...), custom_call_target="tpu_custom_call" | custom-call | flops 1 | bytes 1 | tf_op jit(solution)/shard_map/own_half/pallas_call | solution.py:109
  38.0 2.9 %collective-permute-done.5.refs_3_ = bf16[256,384]{1,0:T(8,128)(2,1)S(1)} collective-permute-done((bf16[256,384]{1,0:T(8,128)(2,1)}, bf16[256,384]{1,0:T(8,128)(2,1)S(1)}, u32[]{:S(2)}, u32[]{:S(2)}) %collective-permute-start.5) | collective-permute-done | bytes 196640 | tf_op jit(solution)/shard_map/ppermute | solution.py:25
  41.5 10.0 %later_half.2 = (bf16[128,768]{1,0:T(8,128)(2,1)}, bf16[768,384]{1,0:T(8,128)(2,1)}, bf16[768,384]{1,0:T(8,128)(2,1)}, bf16[384,512]{1,0:T(8,128)(2,1)}, f32[384,512]{1,0:T(8,128)}) custom-call(s32[28]{0:T(128)} %concatenate.22.refs_0_, s32[192]{0:T(256)} %reshape_squeeze.3.refs_1_, bf16[256,384]{1,0:T(8,128)(2,1)} %copy-done.3, bf16[256,384]{1,0:T(8,128)(2,1)} %copy-done.4, ...), custom_call_target="tpu_custom_call" | custom-call | flops 1 | bytes 1 | tf_op jit(solution)/shard_map/later_half/pallas_call | solution.py:109
  52.9 1.5 %collective-permute-start.11 = (bf16[384,512]{1,0:T(8,128)(2,1)}, bf16[384,512]{1,0:T(8,128)(2,1)S(1)}, u32[]{:S(2)}, u32[]{:S(2)}) collective-permute-start(bf16[384,512]{1,0:T(8,128)(2,1)} %get-tuple-element.180), channel_id=1, source_target_pairs={{0,1},{1,0},{2,3},{3,2},{4,5},{5,4},{6,7},{7,6},{8,9},{9,8},{10,11... | collective-permute-start | bytes 1179656 | tf_op jit(solution)/shard_map/ppermute | solution.py:25
  55.3 12.8 %later_half.3 = (bf16[128,768]{1,0:T(8,128)(2,1)}, bf16[768,384]{1,0:T(8,128)(2,1)}, bf16[768,384]{1,0:T(8,128)(2,1)}, bf16[384,512]{1,0:T(8,128)(2,1)}, f32[384...) custom-call(s32[28]{0:T(128)} %concatenate.22.refs_0_, ...), custom_call_target="tpu_custom_call" | custom-call | flops 1 | bytes 1 | tf_op jit(solution)/shard_map/later_half/pallas_call | solution.py:109
  68.2 1.5 %collective-permute-start.13 = (bf16[128,1024]{1,0:T(8,128)(2,1)}, bf16[128,1024]{1,0:T(8,128)(2,1)S(1)}, u32[]{:S(2)}, u32[]{:S(2)}) collective-permute-start(bf16[128,1024]{1,0:T(8,128)(2,1)} %get-tuple-element.190), channel_id=1, source_target_pairs={{0,1},{1,0},{2,3},{3,2},{4,5},{5,4},{6,7},{7,6},{8,9},{9,8},{10,11... | collective-permute-start | bytes 786440 | tf_op jit(solution)/shard_map/ppermute | solution.py:25
  70.4 2.3 %add_convert_fusion.1 = bf16[384,1024]{1,0:T(8,128)(2,1)S(1)} fusion(f32[384,1024]{1,0:T(8,128)} %get-tuple-element.183, bf16[768,1024]{1,0:T(8,128)(2,1)} %weight_rows.2.refs_26_, bf16[768,384]{1,0:T(8,128)(2,1)S(1)} %collective-permute-done.12), kind=kOutput, calls=%fused_computation.1 | convolution fusion | flops 302776320 | bytes 3440640 | tf_op jit(solution)/shard_map/dot_general | solution.py:657
  73.7 3.9 %collective-permute-done.13 = bf16[128,1024]{1,0:T(8,128)(2,1)S(1)} collective-permute-done((bf16[128,1024]{1,0:T(8,128)(2,1)}, bf16[128,1024]{1,0:T(8,128)(2,1)S(1)}, u32[]{:S(2)}, u32[]{:S(2)}) %collective-permute-start.13) | collective-permute-done | bytes 262176 | tf_op jit(solution)/shard_map/ppermute | solution.py:25
  77.7 1.6 %collective-permute-start.15 = (bf16[128,512]{1,0:T(8,128)(2,1)S(1)}, bf16[128,512]{1,0:T(8,128)(2,1)S(1)}, u32[]{:S(2)}, u32[]{:S(2)}) collective-permute-start(bf16[128,512]{1,0:T(8,128)(2,1)S(1)} %pad_maximum_fusion.3), channel_id=1, source_target_pairs={{0,2},{1,3},{2,0},{3,1},{4,6},{5,7},{6,4},{7,5},{8,10},{9,11},{10,... | collective-permute-start | bytes 393224 | tf_op jit(solution)/shard_map/ppermute | solution.py:25
  82.0 3.4 %collective-permute-done.16 = bf16[384,512]{1,0:T(8,128)(2,1)S(1)} collective-permute-done((bf16[384,512]{1,0:T(8,128)(2,1)}, bf16[384,512]{1,0:T(8,128)(2,1)S(1)}, u32[]{:S(2)}, u32[]{:S(2)}) %collective-permute-start.16) | collective-permute-done | bytes 393248 | tf_op jit(solution)/shard_map/ppermute | solution.py:25
  86.6 2.6 %collective-permute-start.19 = (bf16[128,256]{1,0:T(8,128)(2,1)S(1)}, bf16[128,256]{1,0:T(8,128)(2,1)S(1)}, u32[]{:S(2)}, u32[]{:S(2)}) collective-permute-start(bf16[128,256]{1,0:T(8,128)(2,1)S(1)} %add_convert_fusion.8), channel_id=1, source_target_pairs={{0,4},{1,5},{2,6},{3,7},{4,0},{5,1},{6,2},{7,3},{8,12},{9,13},{10,... | collective-permute-start | bytes 196616 | tf_op jit(solution)/shard_map/ppermute | solution.py:25
  89.8 1.6 %collective-permute-start.20 = (bf16[384,256]{1,0:T(8,128)(2,1)S(1)}, bf16[384,256]{1,0:T(8,128)(2,1)S(1)}, u32[]{:S(2)}, u32[]{:S(2)}) collective-permute-start(bf16[384,256]{1,0:T(8,128)(2,1)S(1)} %pad_maximum_fusion.2), channel_id=1, source_target_pairs={{0,2},{1,3},{2,0},{3,1},{4,6},{5,7},{6,4},{7,5},{8,10},{9,11},{10,... | collective-permute-start | bytes 589832 | tf_op jit(solution)/shard_map/ppermute | solution.py:25
  91.3 1.5 %fusion.5 = f32[384,1024]{1,0:T(8,128)S(1)} fusion(bf16[768,1024]{1,0:T(8,128)(2,1)S(1)} %copy-done.1, bf16[768,384]{1,0:T(8,128)(2,1)} %collective-permute-done.10.refs_25_), kind=kOutput, calls=%fused_computation.7 | convolution fusion | flops 301989888 | bytes 2654208 | tf_op jit(solution)/shard_map/dot_general | solution.py:667
  92.9 1.4 %collective-permute-done.19 = bf16[128,256]{1,0:T(8,128)(2,1)S(1)} collective-permute-done((bf16[128,256]{1,0:T(8,128)(2,1)S(1)}, bf16[128,256]{1,0:T(8,128)(2,1)S(1)}, u32[]{:S(2)}, u32[]{:S(2)}) %collective-permute-start.19) | collective-permute-done | bytes 65568 | tf_op jit(solution)/shard_map/ppermute | solution.py:25
  94.3 2.3 %collective-permute-done.18 = bf16[384,128]{1,0:T(8,128)(2,1)S(1)} collective-permute-done((bf16[384,128]{1,0:T(8,128)(2,1)S(1)}, bf16[384,128]{1,0:T(8,128)(2,1)S(1)}, u32[]{:S(2)}, u32[]{:S(2)}) %collective-permute-start.18) | collective-permute-done | bytes 98336 | tf_op jit(solution)/shard_map/ppermute | solution.py:25
  97.6 2.3 %collective-permute-start.22 = (bf16[384,128]{1,0:T(8,128)(2,1)S(1)}, bf16[384,128]{1,0:T(8,128)(2,1)S(1)}, u32[]{:S(2)}, u32[]{:S(2)}) collective-permute-start(bf16[384,128]{1,0:T(8,128)(2,1)S(1)} %add_convert_fusion.2), channel_id=1, source_target_pairs={{0,4},{1,5},{2,6},{3,7},{4,0},{5,1},{6,2},{7,3},{8,12},{9,13},{10,... | collective-permute-start | bytes 294920 | tf_op jit(solution)/shard_map/ppermute | solution.py:25
  99.8 2.4 %collective-permute-start.23 = (f32[128,256]{1,0:T(8,128)S(1)}, f32[128,256]{1,0:T(8,128)S(1)}, u32[]{:S(2)}, u32[]{:S(2)}) collective-permute-start(f32[128,256]{1,0:T(8,128)S(1)} %convert_add_fusion.2), channel_id=1, source_target_pairs={{0,0},{1,1},{2,8},{3,9},{4,16},{5,17},{6,24},{7,25},{8,2},{9,3},{1... | collective-permute-start | bytes 393224 | tf_op jit(solution)/shard_map/ppermute | solution.py:513
  102.2 1.7 %fusion = bf16[1,384,1024]{2,1,0:T(8,128)(2,1)} fusion(f32[384,1024]{1,0:T(8,128)S(1)} %fusion.1, f32[384,1024]{1,0:T(8,128)S(1)} %fusion.3, f32[384,1024]{1,0:T(8,128)S(1)} %fusion.5, bf16[192,1024]{1,0:T(8,128)(2,1)S(1)} %collective-permute-done.21, bf16[192,1024]{1,0:T(8,128)(2,1)S(1)} %collective-permute-done.17, bf16[768,1024]{1,0:T(8,128)(2,1)S(1)} %copy-done.1, ...), kind=kOutput, calls=%fused_computation.2 | convolution fusion | flops 305528832 | bytes 7372800 | tf_op jit(solution)/shard_map/dot_general | solution.py:667
  105.2 6.5 %collective-permute-done.23 = f32[128,256]{1,0:T(8,128)S(1)} collective-permute-done((f32[128,256]{1,0:T(8,128)S(1)}, f32[128,256]{1,0:T(8,128)S(1)}, u32[]{:S(2)}, u32[]{:S(2)}) %collective-permute-start.23) | collective-permute-done | bytes 131104 | tf_op jit(solution)/shard_map/ppermute | solution.py:513
  (82 shorter events, 15.2 us)
Async XLA Ops:
  0.6 7.8 %collective-permute-start.1 = (bf16[384,1024]{1,0:T(8,128)(2,1)}, bf16[384,1024]{1,0:T(8,128)(2,1)}, u32[]{:S(2)}, u32[]{:S(2)}) collective-permute-start(bf16[384,1024]{1,0:T(8,128)(2,1)} %bitcast.13), channel_id=1, source_target_pairs={{0,8},{8,0},{16,24},{24,16},{1,9},{9,1},{17,25},{25,17},{2,10},{10... | collective-permute-start | bytes 2359304 | tf_op jit(solution)/shard_map/ppermute | solution.py:25
  0.7 7.8 %collective-permute-start.2 = (bf16[384,1024]{1,0:T(8,128)(2,1)}, bf16[384,1024]{1,0:T(8,128)(2,1)}, u32[]{:S(2)}, u32[]{:S(2)}) collective-permute-start(bf16[384,1024]{1,0:T(8,128)(2,1)} %bitcast.18), channel_id=1, source_target_pairs={{0,8},{8,0},{16,24},{24,16},{1,9},{9,1},{17,25},{25,17},{2,10},{10... | collective-permute-start | bytes 2359304 | tf_op jit(solution)/shard_map/ppermute | solution.py:25
  1.2 19.8 %collective-permute-start = (bf16[384,1024]{1,0:T(8,128)(2,1)}, bf16[384,1024]{1,0:T(8,128)(2,1)}, u32[]{:S(2)}, u32[]{:S(2)}) collective-permute-start(bf16[384,1024]{1,0:T(8,128)(2,1)} %bitcast.14), channel_id=1, source_target_pairs={{0,16},{8,24},{16,0},{24,8},{1,17},{9,25},{17,1},{25,9},{2,18},{10... | collective-permute-start | bytes 2359304 | tf_op jit(solution)/shard_map/ppermute | solution.py:25
  21.0 2.6 %collective-permute-start.3 = (bf16[384,1024]{1,0:T(8,128)(2,1)}, bf16[384,1024]{1,0:T(8,128)(2,1)}, u32[]{:S(2)}, u32[]{:S(2)}) collective-permute-start(bf16[384,1024]{1,0:T(8,128)(2,1)} %collective-permute-done.refs_3_.refs_14_), channel_id=1, source_target_pairs={{0,8},{8,0},{16,24},{24,16},{1,9},{9,1},{17,25},{25,17},{2,10},{10... | collective-permute-start | bytes 2359304 | tf_op jit(solution)/shard_map/ppermute | solution.py:25
  21.1 19.8 %collective-permute-start.6 = (bf16[192,1024]{1,0:T(8,128)(2,1)}, bf16[192,1024]{1,0:T(8,128)(2,1)}, u32[]{:S(2)}, u32[]{:S(2)}) collective-permute-start(bf16[192,1024]{1,0:T(8,128)(2,1)} %get-tuple-element.134), channel_id=1, source_target_pairs={{0,16},{8,24},{16,0},{24,8},{1,17},{9,25},{17,1},{25,9},{2,18},{10... | collective-permute-start | bytes 1179656 | tf_op jit(solution)/shard_map/ppermute | solution.py:25
  21.3 16.6 %collective-permute-start.4 = (bf16[256,384]{1,0:T(8,128)(2,1)}, bf16[256,384]{1,0:T(8,128)(2,1)S(1)}, u32[]{:S(2)}, u32[]{:S(2)}) collective-permute-start(bf16[256,384]{1,0:T(8,128)(2,1)} %get-tuple-element.132), channel_id=1, source_target_pairs={{0,16},{8,24},{16,0},{24,8},{1,17},{9,25},{17,1},{25,9},{2,18},{10... | collective-permute-start | bytes 589832 | tf_op jit(solution)/shard_map/ppermute | solution.py:25
  23.1 17.7 %collective-permute-start.5 = (bf16[256,384]{1,0:T(8,128)(2,1)}, bf16[256,384]{1,0:T(8,128)(2,1)S(1)}, u32[]{:S(2)}, u32[]{:S(2)}) collective-permute-start(bf16[256,384]{1,0:T(8,128)(2,1)} %get-tuple-element.133), channel_id=1, source_target_pairs={{0,24},{8,16},{16,8},{24,0},{1,25},{9,17},{17,9},{25,1},{2,26},{10... | collective-permute-start | bytes 589832 | tf_op jit(solution)/shard_map/ppermute | solution.py:25
  40.8 11.5 %collective-permute-start.8 = (bf16[192,1024]{1,0:T(8,128)(2,1)}, bf16[192,1024]{1,0:T(8,128)(2,1)}, u32[]{:S(2)}, u32[]{:S(2)}) collective-permute-start(bf16[192,1024]{1,0:T(8,128)(2,1)} %get-tuple-element.152), channel_id=1, source_target_pairs={{0,16},{8,24},{16,0},{24,8},{1,17},{9,25},{17,1},{25,9},{2,18},{10... | collective-permute-start | bytes 1179656 | tf_op jit(solution)/shard_map/ppermute | solution.py:25
  41.1 11.3 %collective-permute-start.7 = (bf16[192,1024]{1,0:T(8,128)(2,1)}, bf16[192,1024]{1,0:T(8,128)(2,1)}, u32[]{:S(2)}, u32[]{:S(2)}) collective-permute-start(bf16[192,1024]{1,0:T(8,128)(2,1)} %collective-permute-done.6.refs_18_), channel_id=1, source_target_pairs={{0,8},{8,0},{16,24},{24,16},{1,9},{9,1},{17,25},{25,17},{2,10},{10... | collective-permute-start | bytes 1179656 | tf_op jit(solution)/shard_map/ppermute | solution.py:25
  52.4 2.9 %collective-permute-start.10 = (bf16[768,384]{1,0:T(8,128)(2,1)}, bf16[768,384]{1,0:T(8,128)(2,1)}, u32[]{:S(2)}, u32[]{:S(2)}) collective-permute-start(bf16[768,384]{1,0:T(8,128)(2,1)} %get-tuple-element.165), channel_id=1, source_target_pairs={{0,8},{8,0},{16,24},{24,16},{1,9},{9,1},{17,25},{25,17},{2,10},{10... | collective-permute-start | bytes 1769480 | tf_op jit(solution)/shard_map/ppermute | solution.py:25
  52.4 2.9 %collective-permute-start.9 = (bf16[192,1024]{1,0:T(8,128)(2,1)}, bf16[192,1024]{1,0:T(8,128)(2,1)}, u32[]{:S(2)}, u32[]{:S(2)}) collective-permute-start(bf16[192,1024]{1,0:T(8,128)(2,1)} %collective-permute-done.8.refs_19_), channel_id=1, source_target_pairs={{0,8},{8,0},{16,24},{24,16},{1,9},{9,1},{17,25},{25,17},{2,10},{10... | collective-permute-start | bytes 1179656 | tf_op jit(solution)/shard_map/ppermute | solution.py:25
  52.9 15.2 %collective-permute-start.11 = (bf16[384,512]{1,0:T(8,128)(2,1)}, bf16[384,512]{1,0:T(8,128)(2,1)S(1)}, u32[]{:S(2)}, u32[]{:S(2)}) collective-permute-start(bf16[384,512]{1,0:T(8,128)(2,1)} %get-tuple-element.180), channel_id=1, source_target_pairs={{0,1},{1,0},{2,3},{3,2},{4,5},{5,4},{6,7},{7,6},{8,9},{9,8},{10,11... | collective-permute-start | bytes 1179656 | tf_op jit(solution)/shard_map/ppermute | solution.py:25
  68.1 2.3 %collective-permute-start.12 = (bf16[768,384]{1,0:T(8,128)(2,1)}, bf16[768,384]{1,0:T(8,128)(2,1)S(1)}, u32[]{:S(2)}, u32[]{:S(2)}) collective-permute-start(bf16[768,384]{1,0:T(8,128)(2,1)} %get-tuple-element.182), channel_id=1, source_target_pairs={{0,8},{8,0},{16,24},{24,16},{1,9},{9,1},{17,25},{25,17},{2,10},{10... | collective-permute-start | bytes 1769480 | tf_op jit(solution)/shard_map/ppermute | solution.py:25
  68.2 9.4 %collective-permute-start.13 = (bf16[128,1024]{1,0:T(8,128)(2,1)}, bf16[128,1024]{1,0:T(8,128)(2,1)S(1)}, u32[]{:S(2)}, u32[]{:S(2)}) collective-permute-start(bf16[128,1024]{1,0:T(8,128)(2,1)} %get-tuple-element.190), channel_id=1, source_target_pairs={{0,1},{1,0},{2,3},{3,2},{4,5},{5,4},{6,7},{7,6},{8,9},{9,8},{10,11... | collective-permute-start | bytes 786440 | tf_op jit(solution)/shard_map/ppermute | solution.py:25
  69.8 15.7 %collective-permute-start.16 = (bf16[384,512]{1,0:T(8,128)(2,1)}, bf16[384,512]{1,0:T(8,128)(2,1)S(1)}, u32[]{:S(2)}, u32[]{:S(2)}) collective-permute-start(bf16[384,512]{1,0:T(8,128)(2,1)} %get-tuple-element.195), channel_id=1, source_target_pairs={{0,1},{1,0},{2,3},{3,2},{4,5},{5,4},{6,7},{7,6},{8,9},{9,8},{10,11... | collective-permute-start | bytes 1179656 | tf_op jit(solution)/shard_map/ppermute | solution.py:25
  72.8 13.8 %collective-permute-start.17 = (bf16[192,1024]{1,0:T(8,128)(2,1)S(1)}, bf16[192,1024]{1,0:T(8,128)(2,1)S(1)}, u32[]{:S(2)}, u32[]{:S(2)}) collective-permute-start(bf16[192,1024]{1,0:T(8,128)(2,1)S(1)} %get-tuple-element.213), channel_id=1, source_target_pairs={{0,16},{8,24},{16,0},{24,8},{1,17},{9,25},{17,1},{25,9},{2,18},{10... | collective-permute-start | bytes 1179656 | tf_op jit(solution)/shard_map/ppermute | solution.py:25
  77.7 7.8 %collective-permute-start.15 = (bf16[128,512]{1,0:T(8,128)(2,1)S(1)}, bf16[128,512]{1,0:T(8,128)(2,1)S(1)}, u32[]{:S(2)}, u32[]{:S(2)}) collective-permute-start(bf16[128,512]{1,0:T(8,128)(2,1)S(1)} %pad_maximum_fusion.3), channel_id=1, source_target_pairs={{0,2},{1,3},{2,0},{3,1},{4,6},{5,7},{6,4},{7,5},{8,10},{9,11},{10,... | collective-permute-start | bytes 393224 | tf_op jit(solution)/shard_map/ppermute | solution.py:25
  79.4 7.2 %collective-permute-start.14 = (bf16[384,256]{1,0:T(8,128)(2,1)S(1)}, bf16[384,256]{1,0:T(8,128)(2,1)S(1)}, u32[]{:S(2)}, u32[]{:S(2)}) collective-permute-start(bf16[384,256]{1,0:T(8,128)(2,1)S(1)} %pad_maximum_fusion.1), channel_id=1, source_target_pairs={{0,2},{1,3},{2,0},{3,1},{4,6},{5,7},{6,4},{7,5},{8,10},{9,11},{10,... | collective-permute-start | bytes 589832 | tf_op jit(solution)/shard_map/ppermute | solution.py:25
  79.9 13.0 %collective-permute-start.21 = (bf16[192,1024]{1,0:T(8,128)(2,1)S(1)}, bf16[192,1024]{1,0:T(8,128)(2,1)S(1)}, u32[]{:S(2)}, u32[]{:S(2)}) collective-permute-start(bf16[192,1024]{1,0:T(8,128)(2,1)S(1)} %get-tuple-element.201), channel_id=1, source_target_pairs={{0,16},{8,24},{16,0},{24,8},{1,17},{9,25},{17,1},{25,9},{2,18},{10... | collective-permute-start | bytes 1179656 | tf_op jit(solution)/shard_map/ppermute | solution.py:25
  86.6 7.7 %collective-permute-start.19 = (bf16[128,256]{1,0:T(8,128)(2,1)S(1)}, bf16[128,256]{1,0:T(8,128)(2,1)S(1)}, u32[]{:S(2)}, u32[]{:S(2)}) collective-permute-start(bf16[128,256]{1,0:T(8,128)(2,1)S(1)} %add_convert_fusion.8), channel_id=1, source_target_pairs={{0,4},{1,5},{2,6},{3,7},{4,0},{5,1},{6,2},{7,3},{8,12},{9,13},{10,... | collective-permute-start | bytes 196616 | tf_op jit(solution)/shard_map/ppermute | solution.py:25
  89.2 7.4 %collective-permute-start.18 = (bf16[384,128]{1,0:T(8,128)(2,1)S(1)}, bf16[384,128]{1,0:T(8,128)(2,1)S(1)}, u32[]{:S(2)}, u32[]{:S(2)}) collective-permute-start(bf16[384,128]{1,0:T(8,128)(2,1)S(1)} %add_convert_fusion.5), channel_id=1, source_target_pairs={{0,4},{1,5},{2,6},{3,7},{4,0},{5,1},{6,2},{7,3},{8,12},{9,13},{10,... | collective-permute-start | bytes 294920 | tf_op jit(solution)/shard_map/ppermute | solution.py:25
  89.8 7.7 %collective-permute-start.20 = (bf16[384,256]{1,0:T(8,128)(2,1)S(1)}, bf16[384,256]{1,0:T(8,128)(2,1)S(1)}, u32[]{:S(2)}, u32[]{:S(2)}) collective-permute-start(bf16[384,256]{1,0:T(8,128)(2,1)S(1)} %pad_maximum_fusion.2), channel_id=1, source_target_pairs={{0,2},{1,3},{2,0},{3,1},{4,6},{5,7},{6,4},{7,5},{8,10},{9,11},{10,... | collective-permute-start | bytes 589832 | tf_op jit(solution)/shard_map/ppermute | solution.py:25
  97.6 7.0 %collective-permute-start.22 = (bf16[384,128]{1,0:T(8,128)(2,1)S(1)}, bf16[384,128]{1,0:T(8,128)(2,1)S(1)}, u32[]{:S(2)}, u32[]{:S(2)}) collective-permute-start(bf16[384,128]{1,0:T(8,128)(2,1)S(1)} %add_convert_fusion.2), channel_id=1, source_target_pairs={{0,4},{1,5},{2,6},{3,7},{4,0},{5,1},{6,2},{7,3},{8,12},{9,13},{10,... | collective-permute-start | bytes 294920 | tf_op jit(solution)/shard_map/ppermute | solution.py:25
  99.8 11.9 %collective-permute-start.23 = (f32[128,256]{1,0:T(8,128)S(1)}, f32[128,256]{1,0:T(8,128)S(1)}, u32[]{:S(2)}, u32[]{:S(2)}) collective-permute-start(f32[128,256]{1,0:T(8,128)S(1)} %convert_add_fusion.2), channel_id=1, source_target_pairs={{0,0},{1,1},{2,8},{3,9},{4,16},{5,17},{6,24},{7,25},{8,2},{9,3},{1... | collective-permute-start | bytes 393224 | tf_op jit(solution)/shard_map/ppermute | solution.py:513
  (11 other events, 62.7 us)

commit v4 on v3

--- a/solution.py
+++ b/solution.py
@@ -206,7 +206,6 @@
     place_of, offsets, head_base, places, queries_t, out_grads_t, key_refs, sums, put, slots, blocks, head_size
 ):
     keys_t, values_t, keys, values = key_refs
-    key_acc, value_acc = sums
     key_at = lax.broadcasted_iota(jnp.int32, (BLK, BLK), 0)
     query_at = lax.broadcasted_iota(jnp.int32, (BLK, BLK), 1)
     causal = key_at <= query_at
@@ -264,6 +263,7 @@
             value_part = dot(out_grads_t[rows, cols], probs_half, LAST_LAST)
             key_part = dot(queries_t[rows, cols], score_grad, LAST_LAST)
             parts.append((rows, named, key_part, value_part))
+        key_acc, value_acc = sums()
         for rows, named, key_part, value_part in parts:
             for at, part in zip(named, cut):
                 key_acc[at, rows, :] += key_part[:, part]
@@ -321,7 +321,7 @@
                 queries_t().at[own, :],
                 out_grads_t().at[own, :],
                 (keys_t.at[own, :], values_t.at[own, :], keys.at[:, own], values.at[:, own]),
-                (key_acc.at[pair], value_acc.at[pair]),
+                lambda pair=pair: (key_acc.at[pair], value_acc.at[pair]),
                 put,
                 slots,
                 blocks,
@@ -353,9 +353,7 @@
 
     def body(scalars, ready, sent, out_grads_t, stay, leave):
         plan = scalars[0]
-        queries_t, keys_t, values_t, keys, values, key_acc, value_acc = (
-            part() for part in ready[near : near + 7]
-        )
+        queries_t, keys_t, values_t, keys, values = (part() for part in ready[near : near + 5])
         query_grad_first = ready[near + 7]
         tokens_here = ready[near + 8 : near + 8 + count]
         grads_here = ready[near + 8 + count : near + 8 + count + len(grads)]
@@ -382,7 +380,7 @@
             queries_t,
             out_grads_t,
             (keys_t, values_t, keys, values),
-            (key_acc, value_acc),
+            lambda: (ready[near + 5](), ready[near + 6]()),
             put,
             slots,
             blocks,
@@ -393,6 +391,7 @@
         for at in range(0, half, BLK):
             target, cols = columns(at // step, at % step)
             target[:BLK, cols] = query_grad_first()[:, at : at + BLK]
+        key_acc, value_acc = ready[near + 5](), ready[near + 6]()
         for at in range(blocks):
             target, cols = columns(at * BLK // step, at * BLK % step)
             target[BLK : 2 * BLK, cols] = key_acc[at].astype(BF)
@@ -408,7 +407,7 @@
                 for at in range(len(before))
                 for side in (1, 0)
             ]
-            lefts = [(left() if isinstance(left, Held) else left)[step:, :] for left, _, _ in parts]
+            lefts = [left()[...] if isinstance(left, Held) else left[step:, :] for left, _, _ in parts]
             left = jnp.concatenate(lefts, axis=1)
             model_n = rows.shape[1]
             for col in range(0, model_n, 2 * BLK):
@@ -454,9 +453,13 @@
                 for left, right in zip(lefts, pieces):
                     taken = jnp.concatenate([part[:, span] for part in right], axis=0)
                     terms += jnp.dot(left, taken, preferred_element_type=F32)
-                cols = slice(at * width, (at + 1) * width)
-                sent[6][:, cols] = jnp.where(own_rows == 0, terms[BLK:], terms[:BLK]).astype(BF)
-                sent[7][:, cols] = jnp.where(own_rows == 0, terms[:BLK], terms[BLK:])
+                goes = jnp.where(own_rows == 0, terms[BLK:], terms[:BLK]).astype(BF)
+                stays = jnp.where(own_rows == 0, terms[:BLK], terms[BLK:])
+                cols = slice(at * BLK, (at + 1) * BLK)
+                for side in range(width // BLK):
+                    held = slice(side * BLK, (side + 1) * BLK)
+                    sent[6][held, cols] = goes[:, held]
+                    sent[7][held, cols] = stays[:, held]
             sent.start(6)
             sent.start(7)
         put_terms(3, [stay[...], leave[...]], [tokens_here[0::2], tokens_here[1::2]])
@@ -472,10 +475,13 @@
     results += [((3 * BLK, model // 2), BF), ((3 * BLK, model // 2), F32)]
     if final:
         results += [((half - step, model), F32)]
-        operands += whole([part for both in before for part in both])
-        operands += whole([mate_rows, rows])
+        far_places = (slice(step, half), slice(0, 3 * BLK))
+        operands += [(part, far_places) for both in before for part in both]
+        if before:
+            operands += [(mate_rows, (slice(0, len(before) * 3 * BLK), slice(0, model)))]
+        operands += [(rows, None)]
     if last:
-        results += [((BLK, model), BF), ((BLK, model), F32)]
+        results += [((width, model // 2), BF), ((width, model // 2), F32)]
     scratch = [pltpu.VMEM((BLK, half), BF)] + [pltpu.VMEM((3 * BLK, half), BF)] * 2
     return run(body, "later_half", [plan, offsets.reshape(-1)], operands, results, scratch, 8)
 
@@ -586,7 +592,7 @@
 
     def begin_out(attended, terms):
         if direct and ratio == pairs:
-            return terms[0], {p: terms[1][:, p // 2 * head_width : (p // 2 + 1) * head_width] for p in even}
+            return begin(*terms)
         attended_t = jnp.concatenate([first[5], jnp.concatenate(attended, axis=0)], axis=1)
         grads = jnp.concatenate(all_grads, axis=0)
         terms = jnp.dot(attended_t, grads, preferred_element_type=F32)
@@ -639,7 +645,7 @@
     came_out = swap(goes, "batch", 1)
     goes_head, kept_head = begin(*terms[:2])
     pieces = [None] * len(kept)
-    lags = [1] * len(pieces)
+    lags = []
 
     def start(at, turn):
         goes, kept = halves(pieces[at], levels[turn - lags[at]])
@@ -668,15 +674,18 @@
     token_parts = [swap(part[0], "seq", 2 * at) for at, part in enumerate(sent, 1)]
     came_head = swap(goes_head, "batch", 1)
 
-    turn, out_part = 0, None
+    merged = direct and ratio == pairs
+    turn, out_at = 0, 0 if merged else pairs - 1
     while turn < 2 + len(levels):
         transfers = [came for _, _, came in moving]
         if turn == 0:
             came_terms, came_out, sent_after = phase(came_terms, came_out, sent_after)
             pieces = [joined(*both) for both in zip(kept, came_terms)]
+            pieces.append(joined(kept_out, came_out))
+            if merged:
+                pieces = [{p: jnp.concatenate([part[p] for part in pieces], axis=0) for p in even}]
             later_parts = [swap(part[1], "seq", 2 * at) for at, part in enumerate(sent_after, 1)]
-            pieces.append(joined(kept_out, came_out))
-            lags.append(1)
+            lags = [1] * len(pieces)
         elif turn == 1:
             transfers, came_head, token_parts = phase(transfers, came_head, token_parts)
             pieces.append(joined(kept_head, came_head))
@@ -690,13 +699,20 @@
         turn += 1
         moving = [start(at, turn) for at in due(turn)]
         if turn == 1 + len(levels):
-            out_part = to_owner(pieces[pairs - 1][0])[None]
+            out_sum, head_sums = pieces[out_at][0], []
+            if merged:
+                top = 3 * BLK * (pairs - 1)
+                head_sums = [out_sum[at : at + 3 * BLK] for at in range(0, top, 3 * BLK)]
+                out_sum = side_by_side(
+                    [out_sum[at : at + BLK] for at in range(top, top + head_width, BLK)]
+                )
+            out_part = to_owner(out_sum)[None]
 
     grad_hidden = partial
     for both in zip(token_parts, later_parts):
         grad_hidden = grad_hidden + jnp.concatenate(both, axis=0).astype(F32)
     grad_hidden = grad_hidden.astype(BF)
-    head_sums = [pieces[at][0] for at in range(len(pieces)) if at != pairs - 1]
+    head_sums += [pieces[at][0] for at in range(len(pieces)) if at != out_at]
     row_block = width // batch_count
     head_part = jnp.stack([part.reshape(3, BLK, row_block) for part in head_sums], axis=1)
     head_part = head_part.reshape(3, head_width, row_block).transpose(0, 2, 1)

time: 113 us -> 110 us (0.973)
  starting transfers between devices: 20.4 us -> 18.9 us
    ppermute x23 -> x21, starting transfers between devices: 18.1 us -> 15.6 us  [swap(): lax.ppermute(value, axis, [(at, at ^ distance) for at in range(count)])]
    ppermute x1, waiting for transfers between devices: 6.48 us -> 5.32 us  [to_owner(): return lax.ppermute(block_sum, ('seq', 'batch'), moves)]
    ppermute x23 -> x21, waiting for transfers between devices: 23 us -> 24.1 us  [swap(): lax.ppermute(value, axis, [(at, at ^ distance) for at in range(count)])]
  transfers between devices with their start and end apart: 24 -> 22, of which waited for: 13 -> 12; matrix products, arithmetic and copies ran while one was open for 8% -> 8% of each run, Pallas kernels for 45% -> 46%
where the time goes in v4:
time: 110 us
  Pallas kernels  50.4 us (46%)
  waiting for transfers between devices  29.4 us (27%)
  starting transfers between devices  18.9 us (17%)
  matrix products  6.5 us (6%)
  local copies, waits for them, and re-layouts  2.44 us (2%)
  other arithmetic  1.37 us (1%)
    pallas_call x6, Pallas kernels, run(): pl.pallas_call(kernel, in_specs=[pl.BlockSpec(memory_space=pltpu.SMEM)] *...  50.4 us
    ppermute x21, waiting for transfers between devices, swap(): lax.ppermute(value, axis, [(at, at ^ distance) for at in range(count)])  24.1 us
    ppermute x21, starting transfers between devices, swap(): lax.ppermute(value, axis, [(at, at ^ distance) for at in range(count)])  15.6 us
    ppermute x1, waiting for transfers between devices, to_owner(): return lax.ppermute(block_sum, ('seq', 'batch'), moves)  5.32 us
    dot_general x4, matrix products, per_device(): jnp.dot(parts[pair][:row_count], weight, preferred_element_type=F32)  4.26 us
    ppermute x1, starting transfers between devices, to_owner(): return lax.ppermute(block_sum, ('seq', 'batch'), moves)  3.34 us
    dot_general x1, matrix products, per_device(): jnp.dot(mate, mate_rows[(pairs - 1) * 3 * BLK:], preferred_element_type=F32)  2.23 us
  transfers between devices with their start and end apart: 22, of which 12 were waited for; matrix products, arithmetic and copies ran while one was open for 8% of the time, Pallas kernels for 46%

profile of v4, /device:TPU:4, one launch (start us, length us, event | category | flops | bytes accessed | tf_op | source)
XLA Modules:
  0.0 110.0 jit_solution(8734762016712483435)
XLA Ops:
  1.2 2.8 %weight_rows.3.refs_1_.refs_2_.refs_27_ = bf16[768,1024]{1,0:T(8,128)(2,1)} custom-call(s32[1]{0:T(128)} %bitcast.3.refs_0_, bf16[1024,1024]{1,0:T(8,128)(2,1)} %refs_1_.3, bf16[1024,1024]{1,0:T(8,128)(2,1)} %refs_2_.4, bf16[1024,1024]{1,0:T(8,128)(2,1)} %refs_3_.4), custom_call_target="tpu_custom_call" | custom-call | flops 1 | bytes 1 | tf_op jit(solution)/shard_map/weight_rows/pallas_call | solution.py:109
  4.1 2.8 %weight_rows.2.refs_26_ = bf16[768,1024]{1,0:T(8,128)(2,1)} custom-call(s32[1]{0:T(128)} %bitcast.1.refs_0_, bf16[1024,1024]{1,0:T(8,128)(2,1)} %refs_1_.3, bf16[1024,1024]{1,0:T(8,128)(2,1)} %refs_2_.4, bf16[1024,1024]{1,0:T(8,128)(2,1)} %refs_3_.4), custom_call_target="tpu_custom_call" | custom-call | flops 1 | bytes 1 | tf_op jit(solution)/shard_map/weight_rows/pallas_call | solution.py:109
  8.5 8.4 %project.1 = (bf16[256,768]{1,0:T(8,128)(2,1)}, bf16[256,768]{1,0:T(8,128)(2,1)}, bf16[256,768]{1,0:T(8,128)(2,1)}, bf16[256,768]{1,0:T(8,128)(2,1)}, bf16[768,2...) custom-call(s32[28]{0:T(128)} %concatenate.36.refs_0_, ...), custom_call_target="tpu_custom_call" | custom-call | flops 1 | bytes 1 | tf_op jit(solution)/shard_map/project/pallas_call | solution.py:109
  16.9 4.1 %collective-permute-done.refs_3_.refs_14_ = bf16[384,1024]{1,0:T(8,128)(2,1)} collective-permute-done((bf16[384,1024]{1,0:T(8,128)(2,1)}, bf16[384,1024]{1,0:T(8,128)(2,1)}, u32[]{:S(2)}, u32[]{:S(2)}) %collective-permute-start) | collective-permute-done | bytes 786464 | tf_op jit(solution)/shard_map/ppermute | solution.py:25
  21.3 1.7 %collective-permute-start.4 = (bf16[256,384]{1,0:T(8,128)(2,1)}, bf16[256,384]{1,0:T(8,128)(2,1)S(1)}, u32[]{:S(2)}, u32[]{:S(2)}) collective-permute-start(bf16[256,384]{1,0:T(8,128)(2,1)} %get-tuple-element.130), channel_id=1, source_target_pairs={{0,16},{8,24},{16,0},{24,8},{1,17},{9,25},{17,1},{25,9},{2,18},{10... | collective-permute-start | bytes 589832 | tf_op jit(solution)/shard_map/ppermute | solution.py:25
  23.7 14.2 %own_half.1 = (bf16[256,768]{1,0:T(8,128)(2,1)}, bf16[256,1536]{1,0:T(8,128)(2,1)}, bf16[256,1536]{1,0:T(8,128)(2,1)}, bf16[1536,256]{1,0:T(8,128)(2,1)}, bf16[1...) custom-call(s32[28]{0:T(128)} %concatenate.36.refs_0_, ...), custom_call_target="tpu_custom_call" | custom-call | flops 1 | bytes 1 | tf_op jit(solution)/shard_map/own_half/pallas_call | solution.py:109
  37.9 2.9 %collective-permute-done.5.refs_3_ = bf16[256,384]{1,0:T(8,128)(2,1)S(1)} collective-permute-done((bf16[256,384]{1,0:T(8,128)(2,1)}, bf16[256,384]{1,0:T(8,128)(2,1)S(1)}, u32[]{:S(2)}, u32[]{:S(2)}) %collective-permute-start.5) | collective-permute-done | bytes 196640 | tf_op jit(solution)/shard_map/ppermute | solution.py:25
  41.5 9.7 %later_half.2 = (bf16[128,768]{1,0:T(8,128)(2,1)}, bf16[768,384]{1,0:T(8,128)(2,1)}, bf16[768,384]{1,0:T(8,128)(2,1)}, bf16[384,512]{1,0:T(8,128)(2,1)}, f32[384,512]{1,0:T(8,128)}) custom-call(s32[28]{0:T(128)} %concatenate.36.refs_0_, s32[192]{0:T(256)} %reshape_squeeze.3.refs_1_, bf16[256,384]{1,0:T(8,128)(2,1)} %copy-done.3, bf16[256,384]{1,0:T(8,128)(2,1)} %copy-done.4, ...), custom_call_target="tpu_custom_call" | custom-call | flops 1 | bytes 1 | tf_op jit(solution)/shard_map/later_half/pallas_call | solution.py:109
  51.2 1.2 %collective-permute-done.8.refs_19_ = bf16[192,1024]{1,0:T(8,128)(2,1)} collective-permute-done((bf16[192,1024]{1,0:T(8,128)(2,1)}, bf16[192,1024]{1,0:T(8,128)(2,1)}, u32[]{:S(2)}, u32[]{:S(2)}) %collective-permute-start.8) | collective-permute-done | bytes 393248 | tf_op jit(solution)/shard_map/ppermute | solution.py:25
  52.9 1.5 %collective-permute-start.11 = (bf16[384,512]{1,0:T(8,128)(2,1)}, bf16[384,512]{1,0:T(8,128)(2,1)S(1)}, u32[]{:S(2)}, u32[]{:S(2)}) collective-permute-start(bf16[384,512]{1,0:T(8,128)(2,1)} %get-tuple-element.178), channel_id=1, source_target_pairs={{0,1},{1,0},{2,3},{3,2},{4,5},{5,4},{6,7},{7,6},{8,9},{9,8},{10,11... | collective-permute-start | bytes 1179656 | tf_op jit(solution)/shard_map/ppermute | solution.py:25
  55.3 12.4 %later_half.3 = (bf16[128,768]{1,0:T(8,128)(2,1)}, bf16[768,384]{1,0:T(8,128)(2,1)}, bf16[768,384]{1,0:T(8,128)(2,1)}, bf16[384,512]{1,0:T(8,128)(2,1)}, f32[384...) custom-call(s32[28]{0:T(128)} %concatenate.36.refs_0_, ...), custom_call_target="tpu_custom_call" | custom-call | flops 1 | bytes 1 | tf_op jit(solution)/shard_map/later_half/pallas_call | solution.py:109
  67.9 1.5 %collective-permute-start.13 = (bf16[256,512]{1,0:T(8,128)(2,1)}, bf16[256,512]{1,0:T(8,128)(2,1)S(1)}, u32[]{:S(2)}, u32[]{:S(2)}) collective-permute-start(bf16[256,512]{1,0:T(8,128)(2,1)} %get-tuple-element.188), channel_id=1, source_target_pairs={{0,1},{1,0},{2,3},{3,2},{4,5},{5,4},{6,7},{7,6},{8,9},{9,8},{10,11... | collective-permute-start | bytes 786440 | tf_op jit(solution)/shard_map/ppermute | solution.py:25
  70.0 2.2 %add_convert_fusion.1 = bf16[384,1024]{1,0:T(8,128)(2,1)S(1)} fusion(f32[384,1024]{1,0:T(8,128)} %get-tuple-element.181, bf16[768,1024]{1,0:T(8,128)(2,1)} %weight_rows.2.refs_26_, bf16[768,384]{1,0:T(8,128)(2,1)S(1)} %collective-permute-done.12), kind=kOutput, calls=%fused_computation.1 | convolution fusion | flops 302776320 | bytes 3440640 | tf_op jit(solution)/shard_map/dot_general | solution.py:663
  72.9 4.4 %collective-permute-done.13 = bf16[256,512]{1,0:T(8,128)(2,1)S(1)} collective-permute-done((bf16[256,512]{1,0:T(8,128)(2,1)}, bf16[256,512]{1,0:T(8,128)(2,1)S(1)}, u32[]{:S(2)}, u32[]{:S(2)}) %collective-permute-start.13) | collective-permute-done | bytes 262176 | tf_op jit(solution)/shard_map/ppermute | solution.py:25
  77.5 1.6 %collective-permute-start.14 = (bf16[640,256]{1,0:T(8,128)(2,1)S(1)}, bf16[640,256]{1,0:T(8,128)(2,1)S(1)}, u32[]{:S(2)}, u32[]{:S(2)}) collective-permute-start(bf16[640,256]{1,0:T(8,128)(2,1)S(1)} %maximum_maximum_fusion), channel_id=1, source_target_pairs={{0,2},{1,3},{2,0},{3,1},{4,6},{5,7},{6,4},{7,5},{8,10},{9,11},{10,... | collective-permute-start | bytes 983048 | tf_op jit(solution)/shard_map/ppermute | solution.py:25
  80.8 4.3 %collective-permute-done.15 = bf16[384,512]{1,0:T(8,128)(2,1)S(1)} collective-permute-done((bf16[384,512]{1,0:T(8,128)(2,1)}, bf16[384,512]{1,0:T(8,128)(2,1)S(1)}, u32[]{:S(2)}, u32[]{:S(2)}) %collective-permute-start.15) | collective-permute-done | bytes 393248 | tf_op jit(solution)/shard_map/ppermute | solution.py:25
  86.2 2.8 %collective-permute-start.17 = (bf16[640,128]{1,0:T(8,128)(2,1)S(1)}, bf16[640,128]{1,0:T(8,128)(2,1)S(1)}, u32[]{:S(2)}, u32[]{:S(2)}) collective-permute-start(bf16[640,128]{1,0:T(8,128)(2,1)S(1)} %fusion.12), channel_id=1, source_target_pairs={{0,4},{1,5},{2,6},{3,7},{4,0},{5,1},{6,2},{7,3},{8,12},{9,13},{10,... | collective-permute-start | bytes 491528 | tf_op jit(solution)/shard_map/ppermute | solution.py:25
  89.1 1.7 %collective-permute-start.18 = (bf16[384,256]{1,0:T(8,128)(2,1)S(1)}, bf16[384,256]{1,0:T(8,128)(2,1)S(1)}, u32[]{:S(2)}, u32[]{:S(2)}) collective-permute-start(bf16[384,256]{1,0:T(8,128)(2,1)S(1)} %pad_maximum_fusion.1), channel_id=1, source_target_pairs={{0,2},{1,3},{2,0},{3,1},{4,6},{5,7},{6,4},{7,5},{8,10},{9,11},{10,... | collective-permute-start | bytes 589832 | tf_op jit(solution)/shard_map/ppermute | solution.py:25
  90.7 1.5 %fusion.5 = f32[384,1024]{1,0:T(8,128)S(1)} fusion(bf16[768,1024]{1,0:T(8,128)(2,1)S(1)} %copy-done.1, bf16[768,384]{1,0:T(8,128)(2,1)} %collective-permute-done.10.refs_25_), kind=kOutput, calls=%fused_computation.7 | convolution fusion | flops 301989888 | bytes 2654208 | tf_op jit(solution)/shard_map/dot_general | solution.py:673
  92.3 3.2 %collective-permute-done.17 = bf16[640,128]{1,0:T(8,128)(2,1)S(1)} collective-permute-done((bf16[640,128]{1,0:T(8,128)(2,1)S(1)}, bf16[640,128]{1,0:T(8,128)(2,1)S(1)}, u32[]{:S(2)}, u32[]{:S(2)}) %collective-permute-start.17) | collective-permute-done | bytes 163872 | tf_op jit(solution)/shard_map/ppermute | solution.py:25
  96.6 1.3 %collective-permute-start.20 = (bf16[384,128]{1,0:T(8,128)(2,1)S(1)}, bf16[384,128]{1,0:T(8,128)(2,1)S(1)}, u32[]{:S(2)}, u32[]{:S(2)}) collective-permute-start(bf16[384,128]{1,0:T(8,128)(2,1)S(1)} %add_convert_fusion.2), channel_id=1, source_target_pairs={{0,4},{1,5},{2,6},{3,7},{4,0},{5,1},{6,2},{7,3},{8,12},{9,13},{10,... | collective-permute-start | bytes 294920 | tf_op jit(solution)/shard_map/ppermute | solution.py:25
  98.0 3.3 %collective-permute-start.21 = (f32[128,256]{1,0:T(8,128)S(1)}, f32[128,256]{1,0:T(8,128)S(1)}, u32[]{:S(2)}, u32[]{:S(2)}) collective-permute-start(f32[128,256]{1,0:T(8,128)S(1)} %pad_maximum_fusion.2), channel_id=1, source_target_pairs={{0,0},{1,1},{2,8},{3,9},{4,16},{5,17},{6,24},{7,25},{8,2},{9,3},{1... | collective-permute-start | bytes 393224 | tf_op jit(solution)/shard_map/ppermute | solution.py:519
  101.3 1.6 %fusion = bf16[1,384,1024]{2,1,0:T(8,128)(2,1)} fusion(f32[384,1024]{1,0:T(8,128)S(1)} %fusion.1, f32[384,1024]{1,0:T(8,128)S(1)} %fusion.3, f32[384,1024]{1,0:T(8,128)S(1)} %fusion.5, bf16[192,1024]{1,0:T(8,128)(2,1)S(1)} %collective-permute-done.19, bf16[192,1024]{1,0:T(8,128)(2,1)S(1)} %collective-permute-done.16, bf16[768,1024]{1,0:T(8,128)(2,1)S(1)} %copy-done.1, ...), kind=kOutput, calls=%fused_computation.2 | convolution fusion | flops 305528832 | bytes 7372800 | tf_op jit(solution)/shard_map/dot_general | solution.py:673
  103.9 5.3 %collective-permute-done.21 = f32[128,256]{1,0:T(8,128)S(1)} collective-permute-done((f32[128,256]{1,0:T(8,128)S(1)}, f32[128,256]{1,0:T(8,128)S(1)}, u32[]{:S(2)}, u32[]{:S(2)}) %collective-permute-start.21) | collective-permute-done | bytes 131104 | tf_op jit(solution)/shard_map/ppermute | solution.py:519
  (78 shorter events, 12.5 us)
Async XLA Ops:
  0.6 7.8 %collective-permute-start.1 = (bf16[384,1024]{1,0:T(8,128)(2,1)}, bf16[384,1024]{1,0:T(8,128)(2,1)}, u32[]{:S(2)}, u32[]{:S(2)}) collective-permute-start(bf16[384,1024]{1,0:T(8,128)(2,1)} %bitcast.13), channel_id=1, source_target_pairs={{0,8},{8,0},{16,24},{24,16},{1,9},{9,1},{17,25},{25,17},{2,10},{10... | collective-permute-start | bytes 2359304 | tf_op jit(solution)/shard_map/ppermute | solution.py:25
  0.7 7.7 %collective-permute-start.2 = (bf16[384,1024]{1,0:T(8,128)(2,1)}, bf16[384,1024]{1,0:T(8,128)(2,1)}, u32[]{:S(2)}, u32[]{:S(2)}) collective-permute-start(bf16[384,1024]{1,0:T(8,128)(2,1)} %bitcast.18), channel_id=1, source_target_pairs={{0,8},{8,0},{16,24},{24,16},{1,9},{9,1},{17,25},{25,17},{2,10},{10... | collective-permute-start | bytes 2359304 | tf_op jit(solution)/shard_map/ppermute | solution.py:25
  1.2 19.8 %collective-permute-start = (bf16[384,1024]{1,0:T(8,128)(2,1)}, bf16[384,1024]{1,0:T(8,128)(2,1)}, u32[]{:S(2)}, u32[]{:S(2)}) collective-permute-start(bf16[384,1024]{1,0:T(8,128)(2,1)} %bitcast.14), channel_id=1, source_target_pairs={{0,16},{8,24},{16,0},{24,8},{1,17},{9,25},{17,1},{25,9},{2,18},{10... | collective-permute-start | bytes 2359304 | tf_op jit(solution)/shard_map/ppermute | solution.py:25
  21.0 2.6 %collective-permute-start.3 = (bf16[384,1024]{1,0:T(8,128)(2,1)}, bf16[384,1024]{1,0:T(8,128)(2,1)}, u32[]{:S(2)}, u32[]{:S(2)}) collective-permute-start(bf16[384,1024]{1,0:T(8,128)(2,1)} %collective-permute-done.refs_3_.refs_14_), channel_id=1, source_target_pairs={{0,8},{8,0},{16,24},{24,16},{1,9},{9,1},{17,25},{25,17},{2,10},{10... | collective-permute-start | bytes 2359304 | tf_op jit(solution)/shard_map/ppermute | solution.py:25
  21.1 19.8 %collective-permute-start.6 = (bf16[192,1024]{1,0:T(8,128)(2,1)}, bf16[192,1024]{1,0:T(8,128)(2,1)}, u32[]{:S(2)}, u32[]{:S(2)}) collective-permute-start(bf16[192,1024]{1,0:T(8,128)(2,1)} %get-tuple-element.132), channel_id=1, source_target_pairs={{0,16},{8,24},{16,0},{24,8},{1,17},{9,25},{17,1},{25,9},{2,18},{10... | collective-permute-start | bytes 1179656 | tf_op jit(solution)/shard_map/ppermute | solution.py:25
  21.3 16.6 %collective-permute-start.4 = (bf16[256,384]{1,0:T(8,128)(2,1)}, bf16[256,384]{1,0:T(8,128)(2,1)S(1)}, u32[]{:S(2)}, u32[]{:S(2)}) collective-permute-start(bf16[256,384]{1,0:T(8,128)(2,1)} %get-tuple-element.130), channel_id=1, source_target_pairs={{0,16},{8,24},{16,0},{24,8},{1,17},{9,25},{17,1},{25,9},{2,18},{10... | collective-permute-start | bytes 589832 | tf_op jit(solution)/shard_map/ppermute | solution.py:25
  23.1 17.7 %collective-permute-start.5 = (bf16[256,384]{1,0:T(8,128)(2,1)}, bf16[256,384]{1,0:T(8,128)(2,1)S(1)}, u32[]{:S(2)}, u32[]{:S(2)}) collective-permute-start(bf16[256,384]{1,0:T(8,128)(2,1)} %get-tuple-element.131), channel_id=1, source_target_pairs={{0,24},{8,16},{16,8},{24,0},{1,25},{9,17},{17,9},{25,1},{2,26},{10... | collective-permute-start | bytes 589832 | tf_op jit(solution)/shard_map/ppermute | solution.py:25
  40.8 11.5 %collective-permute-start.8 = (bf16[192,1024]{1,0:T(8,128)(2,1)}, bf16[192,1024]{1,0:T(8,128)(2,1)}, u32[]{:S(2)}, u32[]{:S(2)}) collective-permute-start(bf16[192,1024]{1,0:T(8,128)(2,1)} %get-tuple-element.150), channel_id=1, source_target_pairs={{0,16},{8,24},{16,0},{24,8},{1,17},{9,25},{17,1},{25,9},{2,18},{10... | collective-permute-start | bytes 1179656 | tf_op jit(solution)/shard_map/ppermute | solution.py:25
  41.1 11.3 %collective-permute-start.7 = (bf16[192,1024]{1,0:T(8,128)(2,1)}, bf16[192,1024]{1,0:T(8,128)(2,1)}, u32[]{:S(2)}, u32[]{:S(2)}) collective-permute-start(bf16[192,1024]{1,0:T(8,128)(2,1)} %collective-permute-done.6.refs_18_), channel_id=1, source_target_pairs={{0,8},{8,0},{16,24},{24,16},{1,9},{9,1},{17,25},{25,17},{2,10},{10... | collective-permute-start | bytes 1179656 | tf_op jit(solution)/shard_map/ppermute | solution.py:25
  52.4 2.9 %collective-permute-start.10 = (bf16[768,384]{1,0:T(8,128)(2,1)}, bf16[768,384]{1,0:T(8,128)(2,1)}, u32[]{:S(2)}, u32[]{:S(2)}) collective-permute-start(bf16[768,384]{1,0:T(8,128)(2,1)} %get-tuple-element.163), channel_id=1, source_target_pairs={{0,8},{8,0},{16,24},{24,16},{1,9},{9,1},{17,25},{25,17},{2,10},{10... | collective-permute-start | bytes 1769480 | tf_op jit(solution)/shard_map/ppermute | solution.py:25
  52.4 2.9 %collective-permute-start.9 = (bf16[192,1024]{1,0:T(8,128)(2,1)}, bf16[192,1024]{1,0:T(8,128)(2,1)}, u32[]{:S(2)}, u32[]{:S(2)}) collective-permute-start(bf16[192,1024]{1,0:T(8,128)(2,1)} %collective-permute-done.8.refs_19_), channel_id=1, source_target_pairs={{0,8},{8,0},{16,24},{24,16},{1,9},{9,1},{17,25},{25,17},{2,10},{10... | collective-permute-start | bytes 1179656 | tf_op jit(solution)/shard_map/ppermute | solution.py:25
  52.9 14.8 %collective-permute-start.11 = (bf16[384,512]{1,0:T(8,128)(2,1)}, bf16[384,512]{1,0:T(8,128)(2,1)S(1)}, u32[]{:S(2)}, u32[]{:S(2)}) collective-permute-start(bf16[384,512]{1,0:T(8,128)(2,1)} %get-tuple-element.178), channel_id=1, source_target_pairs={{0,1},{1,0},{2,3},{3,2},{4,5},{5,4},{6,7},{7,6},{8,9},{9,8},{10,11... | collective-permute-start | bytes 1179656 | tf_op jit(solution)/shard_map/ppermute | solution.py:25
  67.7 2.3 %collective-permute-start.12 = (bf16[768,384]{1,0:T(8,128)(2,1)}, bf16[768,384]{1,0:T(8,128)(2,1)S(1)}, u32[]{:S(2)}, u32[]{:S(2)}) collective-permute-start(bf16[768,384]{1,0:T(8,128)(2,1)} %get-tuple-element.180), channel_id=1, source_target_pairs={{0,8},{8,0},{16,24},{24,16},{1,9},{9,1},{17,25},{25,17},{2,10},{10... | collective-permute-start | bytes 1769480 | tf_op jit(solution)/shard_map/ppermute | solution.py:25
  67.9 9.4 %collective-permute-start.13 = (bf16[256,512]{1,0:T(8,128)(2,1)}, bf16[256,512]{1,0:T(8,128)(2,1)S(1)}, u32[]{:S(2)}, u32[]{:S(2)}) collective-permute-start(bf16[256,512]{1,0:T(8,128)(2,1)} %get-tuple-element.188), channel_id=1, source_target_pairs={{0,1},{1,0},{2,3},{3,2},{4,5},{5,4},{6,7},{7,6},{8,9},{9,8},{10,11... | collective-permute-start | bytes 786440 | tf_op jit(solution)/shard_map/ppermute | solution.py:25
  69.4 15.8 %collective-permute-start.15 = (bf16[384,512]{1,0:T(8,128)(2,1)}, bf16[384,512]{1,0:T(8,128)(2,1)S(1)}, u32[]{:S(2)}, u32[]{:S(2)}) collective-permute-start(bf16[384,512]{1,0:T(8,128)(2,1)} %get-tuple-element.193), channel_id=1, source_target_pairs={{0,1},{1,0},{2,3},{3,2},{4,5},{5,4},{6,7},{7,6},{8,9},{9,8},{10,11... | collective-permute-start | bytes 1179656 | tf_op jit(solution)/shard_map/ppermute | solution.py:25
  72.3 13.8 %collective-permute-start.16 = (bf16[192,1024]{1,0:T(8,128)(2,1)S(1)}, bf16[192,1024]{1,0:T(8,128)(2,1)S(1)}, u32[]{:S(2)}, u32[]{:S(2)}) collective-permute-start(bf16[192,1024]{1,0:T(8,128)(2,1)S(1)} %get-tuple-element.213), channel_id=1, source_target_pairs={{0,16},{8,24},{16,0},{24,8},{1,17},{9,25},{17,1},{25,9},{2,18},{10... | collective-permute-start | bytes 1179656 | tf_op jit(solution)/shard_map/ppermute | solution.py:25
  77.5 8.7 %collective-permute-start.14 = (bf16[640,256]{1,0:T(8,128)(2,1)S(1)}, bf16[640,256]{1,0:T(8,128)(2,1)S(1)}, u32[]{:S(2)}, u32[]{:S(2)}) collective-permute-start(bf16[640,256]{1,0:T(8,128)(2,1)S(1)} %maximum_maximum_fusion), channel_id=1, source_target_pairs={{0,2},{1,3},{2,0},{3,1},{4,6},{5,7},{6,4},{7,5},{8,10},{9,11},{10,... | collective-permute-start | bytes 983048 | tf_op jit(solution)/shard_map/ppermute | solution.py:25
  79.1 13.2 %collective-permute-start.19 = (bf16[192,1024]{1,0:T(8,128)(2,1)S(1)}, bf16[192,1024]{1,0:T(8,128)(2,1)S(1)}, u32[]{:S(2)}, u32[]{:S(2)}) collective-permute-start(bf16[192,1024]{1,0:T(8,128)(2,1)S(1)} %get-tuple-element.198), channel_id=1, source_target_pairs={{0,16},{8,24},{16,0},{24,8},{1,17},{9,25},{17,1},{25,9},{2,18},{10... | collective-permute-start | bytes 1179656 | tf_op jit(solution)/shard_map/ppermute | solution.py:25
  80.2 8.7 %copy-start.6 = (f32[384,512]{1,0:T(8,128)S(1)}, f32[384,512]{1,0:T(8,128)}, u32[]{:S(2)}) copy-start(f32[384,512]{1,0:T(8,128)} %get-tuple-element.196) | copy-start | bytes 2359300
  80.8 9.9 %copy-start.1 = (bf16[768,1024]{1,0:T(8,128)(2,1)S(1)}, bf16[768,1024]{1,0:T(8,128)(2,1)}, u32[]{:S(2)}) copy-start(bf16[768,1024]{1,0:T(8,128)(2,1)} %weight_rows.2.refs_26_) | copy-start | bytes 4718596
  86.2 9.2 %collective-permute-start.17 = (bf16[640,128]{1,0:T(8,128)(2,1)S(1)}, bf16[640,128]{1,0:T(8,128)(2,1)S(1)}, u32[]{:S(2)}, u32[]{:S(2)}) collective-permute-start(bf16[640,128]{1,0:T(8,128)(2,1)S(1)} %fusion.12), channel_id=1, source_target_pairs={{0,4},{1,5},{2,6},{3,7},{4,0},{5,1},{6,2},{7,3},{8,12},{9,13},{10,... | collective-permute-start | bytes 491528 | tf_op jit(solution)/shard_map/ppermute | solution.py:25
  89.1 7.5 %collective-permute-start.18 = (bf16[384,256]{1,0:T(8,128)(2,1)S(1)}, bf16[384,256]{1,0:T(8,128)(2,1)S(1)}, u32[]{:S(2)}, u32[]{:S(2)}) collective-permute-start(bf16[384,256]{1,0:T(8,128)(2,1)S(1)} %pad_maximum_fusion.1), channel_id=1, source_target_pairs={{0,2},{1,3},{2,0},{3,1},{4,6},{5,7},{6,4},{7,5},{8,10},{9,11},{10,... | collective-permute-start | bytes 589832 | tf_op jit(solution)/shard_map/ppermute | solution.py:25
  96.6 6.6 %collective-permute-start.20 = (bf16[384,128]{1,0:T(8,128)(2,1)S(1)}, bf16[384,128]{1,0:T(8,128)(2,1)S(1)}, u32[]{:S(2)}, u32[]{:S(2)}) collective-permute-start(bf16[384,128]{1,0:T(8,128)(2,1)S(1)} %add_convert_fusion.2), channel_id=1, source_target_pairs={{0,4},{1,5},{2,6},{3,7},{4,0},{5,1},{6,2},{7,3},{8,12},{9,13},{10,... | collective-permute-start | bytes 294920 | tf_op jit(solution)/shard_map/ppermute | solution.py:25
  98.0 11.2 %collective-permute-start.21 = (f32[128,256]{1,0:T(8,128)S(1)}, f32[128,256]{1,0:T(8,128)S(1)}, u32[]{:S(2)}, u32[]{:S(2)}) collective-permute-start(f32[128,256]{1,0:T(8,128)S(1)} %pad_maximum_fusion.2), channel_id=1, source_target_pairs={{0,0},{1,1},{2,8},{3,9},{4,16},{5,17},{6,24},{7,25},{8,2},{9,3},{1... | collective-permute-start | bytes 393224 | tf_op jit(solution)/shard_map/ppermute | solution.py:519
  (9 other events, 37.0 us)

commit v5 on v4

--- a/solution.py
+++ b/solution.py
@@ -340,7 +340,7 @@
 
 
 def later_half(
-    plan, offsets, order_at, far_grads_t, pair, first, tokens, grads, attended, before, rows, mate_rows
+    plan, offsets, order_at, far_grads_t, pair, first, tokens, grads, attended, before, rows
 ):
     width, half = first[0].shape
     heads, blocks, slots = offsets.shape
@@ -402,11 +402,7 @@
             sent.start(at)
         if final:
             parts = [(sent[1], shares_here[-1], pair)]
-            parts += [
-                (shares_here[2 * at + side], shares_here[-1 - side], at)
-                for at in range(len(before))
-                for side in (1, 0)
-            ]
+            parts += [(shares_here[at], shares_here[-1], at) for at in range(len(before))]
             lefts = [left()[...] if isinstance(left, Held) else left[step:, :] for left, _, _ in parts]
             left = jnp.concatenate(lefts, axis=1)
             model_n = rows.shape[1]
@@ -435,8 +431,8 @@
                     )
                 target, cols = sent[at + col // (model // 2)], col % (model // 2)
                 target[:, cols : cols + 2 * BLK] = terms.astype(target.dtype)
-                if cols + 2 * BLK == model // 2:
-                    sent.start(at + col // (model // 2))
+                part = (slice(0, target.shape[0]), slice(cols, cols + 2 * BLK))
+                sent.start(at + col // (model // 2), part)
 
         if last:
             lefts = [attended_here[0]()[...]]
@@ -476,14 +472,12 @@
     if final:
         results += [((half - step, model), F32)]
         far_places = (slice(step, half), slice(0, 3 * BLK))
-        operands += [(part, far_places) for both in before for part in both]
-        if before:
-            operands += [(mate_rows, (slice(0, len(before) * 3 * BLK), slice(0, model)))]
+        operands += [(part, far_places) for part in before]
         operands += [(rows, None)]
     if last:
         results += [((width, model // 2), BF), ((width, model // 2), F32)]
     scratch = [pltpu.VMEM((BLK, half), BF)] + [pltpu.VMEM((3 * BLK, half), BF)] * 2
-    return run(body, "later_half", [plan, offsets.reshape(-1)], operands, results, scratch, 8)
+    return run(body, "later_half", [plan, offsets.reshape(-1)], operands, results, scratch, 6 + model // (2 * BLK))
 
 
 def halves(pieces, low):
@@ -610,7 +604,6 @@
         all_grads = []
         if last:
             late = spread(late, "seq", half_count)
-            late, came = phase(late, came)
             all_grads = near_grads + [part for both in zip(early, late) for part in both]
         far_attended, stay, leave, *terms = later_half(
             plan,
@@ -622,12 +615,11 @@
             all_tokens,
             all_grads if direct and ratio == pairs else [],
             [first[5], *attended] if last and direct and ratio == pairs else [],
-            list(zip(stayed, came)),
+            stayed,
             rows if last else None,
-            mate_rows,
         )
         if last:
-            stay, leave, terms, came_terms = phase(stay, leave, terms, came_terms)
+            stay, leave, terms, came_terms, came = phase(stay, leave, terms, came_terms, came)
         else:
             stay, leave, terms, far_attended, early, late, first = phase(
                 stay, leave, terms, far_attended, early, late, first
@@ -659,9 +651,11 @@
     held = [rows, mate_rows]
     sent = []
     for at in range(1, half_count):
-        mate = came[-1][at * row_count : (at + 1) * row_count]
-        total = jnp.dot(mate, mate_rows[(pairs - 1) * 3 * BLK :], preferred_element_type=F32)
-        total += terms[2][(at - 1) * row_count : at * row_count]
+        total = terms[2][(at - 1) * row_count : at * row_count]
+        for pair in range(pairs):
+            mate = came[pair][at * row_count : (at + 1) * row_count]
+            weight = mate_rows[pair * 3 * BLK : (pair + 1) * 3 * BLK]
+            total += jnp.dot(mate, weight, preferred_element_type=F32)
         sent.append(total.astype(BF))
     cut = row_count // 2
     sent = [(part[:cut], part[cut:]) for part in sent]

time: 110 us -> 110 us (level)
  waiting for transfers between devices: 29.4 us -> 27.7 us
  matrix products: 6.5 us -> 8.05 us
    ppermute x21, waiting for transfers between devices: 24.1 us -> 22.4 us  [swap(): lax.ppermute(value, axis, [(at, at ^ distance) for at in range(count)])]
    dot_general x1 -> x2, matrix products: 2.23 us -> 3.79 us  [per_device(): total += jnp.dot(mate, weight, preferred_element_type=F32)]
  transfers between devices with their start and end apart: 22 -> 22, of which waited for: 12 -> 13; matrix products, arithmetic and copies ran while one was open for 8% -> 10% of each run, Pallas kernels for 46% -> 46%
where the time goes in v5:
time: 110 us
  Pallas kernels  50.1 us (46%)
  waiting for transfers between devices  27.7 us (25%)
  starting transfers between devices  18.9 us (17%)
  matrix products  8.05 us (7%)
  local copies, waits for them, and re-layouts  2.47 us (2%)
  other arithmetic  1.37 us (1%)
    pallas_call x6, Pallas kernels, run(): pl.pallas_call(kernel, in_specs=[pl.BlockSpec(memory_space=pltpu.SMEM)] *...  50.1 us
    ppermute x21, waiting for transfers between devices, swap(): lax.ppermute(value, axis, [(at, at ^ distance) for at in range(count)])  22.4 us
    ppermute x21, starting transfers between devices, swap(): lax.ppermute(value, axis, [(at, at ^ distance) for at in range(count)])  15.7 us
    ppermute x1, waiting for transfers between devices, to_owner(): return lax.ppermute(block_sum, ('seq', 'batch'), moves)  5.24 us
    dot_general x4, matrix products, per_device(): jnp.dot(parts[pair][:row_count], weight, preferred_element_type=F32)  4.26 us
    dot_general x2, matrix products, per_device(): total += jnp.dot(mate, weight, preferred_element_type=F32)  3.79 us
    ppermute x1, starting transfers between devices, to_owner(): return lax.ppermute(block_sum, ('seq', 'batch'), moves)  3.17 us
  transfers between devices with their start and end apart: 22, of which 13 were waited for; matrix products, arithmetic and copies ran while one was open for 10% of the time, Pallas kernels for 46%

profile of v5, /device:TPU:4, one launch (start us, length us, event | category | flops | bytes accessed | tf_op | source)
XLA Modules:
  0.0 109.5 jit_solution(9358132275913989267)
XLA Ops:
  1.2 2.8 %weight_rows.3.refs_1_.refs_2_.refs_25_ = bf16[768,1024]{1,0:T(8,128)(2,1)} custom-call(s32[1]{0:T(128)} %bitcast.3.refs_0_, bf16[1024,1024]{1,0:T(8,128)(2,1)} %refs_1_.3, bf16[1024,1024]{1,0:T(8,128)(2,1)} %refs_2_.4, bf16[1024,1024]{1,0:T(8,128)(2,1)} %refs_3_.4), custom_call_target="tpu_custom_call" | custom-call | flops 1 | bytes 1 | tf_op jit(solution)/shard_map/weight_rows/pallas_call | solution.py:109
  4.1 2.8 %weight_rows.2 = bf16[768,1024]{1,0:T(8,128)(2,1)} custom-call(s32[1]{0:T(128)} %bitcast.1.refs_0_, bf16[1024,1024]{1,0:T(8,128)(2,1)} %refs_1_.3, bf16[1024,1024]{1,0:T(8,128)(2,1)} %refs_2_.4, bf16[1024,1024]{1,0:T(8,128)(2,1)} %refs_3_.4), custom_call_target="tpu_custom_call" | custom-call | flops 1 | bytes 1 | tf_op jit(solution)/shard_map/weight_rows/pallas_call | solution.py:109
  8.5 8.5 %project.1 = (bf16[256,768]{1,0:T(8,128)(2,1)}, bf16[256,768]{1,0:T(8,128)(2,1)}, bf16[256,768]{1,0:T(8,128)(2,1)}, bf16[256,768]{1,0:T(8,128)(2,1)}, bf16[768,2...) custom-call(s32[28]{0:T(128)} %concatenate.36.refs_0_, ...), custom_call_target="tpu_custom_call" | custom-call | flops 1 | bytes 1 | tf_op jit(solution)/shard_map/project/pallas_call | solution.py:109
  17.0 4.1 %collective-permute-done.refs_3_.refs_14_ = bf16[384,1024]{1,0:T(8,128)(2,1)} collective-permute-done((bf16[384,1024]{1,0:T(8,128)(2,1)}, bf16[384,1024]{1,0:T(8,128)(2,1)}, u32[]{:S(2)}, u32[]{:S(2)}) %collective-permute-start) | collective-permute-done | bytes 786464 | tf_op jit(solution)/shard_map/ppermute | solution.py:25
  21.3 1.7 %collective-permute-start.4 = (bf16[256,384]{1,0:T(8,128)(2,1)}, bf16[256,384]{1,0:T(8,128)(2,1)S(1)}, u32[]{:S(2)}, u32[]{:S(2)}) collective-permute-start(bf16[256,384]{1,0:T(8,128)(2,1)} %get-tuple-element.128), channel_id=1, source_target_pairs={{0,16},{8,24},{16,0},{24,8},{1,17},{9,25},{17,1},{25,9},{2,18},{10... | collective-permute-start | bytes 589832 | tf_op jit(solution)/shard_map/ppermute | solution.py:25
  23.7 14.3 %own_half.1 = (bf16[256,768]{1,0:T(8,128)(2,1)}, bf16[256,1536]{1,0:T(8,128)(2,1)}, bf16[256,1536]{1,0:T(8,128)(2,1)}, bf16[1536,256]{1,0:T(8,128)(2,1)}, bf16[1...) custom-call(s32[28]{0:T(128)} %concatenate.36.refs_0_, ...), custom_call_target="tpu_custom_call" | custom-call | flops 1 | bytes 1 | tf_op jit(solution)/shard_map/own_half/pallas_call | solution.py:109
  38.0 2.9 %collective-permute-done.5.refs_3_ = bf16[256,384]{1,0:T(8,128)(2,1)S(1)} collective-permute-done((bf16[256,384]{1,0:T(8,128)(2,1)}, bf16[256,384]{1,0:T(8,128)(2,1)S(1)}, u32[]{:S(2)}, u32[]{:S(2)}) %collective-permute-start.5) | collective-permute-done | bytes 196640 | tf_op jit(solution)/shard_map/ppermute | solution.py:25
  41.5 9.7 %later_half.2 = (bf16[128,768]{1,0:T(8,128)(2,1)}, bf16[768,384]{1,0:T(8,128)(2,1)}, bf16[768,384]{1,0:T(8,128)(2,1)}, bf16[384,512]{1,0:T(8,128)(2,1)}, f32[384,512]{1,0:T(8,128)}) custom-call(s32[28]{0:T(128)} %concatenate.36.refs_0_, s32[192]{0:T(256)} %reshape_squeeze.3.refs_1_, bf16[256,384]{1,0:T(8,128)(2,1)} %copy-done.3, bf16[256,384]{1,0:T(8,128)(2,1)} %copy-done.4, ...), custom_call_target="tpu_custom_call" | custom-call | flops 1 | bytes 1 | tf_op jit(solution)/shard_map/later_half/pallas_call | solution.py:109
  52.9 1.5 %collective-permute-start.10 = (bf16[384,512]{1,0:T(8,128)(2,1)}, bf16[384,512]{1,0:T(8,128)(2,1)S(1)}, u32[]{:S(2)}, u32[]{:S(2)}) collective-permute-start(bf16[384,512]{1,0:T(8,128)(2,1)} %get-tuple-element.171), channel_id=1, source_target_pairs={{0,1},{1,0},{2,3},{3,2},{4,5},{5,4},{6,7},{7,6},{8,9},{9,8},{10,11... | collective-permute-start | bytes 1179656 | tf_op jit(solution)/shard_map/ppermute | solution.py:25
  55.3 12.0 %later_half.3 = (bf16[128,768]{1,0:T(8,128)(2,1)}, bf16[768,384]{1,0:T(8,128)(2,1)}, bf16[768,384]{1,0:T(8,128)(2,1)}, bf16[384,512]{1,0:T(8,128)(2,1)}, f32[384...) custom-call(s32[28]{0:T(128)} %concatenate.36.refs_0_, ...), custom_call_target="tpu_custom_call" | custom-call | flops 1 | bytes 1 | tf_op jit(solution)/shard_map/later_half/pallas_call | solution.py:109
  67.5 1.5 %collective-permute-start.13 = (bf16[256,512]{1,0:T(8,128)(2,1)}, bf16[256,512]{1,0:T(8,128)(2,1)S(1)}, u32[]{:S(2)}, u32[]{:S(2)}) collective-permute-start(bf16[256,512]{1,0:T(8,128)(2,1)} %get-tuple-element.184), channel_id=1, source_target_pairs={{0,1},{1,0},{2,3},{3,2},{4,5},{5,4},{6,7},{7,6},{8,9},{9,8},{10,11... | collective-permute-start | bytes 786440 | tf_op jit(solution)/shard_map/ppermute | solution.py:25
  69.5 1.8 %fusion.15 = f32[384,1024]{1,0:T(8,128)S(1)} fusion(bf16[768,1024]{1,0:T(8,128)(2,1)} %weight_rows.2, bf16[768,384]{1,0:T(8,128)(2,1)} %collective-permute-done.11), kind=kOutput, calls=%fused_computation.13 | convolution fusion | flops 301989888 | bytes 2654208 | tf_op jit(solution)/shard_map/dot_general | solution.py:658
  71.3 2.0 %add_convert_fusion.1 = bf16[384,1024]{1,0:T(8,128)(2,1)S(1)} fusion(f32[384,1024]{1,0:T(8,128)} %get-tuple-element.176, f32[384,1024]{1,0:T(8,128)S(1)} %fusion.15, bf16[768,1024]{1,0:T(8,128)(2,1)S(1)} %copy-done.1, bf16[768,384]{1,0:T(8,128)(2,1)S(1)} %collective-permute-done.12), kind=kOutput, calls=%fused_computation.1 | convolution fusion | flops 303169536 | bytes 5013504 | tf_op jit(solution)/shard_map/dot_general | solution.py:658
  74.1 2.7 %collective-permute-done.13 = bf16[256,512]{1,0:T(8,128)(2,1)S(1)} collective-permute-done((bf16[256,512]{1,0:T(8,128)(2,1)}, bf16[256,512]{1,0:T(8,128)(2,1)S(1)}, u32[]{:S(2)}, u32[]{:S(2)}) %collective-permute-start.13) | collective-permute-done | bytes 262176 | tf_op jit(solution)/shard_map/ppermute | solution.py:25
  77.0 1.7 %collective-permute-start.14 = (bf16[640,256]{1,0:T(8,128)(2,1)S(1)}, bf16[640,256]{1,0:T(8,128)(2,1)S(1)}, u32[]{:S(2)}, u32[]{:S(2)}) collective-permute-start(bf16[640,256]{1,0:T(8,128)(2,1)S(1)} %maximum_maximum_fusion), channel_id=1, source_target_pairs={{0,2},{1,3},{2,0},{3,1},{4,6},{5,7},{6,4},{7,5},{8,10},{9,11},{10,... | collective-permute-start | bytes 983048 | tf_op jit(solution)/shard_map/ppermute | solution.py:25
  80.5 4.2 %collective-permute-done.15 = bf16[384,512]{1,0:T(8,128)(2,1)S(1)} collective-permute-done((bf16[384,512]{1,0:T(8,128)(2,1)}, bf16[384,512]{1,0:T(8,128)(2,1)S(1)}, u32[]{:S(2)}, u32[]{:S(2)}) %collective-permute-start.15) | collective-permute-done | bytes 393248 | tf_op jit(solution)/shard_map/ppermute | solution.py:25
  85.9 2.7 %collective-permute-start.17 = (bf16[640,128]{1,0:T(8,128)(2,1)S(1)}, bf16[640,128]{1,0:T(8,128)(2,1)S(1)}, u32[]{:S(2)}, u32[]{:S(2)}) collective-permute-start(bf16[640,128]{1,0:T(8,128)(2,1)S(1)} %fusion.17), channel_id=1, source_target_pairs={{0,4},{1,5},{2,6},{3,7},{4,0},{5,1},{6,2},{7,3},{8,12},{9,13},{10,... | collective-permute-start | bytes 491528 | tf_op jit(solution)/shard_map/ppermute | solution.py:25
  88.6 1.6 %collective-permute-start.18 = (bf16[384,256]{1,0:T(8,128)(2,1)S(1)}, bf16[384,256]{1,0:T(8,128)(2,1)S(1)}, u32[]{:S(2)}, u32[]{:S(2)}) collective-permute-start(bf16[384,256]{1,0:T(8,128)(2,1)S(1)} %pad_maximum_fusion.1), channel_id=1, source_target_pairs={{0,2},{1,3},{2,0},{3,1},{4,6},{5,7},{6,4},{7,5},{8,10},{9,11},{10,... | collective-permute-start | bytes 589832 | tf_op jit(solution)/shard_map/ppermute | solution.py:25
  90.3 1.5 %fusion.13 = f32[384,1024]{1,0:T(8,128)S(1)} fusion(bf16[768,1024]{1,0:T(8,128)(2,1)S(1)} %copy-done.1, bf16[768,384]{1,0:T(8,128)(2,1)} %collective-permute-done.11), kind=kOutput, calls=%fused_computation.11 | convolution fusion | flops 301989888 | bytes 2654208 | tf_op jit(solution)/shard_map/dot_general | solution.py:667
  92.8 2.3 %collective-permute-done.17 = bf16[640,128]{1,0:T(8,128)(2,1)S(1)} collective-permute-done((bf16[640,128]{1,0:T(8,128)(2,1)S(1)}, bf16[640,128]{1,0:T(8,128)(2,1)S(1)}, u32[]{:S(2)}, u32[]{:S(2)}) %collective-permute-start.17) | collective-permute-done | bytes 163872 | tf_op jit(solution)/shard_map/ppermute | solution.py:25
  96.2 1.3 %collective-permute-start.20 = (bf16[384,128]{1,0:T(8,128)(2,1)S(1)}, bf16[384,128]{1,0:T(8,128)(2,1)S(1)}, u32[]{:S(2)}, u32[]{:S(2)}) collective-permute-start(bf16[384,128]{1,0:T(8,128)(2,1)S(1)} %add_convert_fusion.2), channel_id=1, source_target_pairs={{0,4},{1,5},{2,6},{3,7},{4,0},{5,1},{6,2},{7,3},{8,12},{9,13},{10,... | collective-permute-start | bytes 294920 | tf_op jit(solution)/shard_map/ppermute | solution.py:25
  97.6 3.2 %collective-permute-start.21 = (f32[128,256]{1,0:T(8,128)S(1)}, f32[128,256]{1,0:T(8,128)S(1)}, u32[]{:S(2)}, u32[]{:S(2)}) collective-permute-start(f32[128,256]{1,0:T(8,128)S(1)} %pad_maximum_fusion.2), channel_id=1, source_target_pairs={{0,0},{1,1},{2,8},{3,9},{4,16},{5,17},{6,24},{7,25},{8,2},{9,3},{1... | collective-permute-start | bytes 393224 | tf_op jit(solution)/shard_map/ppermute | solution.py:513
  100.7 1.6 %fusion = bf16[1,384,1024]{2,1,0:T(8,128)(2,1)} fusion(f32[384,1024]{1,0:T(8,128)S(1)} %fusion.1, f32[384,1024]{1,0:T(8,128)S(1)} %fusion.3, f32[384,1024]{1,0:T(8,128)S(1)} %fusion.13, bf16[192,1024]{1,0:T(8,128)(2,1)S(1)} %collective-permute-done.19, bf16[192,1024]{1,0:T(8,128)(2,1)S(1)} %collective-permute-done.16, bf16[768,1024]{1,0:T(8,128)(2,1)S(1)} %copy-done.1, ...), kind=kOutput, calls=%fused_computation.2 | convolution fusion | flops 305528832 | bytes 7372800 | tf_op jit(solution)/shard_map/dot_general | solution.py:667
  103.5 5.2 %collective-permute-done.21 = f32[128,256]{1,0:T(8,128)S(1)} collective-permute-done((f32[128,256]{1,0:T(8,128)S(1)}, f32[128,256]{1,0:T(8,128)S(1)}, u32[]{:S(2)}, u32[]{:S(2)}) %collective-permute-start.21) | collective-permute-done | bytes 131104 | tf_op jit(solution)/shard_map/ppermute | solution.py:513
  (79 shorter events, 15.0 us)
Async XLA Ops:
  0.6 7.8 %collective-permute-start.1 = (bf16[384,1024]{1,0:T(8,128)(2,1)}, bf16[384,1024]{1,0:T(8,128)(2,1)}, u32[]{:S(2)}, u32[]{:S(2)}) collective-permute-start(bf16[384,1024]{1,0:T(8,128)(2,1)} %bitcast.13), channel_id=1, source_target_pairs={{0,8},{8,0},{16,24},{24,16},{1,9},{9,1},{17,25},{25,17},{2,10},{10... | collective-permute-start | bytes 2359304 | tf_op jit(solution)/shard_map/ppermute | solution.py:25
  0.7 7.8 %collective-permute-start.2 = (bf16[384,1024]{1,0:T(8,128)(2,1)}, bf16[384,1024]{1,0:T(8,128)(2,1)}, u32[]{:S(2)}, u32[]{:S(2)}) collective-permute-start(bf16[384,1024]{1,0:T(8,128)(2,1)} %bitcast.18), channel_id=1, source_target_pairs={{0,8},{8,0},{16,24},{24,16},{1,9},{9,1},{17,25},{25,17},{2,10},{10... | collective-permute-start | bytes 2359304 | tf_op jit(solution)/shard_map/ppermute | solution.py:25
  1.2 19.8 %collective-permute-start = (bf16[384,1024]{1,0:T(8,128)(2,1)}, bf16[384,1024]{1,0:T(8,128)(2,1)}, u32[]{:S(2)}, u32[]{:S(2)}) collective-permute-start(bf16[384,1024]{1,0:T(8,128)(2,1)} %bitcast.14), channel_id=1, source_target_pairs={{0,16},{8,24},{16,0},{24,8},{1,17},{9,25},{17,1},{25,9},{2,18},{10... | collective-permute-start | bytes 2359304 | tf_op jit(solution)/shard_map/ppermute | solution.py:25
  21.0 2.6 %collective-permute-start.3 = (bf16[384,1024]{1,0:T(8,128)(2,1)}, bf16[384,1024]{1,0:T(8,128)(2,1)}, u32[]{:S(2)}, u32[]{:S(2)}) collective-permute-start(bf16[384,1024]{1,0:T(8,128)(2,1)} %collective-permute-done.refs_3_.refs_14_), channel_id=1, source_target_pairs={{0,8},{8,0},{16,24},{24,16},{1,9},{9,1},{17,25},{25,17},{2,10},{10... | collective-permute-start | bytes 2359304 | tf_op jit(solution)/shard_map/ppermute | solution.py:25
  21.1 19.8 %collective-permute-start.6 = (bf16[192,1024]{1,0:T(8,128)(2,1)}, bf16[192,1024]{1,0:T(8,128)(2,1)}, u32[]{:S(2)}, u32[]{:S(2)}) collective-permute-start(bf16[192,1024]{1,0:T(8,128)(2,1)} %get-tuple-element.130), channel_id=1, source_target_pairs={{0,16},{8,24},{16,0},{24,8},{1,17},{9,25},{17,1},{25,9},{2,18},{10... | collective-permute-start | bytes 1179656 | tf_op jit(solution)/shard_map/ppermute | solution.py:25
  21.3 16.6 %collective-permute-start.4 = (bf16[256,384]{1,0:T(8,128)(2,1)}, bf16[256,384]{1,0:T(8,128)(2,1)S(1)}, u32[]{:S(2)}, u32[]{:S(2)}) collective-permute-start(bf16[256,384]{1,0:T(8,128)(2,1)} %get-tuple-element.128), channel_id=1, source_target_pairs={{0,16},{8,24},{16,0},{24,8},{1,17},{9,25},{17,1},{25,9},{2,18},{10... | collective-permute-start | bytes 589832 | tf_op jit(solution)/shard_map/ppermute | solution.py:25
  23.1 17.7 %collective-permute-start.5 = (bf16[256,384]{1,0:T(8,128)(2,1)}, bf16[256,384]{1,0:T(8,128)(2,1)S(1)}, u32[]{:S(2)}, u32[]{:S(2)}) collective-permute-start(bf16[256,384]{1,0:T(8,128)(2,1)} %get-tuple-element.129), channel_id=1, source_target_pairs={{0,24},{8,16},{16,8},{24,0},{1,25},{9,17},{17,9},{25,1},{2,26},{10... | collective-permute-start | bytes 589832 | tf_op jit(solution)/shard_map/ppermute | solution.py:25
  40.8 11.5 %collective-permute-start.8 = (bf16[192,1024]{1,0:T(8,128)(2,1)}, bf16[192,1024]{1,0:T(8,128)(2,1)}, u32[]{:S(2)}, u32[]{:S(2)}) collective-permute-start(bf16[192,1024]{1,0:T(8,128)(2,1)} %get-tuple-element.148), channel_id=1, source_target_pairs={{0,16},{8,24},{16,0},{24,8},{1,17},{9,25},{17,1},{25,9},{2,18},{10... | collective-permute-start | bytes 1179656 | tf_op jit(solution)/shard_map/ppermute | solution.py:25
  41.1 11.3 %collective-permute-start.7 = (bf16[192,1024]{1,0:T(8,128)(2,1)}, bf16[192,1024]{1,0:T(8,128)(2,1)}, u32[]{:S(2)}, u32[]{:S(2)}) collective-permute-start(bf16[192,1024]{1,0:T(8,128)(2,1)} %collective-permute-done.6.refs_18_), channel_id=1, source_target_pairs={{0,8},{8,0},{16,24},{24,16},{1,9},{9,1},{17,25},{25,17},{2,10},{10... | collective-permute-start | bytes 1179656 | tf_op jit(solution)/shard_map/ppermute | solution.py:25
  52.4 14.9 %collective-permute-start.11 = (bf16[768,384]{1,0:T(8,128)(2,1)}, bf16[768,384]{1,0:T(8,128)(2,1)}, u32[]{:S(2)}, u32[]{:S(2)}) collective-permute-start(bf16[768,384]{1,0:T(8,128)(2,1)} %get-tuple-element.172), channel_id=1, source_target_pairs={{0,8},{8,0},{16,24},{24,16},{1,9},{9,1},{17,25},{25,17},{2,10},{10... | collective-permute-start | bytes 1769480 | tf_op jit(solution)/shard_map/ppermute | solution.py:25
  52.4 2.9 %collective-permute-start.9 = (bf16[192,1024]{1,0:T(8,128)(2,1)}, bf16[192,1024]{1,0:T(8,128)(2,1)}, u32[]{:S(2)}, u32[]{:S(2)}) collective-permute-start(bf16[192,1024]{1,0:T(8,128)(2,1)} %collective-permute-done.8.refs_19_), channel_id=1, source_target_pairs={{0,8},{8,0},{16,24},{24,16},{1,9},{9,1},{17,25},{25,17},{2,10},{10... | collective-permute-start | bytes 1179656 | tf_op jit(solution)/shard_map/ppermute | solution.py:25
  52.9 14.4 %collective-permute-start.10 = (bf16[384,512]{1,0:T(8,128)(2,1)}, bf16[384,512]{1,0:T(8,128)(2,1)S(1)}, u32[]{:S(2)}, u32[]{:S(2)}) collective-permute-start(bf16[384,512]{1,0:T(8,128)(2,1)} %get-tuple-element.171), channel_id=1, source_target_pairs={{0,1},{1,0},{2,3},{3,2},{4,5},{5,4},{6,7},{7,6},{8,9},{9,8},{10,11... | collective-permute-start | bytes 1179656 | tf_op jit(solution)/shard_map/ppermute | solution.py:25
  67.3 4.0 %collective-permute-start.12 = (bf16[768,384]{1,0:T(8,128)(2,1)}, bf16[768,384]{1,0:T(8,128)(2,1)S(1)}, u32[]{:S(2)}, u32[]{:S(2)}) collective-permute-start(bf16[768,384]{1,0:T(8,128)(2,1)} %get-tuple-element.175), channel_id=1, source_target_pairs={{0,8},{8,0},{16,24},{24,16},{1,9},{9,1},{17,25},{25,17},{2,10},{10... | collective-permute-start | bytes 1769480 | tf_op jit(solution)/shard_map/ppermute | solution.py:25
  67.5 9.3 %collective-permute-start.13 = (bf16[256,512]{1,0:T(8,128)(2,1)}, bf16[256,512]{1,0:T(8,128)(2,1)S(1)}, u32[]{:S(2)}, u32[]{:S(2)}) collective-permute-start(bf16[256,512]{1,0:T(8,128)(2,1)} %get-tuple-element.184), channel_id=1, source_target_pairs={{0,1},{1,0},{2,3},{3,2},{4,5},{5,4},{6,7},{7,6},{8,9},{9,8},{10,11... | collective-permute-start | bytes 786440 | tf_op jit(solution)/shard_map/ppermute | solution.py:25
  69.0 15.7 %collective-permute-start.15 = (bf16[384,512]{1,0:T(8,128)(2,1)}, bf16[384,512]{1,0:T(8,128)(2,1)S(1)}, u32[]{:S(2)}, u32[]{:S(2)}) collective-permute-start(bf16[384,512]{1,0:T(8,128)(2,1)} %get-tuple-element.189), channel_id=1, source_target_pairs={{0,1},{1,0},{2,3},{3,2},{4,5},{5,4},{6,7},{7,6},{8,9},{9,8},{10,11... | collective-permute-start | bytes 1179656 | tf_op jit(solution)/shard_map/ppermute | solution.py:25
  73.4 12.4 %collective-permute-start.16 = (bf16[192,1024]{1,0:T(8,128)(2,1)S(1)}, bf16[192,1024]{1,0:T(8,128)(2,1)S(1)}, u32[]{:S(2)}, u32[]{:S(2)}) collective-permute-start(bf16[192,1024]{1,0:T(8,128)(2,1)S(1)} %get-tuple-element.209), channel_id=1, source_target_pairs={{0,16},{8,24},{16,0},{24,8},{1,17},{9,25},{17,1},{25,9},{2,18},{10... | collective-permute-start | bytes 1179656 | tf_op jit(solution)/shard_map/ppermute | solution.py:25
  74.1 5.3 %copy-start.2 = (bf16[768,384]{1,0:T(8,128)(2,1)S(1)}, bf16[768,384]{1,0:T(8,128)(2,1)}, u32[]{:S(2)}) copy-start(bf16[768,384]{1,0:T(8,128)(2,1)} %get-tuple-element.178.refs_24_) | copy-start | bytes 1769476
  77.0 8.8 %collective-permute-start.14 = (bf16[640,256]{1,0:T(8,128)(2,1)S(1)}, bf16[640,256]{1,0:T(8,128)(2,1)S(1)}, u32[]{:S(2)}, u32[]{:S(2)}) collective-permute-start(bf16[640,256]{1,0:T(8,128)(2,1)S(1)} %maximum_maximum_fusion), channel_id=1, source_target_pairs={{0,2},{1,3},{2,0},{3,1},{4,6},{5,7},{6,4},{7,5},{8,10},{9,11},{10,... | collective-permute-start | bytes 983048 | tf_op jit(solution)/shard_map/ppermute | solution.py:25
  78.7 14.1 %collective-permute-start.19 = (bf16[192,1024]{1,0:T(8,128)(2,1)S(1)}, bf16[192,1024]{1,0:T(8,128)(2,1)S(1)}, u32[]{:S(2)}, u32[]{:S(2)}) collective-permute-start(bf16[192,1024]{1,0:T(8,128)(2,1)S(1)} %get-tuple-element.194), channel_id=1, source_target_pairs={{0,16},{8,24},{16,0},{24,8},{1,17},{9,25},{17,1},{25,9},{2,18},{10... | collective-permute-start | bytes 1179656 | tf_op jit(solution)/shard_map/ppermute | solution.py:25
  80.0 8.6 %copy-start.6 = (f32[384,512]{1,0:T(8,128)S(1)}, f32[384,512]{1,0:T(8,128)}, u32[]{:S(2)}) copy-start(f32[384,512]{1,0:T(8,128)} %get-tuple-element.192) | copy-start | bytes 2359300
  85.9 9.2 %collective-permute-start.17 = (bf16[640,128]{1,0:T(8,128)(2,1)S(1)}, bf16[640,128]{1,0:T(8,128)(2,1)S(1)}, u32[]{:S(2)}, u32[]{:S(2)}) collective-permute-start(bf16[640,128]{1,0:T(8,128)(2,1)S(1)} %fusion.17), channel_id=1, source_target_pairs={{0,4},{1,5},{2,6},{3,7},{4,0},{5,1},{6,2},{7,3},{8,12},{9,13},{10,... | collective-permute-start | bytes 491528 | tf_op jit(solution)/shard_map/ppermute | solution.py:25
  88.6 7.5 %collective-permute-start.18 = (bf16[384,256]{1,0:T(8,128)(2,1)S(1)}, bf16[384,256]{1,0:T(8,128)(2,1)S(1)}, u32[]{:S(2)}, u32[]{:S(2)}) collective-permute-start(bf16[384,256]{1,0:T(8,128)(2,1)S(1)} %pad_maximum_fusion.1), channel_id=1, source_target_pairs={{0,2},{1,3},{2,0},{3,1},{4,6},{5,7},{6,4},{7,5},{8,10},{9,11},{10,... | collective-permute-start | bytes 589832 | tf_op jit(solution)/shard_map/ppermute | solution.py:25
  96.2 6.6 %collective-permute-start.20 = (bf16[384,128]{1,0:T(8,128)(2,1)S(1)}, bf16[384,128]{1,0:T(8,128)(2,1)S(1)}, u32[]{:S(2)}, u32[]{:S(2)}) collective-permute-start(bf16[384,128]{1,0:T(8,128)(2,1)S(1)} %add_convert_fusion.2), channel_id=1, source_target_pairs={{0,4},{1,5},{2,6},{3,7},{4,0},{5,1},{6,2},{7,3},{8,12},{9,13},{10,... | collective-permute-start | bytes 294920 | tf_op jit(solution)/shard_map/ppermute | solution.py:25
  97.6 11.1 %collective-permute-start.21 = (f32[128,256]{1,0:T(8,128)S(1)}, f32[128,256]{1,0:T(8,128)S(1)}, u32[]{:S(2)}, u32[]{:S(2)}) collective-permute-start(f32[128,256]{1,0:T(8,128)S(1)} %pad_maximum_fusion.2), channel_id=1, source_target_pairs={{0,0},{1,1},{2,8},{3,9},{4,16},{5,17},{6,24},{7,25},{8,2},{9,3},{1... | collective-permute-start | bytes 393224 | tf_op jit(solution)/shard_map/ppermute | solution.py:513
  (9 other events, 29.8 us)

commit v6 on v5

--- a/solution.py
+++ b/solution.py
@@ -700,7 +700,7 @@
                 out_sum = side_by_side(
                     [out_sum[at : at + BLK] for at in range(top, top + head_width, BLK)]
                 )
-            out_part = to_owner(out_sum)[None]
+            out_part = to_owner(out_sum.astype(BF)).astype(F32)[None]
 
     grad_hidden = partial
     for both in zip(token_parts, later_parts):

time: 110 us -> 111 us (level)
  the two profiles are of different devices: /device:TPU:4 before, /device:TPU:0 now
where the time goes in v6:
time: 111 us
  Pallas kernels  49.9 us (45%)
  starting transfers between devices  28.3 us (25%)
  waiting for transfers between devices  20.1 us (18%)
  matrix products  8.05 us (7%)
  local copies, waits for them, and re-layouts  2.03 us (2%)
  other arithmetic  1.4 us (1%)
    pallas_call x6, Pallas kernels, run(): pl.pallas_call(kernel, in_specs=[pl.BlockSpec(memory_space=pltpu.SMEM)] *...  49.9 us
    ppermute x21, starting transfers between devices, swap(): lax.ppermute(value, axis, [(at, at ^ distance) for at in range(count)])  27.7 us
    ppermute x21, waiting for transfers between devices, swap(): lax.ppermute(value, axis, [(at, at ^ distance) for at in range(count)])  20.1 us
    dot_general x4, matrix products, per_device(): jnp.dot(parts[pair][:row_count], weight, preferred_element_type=F32)  4.26 us
    dot_general x2, matrix products, per_device(): total += jnp.dot(mate, weight, preferred_element_type=F32)  3.79 us
  transfers between devices with their start and end apart: 22, of which 12 were waited for; matrix products, arithmetic and copies ran while one was open for 9% of the time, Pallas kernels for 45%

profile of v6, /device:TPU:0, one launch (start us, length us, event | category | flops | bytes accessed | tf_op | source)
XLA Modules:
  0.0 110.9 jit_solution(6733313319866496447)
XLA Ops:
  1.2 2.9 %collective-permute-start = (bf16[384,1024]{1,0:T(8,128)(2,1)}, bf16[384,1024]{1,0:T(8,128)(2,1)}, u32[]{:S(2)}, u32[]{:S(2)}) collective-permute-start(bf16[384,1024]{1,0:T(8,128)(2,1)} %bitcast.16), channel_id=1, source_target_pairs={{0,16},{8,24},{16,0},{24,8},{1,17},{9,25},{17,1},{25,9},{2,18},{10... | collective-permute-start | bytes 2359304 | tf_op jit(solution)/shard_map/ppermute | solution.py:25
  4.2 2.8 %weight_rows.3.refs_1_.refs_2_.refs_25_ = bf16[768,1024]{1,0:T(8,128)(2,1)} custom-call(s32[1]{0:T(128)} %bitcast.3.refs_0_, bf16[1024,1024]{1,0:T(8,128)(2,1)} %refs_1_.3, bf16[1024,1024]{1,0:T(8,128)(2,1)} %refs_2_.4, bf16[1024,1024]{1,0:T(8,128)(2,1)} %refs_3_.4), custom_call_target="tpu_custom_call" | custom-call | flops 1 | bytes 1 | tf_op jit(solution)/shard_map/weight_rows/pallas_call | solution.py:109
  7.0 2.8 %weight_rows.2 = bf16[768,1024]{1,0:T(8,128)(2,1)} custom-call(s32[1]{0:T(128)} %bitcast.1.refs_0_, bf16[1024,1024]{1,0:T(8,128)(2,1)} %refs_1_.3, bf16[1024,1024]{1,0:T(8,128)(2,1)} %refs_2_.4, bf16[1024,1024]{1,0:T(8,128)(2,1)} %refs_3_.4), custom_call_target="tpu_custom_call" | custom-call | flops 1 | bytes 1 | tf_op jit(solution)/shard_map/weight_rows/pallas_call | solution.py:109
  11.4 8.5 %project.1 = (bf16[256,768]{1,0:T(8,128)(2,1)}, bf16[256,768]{1,0:T(8,128)(2,1)}, bf16[256,768]{1,0:T(8,128)(2,1)}, bf16[256,768]{1,0:T(8,128)(2,1)}, bf16[768,2...) custom-call(s32[28]{0:T(128)} %concatenate.37.refs_0_, ...), custom_call_target="tpu_custom_call" | custom-call | flops 1 | bytes 1 | tf_op jit(solution)/shard_map/project/pallas_call | solution.py:109
  19.9 2.4 %collective-permute-done.refs_3_.refs_14_ = bf16[384,1024]{1,0:T(8,128)(2,1)} collective-permute-done((bf16[384,1024]{1,0:T(8,128)(2,1)}, bf16[384,1024]{1,0:T(8,128)(2,1)}, u32[]{:S(2)}, u32[]{:S(2)}) %collective-permute-start) | collective-permute-done | bytes 786464 | tf_op jit(solution)/shard_map/ppermute | solution.py:25
  22.3 1.7 %collective-permute-start.6 = (bf16[192,1024]{1,0:T(8,128)(2,1)}, bf16[192,1024]{1,0:T(8,128)(2,1)}, u32[]{:S(2)}, u32[]{:S(2)}) collective-permute-start(bf16[192,1024]{1,0:T(8,128)(2,1)} %get-tuple-element.130), channel_id=1, source_target_pairs={{0,16},{8,24},{16,0},{24,8},{1,17},{9,25},{17,1},{25,9},{2,18},{10... | collective-permute-start | bytes 1179656 | tf_op jit(solution)/shard_map/ppermute | solution.py:25
  25.6 14.2 %own_half.1 = (bf16[256,768]{1,0:T(8,128)(2,1)}, bf16[256,1536]{1,0:T(8,128)(2,1)}, bf16[256,1536]{1,0:T(8,128)(2,1)}, bf16[1536,256]{1,0:T(8,128)(2,1)}, bf16[1...) custom-call(s32[28]{0:T(128)} %concatenate.37.refs_0_, ...), custom_call_target="tpu_custom_call" | custom-call | flops 1 | bytes 1 | tf_op jit(solution)/shard_map/own_half/pallas_call | solution.py:109
  39.9 2.2 %collective-permute-done.5.refs_3_ = bf16[256,384]{1,0:T(8,128)(2,1)S(1)} collective-permute-done((bf16[256,384]{1,0:T(8,128)(2,1)}, bf16[256,384]{1,0:T(8,128)(2,1)S(1)}, u32[]{:S(2)}, u32[]{:S(2)}) %collective-permute-start.5) | collective-permute-done | bytes 196640 | tf_op jit(solution)/shard_map/ppermute | solution.py:25
  42.1 1.7 %collective-permute-start.8 = (bf16[192,1024]{1,0:T(8,128)(2,1)}, bf16[192,1024]{1,0:T(8,128)(2,1)}, u32[]{:S(2)}, u32[]{:S(2)}) collective-permute-start(bf16[192,1024]{1,0:T(8,128)(2,1)} %get-tuple-element.148), channel_id=1, source_target_pairs={{0,16},{8,24},{16,0},{24,8},{1,17},{9,25},{17,1},{25,9},{2,18},{10... | collective-permute-start | bytes 1179656 | tf_op jit(solution)/shard_map/ppermute | solution.py:25
  43.8 9.7 %later_half.2 = (bf16[128,768]{1,0:T(8,128)(2,1)}, bf16[768,384]{1,0:T(8,128)(2,1)}, bf16[768,384]{1,0:T(8,128)(2,1)}, bf16[384,512]{1,0:T(8,128)(2,1)}, f32[384,512]{1,0:T(8,128)}) custom-call(s32[28]{0:T(128)} %concatenate.37.refs_0_, s32[192]{0:T(256)} %reshape_squeeze.3.refs_1_, bf16[256,384]{1,0:T(8,128)(2,1)} %copy-done.3, bf16[256,384]{1,0:T(8,128)(2,1)} %copy-done.4, ...), custom_call_target="tpu_custom_call" | custom-call | flops 1 | bytes 1 | tf_op jit(solution)/shard_map/later_half/pallas_call | solution.py:109
  54.2 1.7 %collective-permute-start.10 = (bf16[384,512]{1,0:T(8,128)(2,1)}, bf16[384,512]{1,0:T(8,128)(2,1)S(1)}, u32[]{:S(2)}, u32[]{:S(2)}) collective-permute-start(bf16[384,512]{1,0:T(8,128)(2,1)} %get-tuple-element.171), channel_id=1, source_target_pairs={{0,1},{1,0},{2,3},{3,2},{4,5},{5,4},{6,7},{7,6},{8,9},{9,8},{10,11... | collective-permute-start | bytes 1179656 | tf_op jit(solution)/shard_map/ppermute | solution.py:25
  56.6 11.9 %later_half.3 = (bf16[128,768]{1,0:T(8,128)(2,1)}, bf16[768,384]{1,0:T(8,128)(2,1)}, bf16[768,384]{1,0:T(8,128)(2,1)}, bf16[384,512]{1,0:T(8,128)(2,1)}, f32[384...) custom-call(s32[28]{0:T(128)} %concatenate.37.refs_0_, ...), custom_call_target="tpu_custom_call" | custom-call | flops 1 | bytes 1 | tf_op jit(solution)/shard_map/later_half/pallas_call | solution.py:109
  71.1 1.8 %fusion.15 = f32[384,1024]{1,0:T(8,128)S(1)} fusion(bf16[768,1024]{1,0:T(8,128)(2,1)} %weight_rows.2, bf16[768,384]{1,0:T(8,128)(2,1)} %collective-permute-done.11), kind=kOutput, calls=%fused_computation.13 | convolution fusion | flops 301989888 | bytes 2654208 | tf_op jit(solution)/shard_map/dot_general | solution.py:658
  72.9 2.0 %add_convert_fusion.1 = bf16[384,1024]{1,0:T(8,128)(2,1)S(1)} fusion(f32[384,1024]{1,0:T(8,128)} %get-tuple-element.176, f32[384,1024]{1,0:T(8,128)S(1)} %fusion.15, bf16[768,1024]{1,0:T(8,128)(2,1)S(1)} %copy-done.1, bf16[768,384]{1,0:T(8,128)(2,1)S(1)} %collective-permute-done.12), kind=kOutput, calls=%fused_computation.1 | convolution fusion | flops 303169536 | bytes 5013504 | tf_op jit(solution)/shard_map/dot_general | solution.py:658
  76.5 1.9 %collective-permute-done.13 = bf16[256,512]{1,0:T(8,128)(2,1)S(1)} collective-permute-done((bf16[256,512]{1,0:T(8,128)(2,1)}, bf16[256,512]{1,0:T(8,128)(2,1)S(1)}, u32[]{:S(2)}, u32[]{:S(2)}) %collective-permute-start.13) | collective-permute-done | bytes 262176 | tf_op jit(solution)/shard_map/ppermute | solution.py:25
  78.6 1.7 %collective-permute-start.14 = (bf16[640,256]{1,0:T(8,128)(2,1)S(1)}, bf16[640,256]{1,0:T(8,128)(2,1)S(1)}, u32[]{:S(2)}, u32[]{:S(2)}) collective-permute-start(bf16[640,256]{1,0:T(8,128)(2,1)S(1)} %maximum_maximum_fusion), channel_id=1, source_target_pairs={{0,2},{1,3},{2,0},{3,1},{4,6},{5,7},{6,4},{7,5},{8,10},{9,11},{10,... | collective-permute-start | bytes 983048 | tf_op jit(solution)/shard_map/ppermute | solution.py:25
  82.8 3.2 %collective-permute-done.15 = bf16[384,512]{1,0:T(8,128)(2,1)S(1)} collective-permute-done((bf16[384,512]{1,0:T(8,128)(2,1)}, bf16[384,512]{1,0:T(8,128)(2,1)S(1)}, u32[]{:S(2)}, u32[]{:S(2)}) %collective-permute-start.15) | collective-permute-done | bytes 393248 | tf_op jit(solution)/shard_map/ppermute | solution.py:25
  87.1 2.7 %collective-permute-start.17 = (bf16[640,128]{1,0:T(8,128)(2,1)S(1)}, bf16[640,128]{1,0:T(8,128)(2,1)S(1)}, u32[]{:S(2)}, u32[]{:S(2)}) collective-permute-start(bf16[640,128]{1,0:T(8,128)(2,1)S(1)} %fusion.17), channel_id=1, source_target_pairs={{0,4},{1,5},{2,6},{3,7},{4,0},{5,1},{6,2},{7,3},{8,12},{9,13},{10,... | collective-permute-start | bytes 491528 | tf_op jit(solution)/shard_map/ppermute | solution.py:25
  89.9 1.7 %collective-permute-start.18 = (bf16[384,256]{1,0:T(8,128)(2,1)S(1)}, bf16[384,256]{1,0:T(8,128)(2,1)S(1)}, u32[]{:S(2)}, u32[]{:S(2)}) collective-permute-start(bf16[384,256]{1,0:T(8,128)(2,1)S(1)} %pad_maximum_fusion.1), channel_id=1, source_target_pairs={{0,2},{1,3},{2,0},{3,1},{4,6},{5,7},{6,4},{7,5},{8,10},{9,11},{10,... | collective-permute-start | bytes 589832 | tf_op jit(solution)/shard_map/ppermute | solution.py:25
  91.5 1.5 %fusion.13 = f32[384,1024]{1,0:T(8,128)S(1)} fusion(bf16[768,1024]{1,0:T(8,128)(2,1)S(1)} %copy-done.1, bf16[768,384]{1,0:T(8,128)(2,1)} %collective-permute-done.11), kind=kOutput, calls=%fused_computation.11 | convolution fusion | flops 301989888 | bytes 2654208 | tf_op jit(solution)/shard_map/dot_general | solution.py:667
  94.1 2.1 %collective-permute-done.17 = bf16[640,128]{1,0:T(8,128)(2,1)S(1)} collective-permute-done((bf16[640,128]{1,0:T(8,128)(2,1)S(1)}, bf16[640,128]{1,0:T(8,128)(2,1)S(1)}, u32[]{:S(2)}, u32[]{:S(2)}) %collective-permute-start.17) | collective-permute-done | bytes 163872 | tf_op jit(solution)/shard_map/ppermute | solution.py:25
  98.1 5.5 %collective-permute-start.20 = (bf16[384,128]{1,0:T(8,128)(2,1)S(1)}, bf16[384,128]{1,0:T(8,128)(2,1)S(1)}, u32[]{:S(2)}, u32[]{:S(2)}) collective-permute-start(bf16[384,128]{1,0:T(8,128)(2,1)S(1)} %add_convert_fusion.2), channel_id=1, source_target_pairs={{0,4},{1,5},{2,6},{3,7},{4,0},{5,1},{6,2},{7,3},{8,12},{9,13},{10,... | collective-permute-start | bytes 294920 | tf_op jit(solution)/shard_map/ppermute | solution.py:25
  103.6 1.6 %fusion = bf16[1,384,1024]{2,1,0:T(8,128)(2,1)} fusion(f32[384,1024]{1,0:T(8,128)S(1)} %fusion.1, f32[384,1024]{1,0:T(8,128)S(1)} %fusion.3, f32[384,1024]{1,0:T(8,128)S(1)} %fusion.13, bf16[192,1024]{1,0:T(8,128)(2,1)S(1)} %collective-permute-done.19, bf16[192,1024]{1,0:T(8,128)(2,1)S(1)} %collective-permute-done.16, bf16[768,1024]{1,0:T(8,128)(2,1)S(1)} %copy-done.1, ...), kind=kOutput, calls=%fused_computation.2 | convolution fusion | flops 305528832 | bytes 7372800 | tf_op jit(solution)/shard_map/dot_general | solution.py:667
  105.2 4.2 %collective-permute-done.20 = bf16[384,128]{1,0:T(8,128)(2,1)S(1)} collective-permute-done((bf16[384,128]{1,0:T(8,128)(2,1)S(1)}, bf16[384,128]{1,0:T(8,128)(2,1)S(1)}, u32[]{:S(2)}, u32[]{:S(2)}) %collective-permute-start.20) | collective-permute-done | bytes 98336 | tf_op jit(solution)/shard_map/ppermute | solution.py:25
  (80 shorter events, 17.3 us)
Async XLA Ops:
  0.6 10.8 %collective-permute-start.1 = (bf16[384,1024]{1,0:T(8,128)(2,1)}, bf16[384,1024]{1,0:T(8,128)(2,1)}, u32[]{:S(2)}, u32[]{:S(2)}) collective-permute-start(bf16[384,1024]{1,0:T(8,128)(2,1)} %bitcast.15), channel_id=1, source_target_pairs={{0,8},{8,0},{16,24},{24,16},{1,9},{9,1},{17,25},{25,17},{2,10},{10... | collective-permute-start | bytes 2359304 | tf_op jit(solution)/shard_map/ppermute | solution.py:25
  1.1 10.2 %collective-permute-start.2 = (bf16[384,1024]{1,0:T(8,128)(2,1)}, bf16[384,1024]{1,0:T(8,128)(2,1)}, u32[]{:S(2)}, u32[]{:S(2)}) collective-permute-start(bf16[384,1024]{1,0:T(8,128)(2,1)} %bitcast.20), channel_id=1, source_target_pairs={{0,8},{8,0},{16,24},{24,16},{1,9},{9,1},{17,25},{25,17},{2,10},{10... | collective-permute-start | bytes 2359304 | tf_op jit(solution)/shard_map/ppermute | solution.py:25
  1.2 21.0 %collective-permute-start = (bf16[384,1024]{1,0:T(8,128)(2,1)}, bf16[384,1024]{1,0:T(8,128)(2,1)}, u32[]{:S(2)}, u32[]{:S(2)}) collective-permute-start(bf16[384,1024]{1,0:T(8,128)(2,1)} %bitcast.16), channel_id=1, source_target_pairs={{0,16},{8,24},{16,0},{24,8},{1,17},{9,25},{17,1},{25,9},{2,18},{10... | collective-permute-start | bytes 2359304 | tf_op jit(solution)/shard_map/ppermute | solution.py:25
  22.3 3.3 %collective-permute-start.3 = (bf16[384,1024]{1,0:T(8,128)(2,1)}, bf16[384,1024]{1,0:T(8,128)(2,1)}, u32[]{:S(2)}, u32[]{:S(2)}) collective-permute-start(bf16[384,1024]{1,0:T(8,128)(2,1)} %collective-permute-done.refs_3_.refs_14_), channel_id=1, source_target_pairs={{0,8},{8,0},{16,24},{24,16},{1,9},{9,1},{17,25},{25,17},{2,10},{10... | collective-permute-start | bytes 2359304 | tf_op jit(solution)/shard_map/ppermute | solution.py:25
  22.3 19.8 %collective-permute-start.6 = (bf16[192,1024]{1,0:T(8,128)(2,1)}, bf16[192,1024]{1,0:T(8,128)(2,1)}, u32[]{:S(2)}, u32[]{:S(2)}) collective-permute-start(bf16[192,1024]{1,0:T(8,128)(2,1)} %get-tuple-element.130), channel_id=1, source_target_pairs={{0,16},{8,24},{16,0},{24,8},{1,17},{9,25},{17,1},{25,9},{2,18},{10... | collective-permute-start | bytes 1179656 | tf_op jit(solution)/shard_map/ppermute | solution.py:25
  24.0 15.8 %collective-permute-start.4 = (bf16[256,384]{1,0:T(8,128)(2,1)}, bf16[256,384]{1,0:T(8,128)(2,1)S(1)}, u32[]{:S(2)}, u32[]{:S(2)}) collective-permute-start(bf16[256,384]{1,0:T(8,128)(2,1)} %get-tuple-element.128), channel_id=1, source_target_pairs={{0,16},{8,24},{16,0},{24,8},{1,17},{9,25},{17,1},{25,9},{2,18},{10... | collective-permute-start | bytes 589832 | tf_op jit(solution)/shard_map/ppermute | solution.py:25
  24.3 17.7 %collective-permute-start.5 = (bf16[256,384]{1,0:T(8,128)(2,1)}, bf16[256,384]{1,0:T(8,128)(2,1)S(1)}, u32[]{:S(2)}, u32[]{:S(2)}) collective-permute-start(bf16[256,384]{1,0:T(8,128)(2,1)} %get-tuple-element.129), channel_id=1, source_target_pairs={{0,24},{8,16},{16,8},{24,0},{1,25},{9,17},{17,9},{25,1},{2,26},{10... | collective-permute-start | bytes 589832 | tf_op jit(solution)/shard_map/ppermute | solution.py:25
  42.1 11.5 %collective-permute-start.8 = (bf16[192,1024]{1,0:T(8,128)(2,1)}, bf16[192,1024]{1,0:T(8,128)(2,1)}, u32[]{:S(2)}, u32[]{:S(2)}) collective-permute-start(bf16[192,1024]{1,0:T(8,128)(2,1)} %get-tuple-element.148), channel_id=1, source_target_pairs={{0,16},{8,24},{16,0},{24,8},{1,17},{9,25},{17,1},{25,9},{2,18},{10... | collective-permute-start | bytes 1179656 | tf_op jit(solution)/shard_map/ppermute | solution.py:25
  43.8 9.8 %collective-permute-start.7 = (bf16[192,1024]{1,0:T(8,128)(2,1)}, bf16[192,1024]{1,0:T(8,128)(2,1)}, u32[]{:S(2)}, u32[]{:S(2)}) collective-permute-start(bf16[192,1024]{1,0:T(8,128)(2,1)} %collective-permute-done.6.refs_18_), channel_id=1, source_target_pairs={{0,8},{8,0},{16,24},{24,16},{1,9},{9,1},{17,25},{25,17},{2,10},{10... | collective-permute-start | bytes 1179656 | tf_op jit(solution)/shard_map/ppermute | solution.py:25
  53.6 15.0 %collective-permute-start.11 = (bf16[768,384]{1,0:T(8,128)(2,1)}, bf16[768,384]{1,0:T(8,128)(2,1)}, u32[]{:S(2)}, u32[]{:S(2)}) collective-permute-start(bf16[768,384]{1,0:T(8,128)(2,1)} %get-tuple-element.172), channel_id=1, source_target_pairs={{0,8},{8,0},{16,24},{24,16},{1,9},{9,1},{17,25},{25,17},{2,10},{10... | collective-permute-start | bytes 1769480 | tf_op jit(solution)/shard_map/ppermute | solution.py:25
  54.1 2.5 %collective-permute-start.9 = (bf16[192,1024]{1,0:T(8,128)(2,1)}, bf16[192,1024]{1,0:T(8,128)(2,1)}, u32[]{:S(2)}, u32[]{:S(2)}) collective-permute-start(bf16[192,1024]{1,0:T(8,128)(2,1)} %collective-permute-done.8.refs_19_), channel_id=1, source_target_pairs={{0,8},{8,0},{16,24},{24,16},{1,9},{9,1},{17,25},{25,17},{2,10},{10... | collective-permute-start | bytes 1179656 | tf_op jit(solution)/shard_map/ppermute | solution.py:25
  54.2 14.4 %collective-permute-start.10 = (bf16[384,512]{1,0:T(8,128)(2,1)}, bf16[384,512]{1,0:T(8,128)(2,1)S(1)}, u32[]{:S(2)}, u32[]{:S(2)}) collective-permute-start(bf16[384,512]{1,0:T(8,128)(2,1)} %get-tuple-element.171), channel_id=1, source_target_pairs={{0,1},{1,0},{2,3},{3,2},{4,5},{5,4},{6,7},{7,6},{8,9},{9,8},{10,11... | collective-permute-start | bytes 1179656 | tf_op jit(solution)/shard_map/ppermute | solution.py:25
  68.6 4.3 %collective-permute-start.12 = (bf16[768,384]{1,0:T(8,128)(2,1)}, bf16[768,384]{1,0:T(8,128)(2,1)S(1)}, u32[]{:S(2)}, u32[]{:S(2)}) collective-permute-start(bf16[768,384]{1,0:T(8,128)(2,1)} %get-tuple-element.175), channel_id=1, source_target_pairs={{0,8},{8,0},{16,24},{24,16},{1,9},{9,1},{17,25},{25,17},{2,10},{10... | collective-permute-start | bytes 1769480 | tf_op jit(solution)/shard_map/ppermute | solution.py:25
  69.0 9.4 %collective-permute-start.13 = (bf16[256,512]{1,0:T(8,128)(2,1)}, bf16[256,512]{1,0:T(8,128)(2,1)S(1)}, u32[]{:S(2)}, u32[]{:S(2)}) collective-permute-start(bf16[256,512]{1,0:T(8,128)(2,1)} %get-tuple-element.184), channel_id=1, source_target_pairs={{0,1},{1,0},{2,3},{3,2},{4,5},{5,4},{6,7},{7,6},{8,9},{9,8},{10,11... | collective-permute-start | bytes 786440 | tf_op jit(solution)/shard_map/ppermute | solution.py:25
  70.6 15.5 %collective-permute-start.15 = (bf16[384,512]{1,0:T(8,128)(2,1)}, bf16[384,512]{1,0:T(8,128)(2,1)S(1)}, u32[]{:S(2)}, u32[]{:S(2)}) collective-permute-start(bf16[384,512]{1,0:T(8,128)(2,1)} %get-tuple-element.189), channel_id=1, source_target_pairs={{0,1},{1,0},{2,3},{3,2},{4,5},{5,4},{6,7},{7,6},{8,9},{9,8},{10,11... | collective-permute-start | bytes 1179656 | tf_op jit(solution)/shard_map/ppermute | solution.py:25
  75.0 12.1 %collective-permute-start.16 = (bf16[192,1024]{1,0:T(8,128)(2,1)S(1)}, bf16[192,1024]{1,0:T(8,128)(2,1)S(1)}, u32[]{:S(2)}, u32[]{:S(2)}) collective-permute-start(bf16[192,1024]{1,0:T(8,128)(2,1)S(1)} %get-tuple-element.211), channel_id=1, source_target_pairs={{0,16},{8,24},{16,0},{24,8},{1,17},{9,25},{17,1},{25,9},{2,18},{10... | collective-permute-start | bytes 1179656 | tf_op jit(solution)/shard_map/ppermute | solution.py:25
  76.5 5.2 %copy-start.2 = (bf16[768,384]{1,0:T(8,128)(2,1)S(1)}, bf16[768,384]{1,0:T(8,128)(2,1)}, u32[]{:S(2)}) copy-start(bf16[768,384]{1,0:T(8,128)(2,1)} %get-tuple-element.178.refs_24_) | copy-start | bytes 1769476
  78.6 8.3 %collective-permute-start.14 = (bf16[640,256]{1,0:T(8,128)(2,1)S(1)}, bf16[640,256]{1,0:T(8,128)(2,1)S(1)}, u32[]{:S(2)}, u32[]{:S(2)}) collective-permute-start(bf16[640,256]{1,0:T(8,128)(2,1)S(1)} %maximum_maximum_fusion), channel_id=1, source_target_pairs={{0,2},{1,3},{2,0},{3,1},{4,6},{5,7},{6,4},{7,5},{8,10},{9,11},{10,... | collective-permute-start | bytes 983048 | tf_op jit(solution)/shard_map/ppermute | solution.py:25
  80.3 13.8 %collective-permute-start.19 = (bf16[192,1024]{1,0:T(8,128)(2,1)S(1)}, bf16[192,1024]{1,0:T(8,128)(2,1)S(1)}, u32[]{:S(2)}, u32[]{:S(2)}) collective-permute-start(bf16[192,1024]{1,0:T(8,128)(2,1)S(1)} %get-tuple-element.194), channel_id=1, source_target_pairs={{0,16},{8,24},{16,0},{24,8},{1,17},{9,25},{17,1},{25,9},{2,18},{10... | collective-permute-start | bytes 1179656 | tf_op jit(solution)/shard_map/ppermute | solution.py:25
  82.2 7.6 %copy-start.6 = (f32[384,512]{1,0:T(8,128)S(1)}, f32[384,512]{1,0:T(8,128)}, u32[]{:S(2)}) copy-start(f32[384,512]{1,0:T(8,128)} %get-tuple-element.192) | copy-start | bytes 2359300
  87.1 9.0 %collective-permute-start.17 = (bf16[640,128]{1,0:T(8,128)(2,1)S(1)}, bf16[640,128]{1,0:T(8,128)(2,1)S(1)}, u32[]{:S(2)}, u32[]{:S(2)}) collective-permute-start(bf16[640,128]{1,0:T(8,128)(2,1)S(1)} %fusion.17), channel_id=1, source_target_pairs={{0,4},{1,5},{2,6},{3,7},{4,0},{5,1},{6,2},{7,3},{8,12},{9,13},{10,... | collective-permute-start | bytes 491528 | tf_op jit(solution)/shard_map/ppermute | solution.py:25
  89.9 7.4 %collective-permute-start.18 = (bf16[384,256]{1,0:T(8,128)(2,1)S(1)}, bf16[384,256]{1,0:T(8,128)(2,1)S(1)}, u32[]{:S(2)}, u32[]{:S(2)}) collective-permute-start(bf16[384,256]{1,0:T(8,128)(2,1)S(1)} %pad_maximum_fusion.1), channel_id=1, source_target_pairs={{0,2},{1,3},{2,0},{3,1},{4,6},{5,7},{6,4},{7,5},{8,10},{9,11},{10,... | collective-permute-start | bytes 589832 | tf_op jit(solution)/shard_map/ppermute | solution.py:25
  97.4 7.8 %collective-permute-start.21 = (bf16[128,256]{1,0:T(8,128)(2,1)S(1)}, bf16[128,256]{1,0:T(8,128)(2,1)S(1)}, u32[]{:S(2)}, u32[]{:S(2)}) collective-permute-start(bf16[128,256]{1,0:T(8,128)(2,1)S(1)} %pad_maximum_fusion.2), channel_id=1, source_target_pairs={{0,0},{1,1},{2,8},{3,9},{4,16},{5,17},{6,24},{7,25},{8,2},{9,3},{1... | collective-permute-start | bytes 196616 | tf_op jit(solution)/shard_map/ppermute | solution.py:513
  98.1 11.3 %collective-permute-start.20 = (bf16[384,128]{1,0:T(8,128)(2,1)S(1)}, bf16[384,128]{1,0:T(8,128)(2,1)S(1)}, u32[]{:S(2)}, u32[]{:S(2)}) collective-permute-start(bf16[384,128]{1,0:T(8,128)(2,1)S(1)} %add_convert_fusion.2), channel_id=1, source_target_pairs={{0,4},{1,5},{2,6},{3,7},{4,0},{5,1},{6,2},{7,3},{8,12},{9,13},{10,... | collective-permute-start | bytes 294920 | tf_op jit(solution)/shard_map/ppermute | solution.py:25
  (9 other events, 32.6 us)
